TPU v7x, 32 devices: a whole 2x2x4 slice. The times are simulated.
32 devices in a mesh: fsdp: 8 (over z, x), tp: 4 (over y, core).
Axes of the slice: x: 2, y: 2, z: 4, core: 2. Of those that a mesh axis runs over, the one named last changes fastest.
Arguments:
- inputs: bfloat16 [8192, 2048], P(('fsdp', 'tp')), may hold values from -6 to 6
- segments: int32 [8, 1024], P('fsdp'), may hold values from 0 to 1, as said below
- ln_gain: bfloat16 [2048], replicated, may hold values from 0.099609375 to 1.8984375
- ln_bias: bfloat16 [2048], replicated, may hold values from -4 to 4
- w_qkv: bfloat16 [3, 2048, 2048], P(None, 'fsdp', 'tp'), may hold values from -0.1875 to 0.1875
- b_qkv: bfloat16 [3, 2048], P(None, 'tp'), may hold values from -6 to 6
- w_out: bfloat16 [2048, 2048], P('tp', 'fsdp'), may hold values from -0.5 to 0.5
- b_out: bfloat16 [2048], replicated, may hold values from -4 to 4
- w_fc1: bfloat16 [2048, 8192], P('fsdp', 'tp'), may hold values from -0.125 to 0.125
- b_fc1: bfloat16 [8192], P('tp'), may hold values from -6 to 6
- w_fc2: bfloat16 [8192, 2048], P('tp', 'fsdp'), may hold values from -0.0625 to 0.0625
- b_fc2: bfloat16 [2048], replicated, may hold values from -4 to 4
- cotangent: bfloat16 [8192, 2048], P(('fsdp', 'tp')), may hold values from -6 to 6
Outputs:
- outputs: bfloat16 [8192, 2048], P(('fsdp', 'tp'))
- grad_inputs: float32 [8192, 2048], P(('fsdp', 'tp'))
- grad_ln_gain: float32 [2048], replicated
- grad_ln_bias: float32 [2048], replicated
- grad_w_qkv: float32 [3, 2048, 2048], P(None, 'fsdp', 'tp')
- grad_b_qkv: float32 [3, 2048], replicated
- grad_w_out: float32 [2048, 2048], P('tp', 'fsdp')
- grad_b_out: float32 [2048], replicated
- grad_w_fc1: float32 [2048, 8192], P('fsdp', 'tp')
- grad_b_fc1: float32 [8192], replicated
- grad_w_fc2: float32 [8192, 2048], P('tp', 'fsdp')
- grad_b_fc2: float32 [2048], replicated
Inputs may be any that keep to these rules, and one draw needn't show every extreme that they name: `segments`: each row never falls and holds documents 0 and 1; document 1 starts at a position from 204 to 255 or from 769 to 820.
All inputs are finite; a program needn't handle non-finite values.
Results may differ from a plain program's by a relative error of at most 0.012.
The roundings to bfloat16 on the way count: a program that leaves them out, or rounds other values in their place, can miss the bound.
Values may be sent and summed in bfloat16 or wider, within the bound.
A program may use at most 192 MiB of HBM per device.

v0:
```python
import math

import jax
import jax.numpy as jnp
from jax import lax
from jax.sharding import PartitionSpec as P

D = 2048
HEAD_DIM = 64
ROT = 32
FF = 8192


norm_epsilon = 1e-05
masked_score = -1e30


def gelu_tanh(values):
    return (
        0.5
        * values
        * (1.0 + jnp.tanh(0.7978845608028654 * (values + 0.044715 * values * values * values)))
    )


def layer_norm(tokens_in, gain, offset):
    centre = jnp.mean(tokens_in, axis=-1, keepdims=True)
    centred = tokens_in - centre
    spread = jnp.mean(centred * centred, axis=-1, keepdims=True)
    return centred * lax.rsqrt(spread + norm_epsilon) * gain + offset


def doc_positions(segment_row):
    places = jnp.arange(segment_row.shape[0], dtype=jnp.int32)
    opened = jnp.concatenate([jnp.ones((1,), dtype=jnp.bool_), segment_row[1:] != segment_row[:-1]])
    opening = lax.cummax(jnp.where(opened, places, jnp.zeros_like(places)), axis=0)
    return places - opening


def rotary_tables(segment_row):
    frequency = jnp.exp(jnp.arange(0, ROT, 2, dtype=jnp.float32) * (-math.log(10000.0) / ROT))
    angles = doc_positions(segment_row).astype(jnp.float32)[:, None] * frequency[None, :]
    angles = jnp.concatenate([angles, angles], axis=-1)[:, None, :]
    return (jnp.cos(angles), jnp.sin(angles))


def rotate(heads_data, cosine, sine_part):
    turned = heads_data[..., :ROT]
    half_rot = ROT // 2
    swapped = jnp.concatenate([-turned[..., half_rot:], turned[..., :half_rot]], axis=-1)
    return jnp.concatenate([turned * cosine + swapped * sine_part, heads_data[..., ROT:]], axis=-1)


def allowed_pairs(segment_row, first_row, row_count):
    places = jnp.arange(segment_row.shape[0], dtype=jnp.int32)
    row_places = places[first_row : first_row + row_count]
    row_segments = segment_row[first_row : first_row + row_count]
    return (row_places[:, None] >= places[None, :]) & (
        row_segments[:, None] == segment_row[None, :]
    )


def local(
    inputs,
    segments,
    ln_gain,
    ln_bias,
    w_qkv,
    b_qkv,
    w_out,
    b_out,
    w_fc1,
    b_fc1,
    w_fc2,
    b_fc2,
    cotangent,
):
    wide = jnp.float32
    narrow = jnp.bfloat16
    tokens_in = inputs.astype(wide)
    normed_local, norm_back = jax.vjp(
        layer_norm, tokens_in, ln_gain.astype(wide), ln_bias.astype(wide)
    )
    normed = lax.all_gather(normed_local.astype(narrow), "tp", axis=0, tiled=True)
    full_qkv, full_out, full_fc1, full_fc2 = (
        lax.all_gather(w_qkv, "fsdp", axis=1, tiled=True),
        lax.all_gather(w_out, "fsdp", axis=1, tiled=True),
        lax.all_gather(w_fc1, "fsdp", axis=0, tiled=True),
        lax.all_gather(w_fc2, "fsdp", axis=1, tiled=True),
    )
    length = normed.shape[0]
    width_local = full_qkv.shape[2]
    local_heads = width_local // HEAD_DIM
    scale = HEAD_DIM ** (-0.5)
    segment_row = segments[0]
    cosine, sine_part = rotary_tables(segment_row)
    projected = (
        jnp.einsum("td,kde->kte", normed, full_qkv, preferred_element_type=wide)
        + b_qkv.astype(wide)[:, None, :]
    )

    def turn_pair(query_flat, key_flat):
        return (
            rotate(query_flat.reshape(length, local_heads, HEAD_DIM), cosine, sine_part),
            rotate(key_flat.reshape(length, local_heads, HEAD_DIM), cosine, sine_part),
        )

    turned, turn_back = jax.vjp(turn_pair, projected[0], projected[1])
    queries = turned[0].astype(narrow)
    key_heads = turned[1].astype(narrow)
    values = projected[2].astype(narrow).reshape(length, local_heads, HEAD_DIM)
    row_block = min(512, length)
    mixed_parts = []
    log_totals = []
    for first_row in range(0, length, row_block):
        allowed = allowed_pairs(segment_row, first_row, row_block)
        scores = (
            jnp.einsum(
                "qhd,khd->hqk",
                queries[first_row : first_row + row_block],
                key_heads,
                preferred_element_type=wide,
            )
            * scale
        )
        masked = jnp.where(allowed[None], scores, masked_score)
        largest = jnp.max(masked, axis=-1, keepdims=True)
        exponent = jnp.exp(masked - largest)
        summed = jnp.sum(exponent, axis=-1, keepdims=True)
        weights_soft = (exponent / summed).astype(narrow)
        mixed_parts.append(
            jnp.einsum("hqk,khd->qhd", weights_soft, values, preferred_element_type=wide)
        )
        log_totals.append(largest + jnp.log(summed))
    mixed_heads = jnp.concatenate(mixed_parts, axis=0).reshape(length, width_local).astype(narrow)
    hidden = jnp.dot(normed, full_fc1, preferred_element_type=wide) + b_fc1.astype(wide)
    active, gelu_back = jax.vjp(gelu_tanh, hidden)
    active_low = active.astype(narrow)
    branches = jnp.dot(mixed_heads, full_out, preferred_element_type=wide) + jnp.dot(
        active_low, full_fc2, preferred_element_type=wide
    )
    branch_local = lax.psum_scatter(branches, "tp", scatter_dimension=0, tiled=True)
    outputs = (tokens_in + branch_local + b_out.astype(wide) + b_fc2.astype(wide)).astype(narrow)
    grad_rows = lax.all_gather(cotangent, "tp", axis=0, tiled=True)
    back_qkv, back_out, back_fc1, back_fc2 = (
        lax.all_gather(w_qkv, "fsdp", axis=1, tiled=True),
        lax.all_gather(w_out, "fsdp", axis=1, tiled=True),
        lax.all_gather(w_fc1, "fsdp", axis=0, tiled=True),
        lax.all_gather(w_fc2, "fsdp", axis=1, tiled=True),
    )
    grad_mixed = jnp.einsum("td,ed->te", grad_rows, back_out, preferred_element_type=wide).astype(
        narrow
    )
    grad_w_out = jnp.einsum("te,td->ed", mixed_heads, grad_rows, preferred_element_type=wide)
    grad_active = jnp.einsum("td,fd->tf", grad_rows, back_fc2, preferred_element_type=wide)
    grad_hidden = gelu_back(grad_active)[0].astype(narrow)
    grad_w_fc2 = jnp.einsum("tf,td->fd", active_low, grad_rows, preferred_element_type=wide)
    grad_w_fc1 = jnp.einsum("td,tf->df", normed, grad_hidden, preferred_element_type=wide)
    grad_heads = grad_mixed.reshape(length, local_heads, HEAD_DIM)
    grad_keys = jnp.zeros((length, local_heads, HEAD_DIM), wide)
    grad_values = jnp.zeros((length, local_heads, HEAD_DIM), wide)
    grad_query_parts = []
    for block_number, first_row in enumerate(range(0, length, row_block)):
        allowed = allowed_pairs(segment_row, first_row, row_block)
        query_rows = queries[first_row : first_row + row_block]
        scores = (
            jnp.einsum("qhd,khd->hqk", query_rows, key_heads, preferred_element_type=wide) * scale
        )
        masked = jnp.where(allowed[None], scores, masked_score)
        probs_exact = jnp.exp(masked - log_totals[block_number])
        weights_soft = probs_exact.astype(narrow)
        grad_heads_rows = grad_heads[first_row : first_row + row_block]
        grad_probs = jnp.einsum(
            "qhd,khd->hqk", grad_heads_rows, values, preferred_element_type=wide
        )
        inner = jnp.sum(probs_exact * grad_probs, axis=-1, keepdims=True)
        grad_scores = (probs_exact * (grad_probs - inner)).astype(narrow)
        grad_query_parts.append(
            jnp.einsum("hqk,khd->qhd", grad_scores, key_heads, preferred_element_type=wide) * scale
        )
        grad_keys = (
            grad_keys
            + jnp.einsum("hqk,qhd->khd", grad_scores, query_rows, preferred_element_type=wide)
            * scale
        )
        grad_values = grad_values + jnp.einsum(
            "hqk,qhd->khd", weights_soft, grad_heads_rows, preferred_element_type=wide
        )
    grad_query_pre, grad_key_pre = turn_back((jnp.concatenate(grad_query_parts, axis=0), grad_keys))
    grad_projected = jnp.stack(
        [grad_query_pre, grad_key_pre, grad_values.reshape(length, width_local)]
    ).astype(narrow)
    grad_w_qkv = jnp.einsum("td,kte->kde", normed, grad_projected, preferred_element_type=wide)
    grad_normed = jnp.einsum(
        "kte,kde->td", grad_projected, back_qkv, preferred_element_type=wide
    ) + jnp.einsum("tf,df->td", grad_hidden, back_fc1, preferred_element_type=wide)
    grad_normed_local = lax.psum_scatter(grad_normed, "tp", scatter_dimension=0, tiled=True)
    grad_tokens, grad_gain, grad_offset = norm_back(grad_normed_local)
    grad_tokens = grad_tokens + cotangent.astype(wide)
    summed_qkv, summed_out, summed_fc1, summed_fc2 = (
        lax.psum_scatter(grad_w_qkv, "fsdp", scatter_dimension=1, tiled=True),
        lax.psum_scatter(grad_w_out, "fsdp", scatter_dimension=1, tiled=True),
        lax.psum_scatter(grad_w_fc1, "fsdp", scatter_dimension=0, tiled=True),
        lax.psum_scatter(grad_w_fc2, "fsdp", scatter_dimension=1, tiled=True),
    )
    tp_place = lax.axis_index("tp")
    anchor = jnp.zeros((), jnp.int32)
    bias_qkv_full = lax.dynamic_update_slice(
        jnp.zeros((3, D), wide),
        jnp.sum(grad_projected.astype(wide), axis=1),
        (anchor, tp_place * width_local),
    )
    hidden_local = grad_hidden.shape[1]
    bias_fc1_full = lax.dynamic_update_slice(
        jnp.zeros((FF,), wide),
        jnp.sum(grad_hidden.astype(wide), axis=0),
        (tp_place * hidden_local,),
    )
    cotangent_sum = jnp.sum(cotangent.astype(wide), axis=0)
    total_qkv, total_fc1, total_gain, total_offset, total_out = lax.psum(
        (bias_qkv_full, bias_fc1_full, grad_gain, grad_offset, cotangent_sum), ("fsdp", "tp")
    )
    return (
        outputs,
        grad_tokens,
        total_gain,
        total_offset,
        summed_qkv,
        total_qkv,
        summed_out,
        total_out,
        summed_fc1,
        total_fc1,
        summed_fc2,
        total_out,
    )


def solution(mesh):
    return jax.shard_map(
        local,
        mesh=mesh,
        in_specs=(
            P(("fsdp", "tp"), None),
            P("fsdp", None),
            P(),
            P(),
            P(None, "fsdp", "tp"),
            P(None, "tp"),
            P("tp", "fsdp"),
            P(),
            P("fsdp", "tp"),
            P("tp"),
            P("tp", "fsdp"),
            P(),
            P(("fsdp", "tp"), None),
        ),
        out_specs=(
            P(("fsdp", "tp"), None),
            P(("fsdp", "tp"), None),
            P(),
            P(),
            P(None, "fsdp", "tp"),
            P(),
            P("tp", "fsdp"),
            P(),
            P("fsdp", "tp"),
            P(),
            P("tp", "fsdp"),
            P(),
        ),
        check_vma=False,
    )
```

profile of v0, /device:TPU:0, one launch (start us, length us, event | category | flops | bytes accessed | tf_op | source)
XLA Modules:
  0.0 1699.6 jit_solution(16875702286805319734)
XLA Ops:
  14.4 2.7 fusion.30
  17.1 2.3 copy.32
  23.7 40.2 %all-gather.11.cloned.1.call-done = bf16[512,2048]{1,0:T(8,128)(2,1)} async-done(((bf16[512,256]{1,0:T(8,128)(2,1)}), bf16[512,2048]{1,0:T(8,128)(2,1)}) %all-gather.11.cloned.1.call-update) | async-done | bytes 2097168 | tf_op jit(solution)/shard_map/all_gather | solution.py:87
  63.9 34.3 %all-gather.17.cloned.1.call-done = bf16[1024,2048]{1,0:T(8,128)(2,1)} async-done(((bf16[256,2048]{1,0:T(8,128)(2,1)}), bf16[1024,2048]{1,0:T(8,128)(2,1)}) %all-gather.17.cloned.1.call-update) | async-done | bytes 4194320 | tf_op jit(solution)/shard_map/all_gather | solution.py:144
  98.2 5.2 convolution_convert_fusion
  104.4 30.4 %all-gather.7.cloned.1.call-done = bf16[1024,2048]{1,0:T(8,128)(2,1)} async-done(((bf16[256,2048]{1,0:T(8,128)(2,1)}), bf16[1024,2048]{1,0:T(8,128)(2,1)}) %all-gather.7.cloned.1.call-update) | async-done | bytes 4194320 | tf_op jit(solution)/shard_map/all_gather | solution.py:84
  134.8 102.4 %all-gather.9.cloned.1.call-done = bf16[3,2048,512]{1,2,0:T(8,128)(2,1)} async-done(((bf16[3,256,512]{1,2,0:T(8,128)(2,1)}), bf16[3,2048,512]{1,2,0:T(8,128)(2,1)}) %all-gather.9.cloned.1.call-update) | async-done | bytes 6291472 | tf_op jit(solution)/shard_map/all_gather | solution.py:86
  237.3 10.1 add_bitcast_fusion
  249.1 3.1 fusion.73
  252.2 3.5 fusion.1
  255.8 7.7 fusion.74
  263.5 7.8 fusion
  271.3 3.4 fusion.10
  274.8 8.4 add_convert_fusion
  283.2 2.3 copy.35
  285.5 13.3 multiply_reduce_fusion.1
  298.8 12.3 multiply_convert_fusion.1
  311.1 4.3 copy-done.2
  317.0 7.1 fusion.42
  324.1 10.2 multiply_reduce_fusion
  334.2 10.2 multiply_convert_fusion
  344.5 6.5 fusion.41
  358.9 3.5 all-gather.13.cloned.1.call-done
  362.4 14.5 fusion.75
  376.9 111.0 %all-gather.15.cloned.1.call-done = bf16[2048,2048]{1,0:T(8,128)(2,1)} async-done(((bf16[2048,256]{1,0:T(8,128)(2,1)}), bf16[2048,2048]{1,0:T(8,128)(2,1)}) %all-gather.15.cloned.1.call-update) | async-done | bytes 8388624 | tf_op jit(solution)/shard_map/all_gather | solution.py:89
  487.9 20.4 %convert_reduce_fusion = (f32[2048]{0:T(1024)S(1)}, bf16[1024,2048]{1,0:T(8,128)(2,1)S(1)}) fusion(f32[1024,2048]{1,0:T(8,128)} %fusion.75, f32[2048]{0:T(1024)S(1)} %convert_element_type.93, bf16[1024,2048]{1,0:T(8,128)(2,1)} %all-gather.17.cloned.1.call-done, bf16[2048,2048]{1,0:T(8,128)(2,1)} %all-gather.15.cloned.1.call-done), kind=kOutput, calls=%fused_computation.29 | convolution fusion | flops 8646555648 | bytes 25182208 | tf_op jit(solution)/shard_map/td,fd->tf/dot_general | solution.py:155
  508.3 11.2 fusion.76
  519.6 12.9 bitcast_add_fusion
  533.7 9.7 fusion.46
  543.5 8.5 fusion.45
  552.1 12.5 fusion.64
  564.6 5.7 convolution_add_fusion
  571.0 2.3 convert_reduce_fusion.1
  574.0 28.7 %reduce-scatter.9.cloned.1.call-done = f32[256,2048]{1,0:T(8,128)} async-done(((f32[1024,2048]{1,0:T(8,128)}), f32[256,2048]{1,0:T(8,128)}) %reduce-scatter.9.cloned.1.call-update) | async-done | bytes 2097168 | tf_op jit(solution)/shard_map/reduce_scatter | solution.py:197
  602.7 2.7 fusion.65
  605.4 3.1 fusion.31
  608.5 68.7 %reduce-scatter.7.cloned.1.call-done = f32[256,2048]{1,0:T(8,128)} async-done(((f32[1024,2048]{1,0:T(8,128)}), f32[256,2048]{1,0:T(8,128)}) %reduce-scatter.7.cloned.1.call-update) | async-done | bytes 2097168 | tf_op jit(solution)/shard_map/reduce_scatter | solution.py:142
  677.2 6.0 convert_reduce_fusion.3
  683.3 12.5 convolution_bitcast_fusion
  695.8 6.6 fusion.77
  702.5 17.5 %fusion.63 = f32[2048,2048]{1,0:T(8,128)} fusion(bf16[1024,2048]{1,0:T(8,128)(2,1)} %all-gather.17.cloned.1.call-done, f32[1024,2048]{1,0:T(8,128)} %fusion.75, f32[2048]{0:T(1024)S(1)} %convert_element_type.93), kind=kOutput, calls=%fused_computation.132 | convolution fusion | flops 8610906112 | bytes 29368320 | tf_op jit(solution)/shard_map/tf,td->fd/dot_general | solution.py:157
  720.1 15.3 fusion.78
  735.4 71.7 %all-reduce.11.cloned.1.call-done = (f32[2048]{0:T(1024)}, f32[2048]{0:T(1024)}, f32[3,2048]{1,0:T(4,128)}, f32[2048]{0:T(1024)}, f32[8192]{0:T(1024)}) async-done(((f32[2048]{0:T(1024)}, f32[2048]{0:T(1024)}, f32[3,2048]{1,0:T(4,128)}, f32[2048]{0:T(1024)}, f32[8192]{0:T(1024)}), (f32[2048]{0:T(1024)}, f32[2048]{0:T(1024)}, f32[3,2048]{1,0:T(4,128)}, f32[2048]{0:T(1024)}, ...) | async-done | bytes 81936 | tf_op jit(solution)/shard_map/psum | solution.py:220
  807.1 212.5 %reduce-scatter.11.cloned.1.call-done = f32[3,256,512]{1,2,0:T(8,128)} async-done(((f32[3,2048,512]{1,2,0:T(8,128)}), f32[3,256,512]{1,2,0:T(8,128)}) %reduce-scatter.11.cloned.1.call-update) | async-done | bytes 1572880 | tf_op jit(solution)/shard_map/reduce_scatter | solution.py:201
  1019.6 3.0 copy.38
  1022.6 88.8 %reduce-scatter.13.cloned.1.call-done = f32[512,256]{1,0:T(8,128)} async-done(((f32[512,2048]{1,0:T(8,128)}), f32[512,256]{1,0:T(8,128)}) %reduce-scatter.13.cloned.1.call-update) | async-done | bytes 524304 | tf_op jit(solution)/shard_map/reduce_scatter | solution.py:202
  1111.4 287.3 %reduce-scatter.17.cloned.1.call-done = f32[2048,256]{1,0:T(8,128)} async-done(((f32[2048,2048]{1,0:T(8,128)}), f32[2048,256]{1,0:T(8,128)}) %reduce-scatter.17.cloned.1.call-update) | async-done | bytes 2097168 | tf_op jit(solution)/shard_map/reduce_scatter | solution.py:204
  1398.7 286.1 %reduce-scatter.15.cloned.1.call-done = f32[256,2048]{1,0:T(8,128)} async-done(((f32[2048,2048]{1,0:T(8,128)}), f32[256,2048]{1,0:T(8,128)}) %reduce-scatter.15.cloned.1.call-update) | async-done | bytes 2097168 | tf_op jit(solution)/shard_map/reduce_scatter | solution.py:203
  (201 shorter events, 34.2 us)
Async XLA Ops:
  7.2 13.5 copy-start.33
  7.2 14.3 copy-start.46
  7.2 14.3 copy-start.47
  7.2 56.7 %all-gather.11.cloned.1.call-start = ((), (), s32[]{:S(2)}) async-start(), calls=%async_computation.8 | async-start | bytes 2359296 | tf_op jit(solution)/shard_map/all_gather | solution.py:87
  7.9 90.2 %all-gather.17.cloned.1.call-start = ((), (), s32[]{:S(2)}) async-start(), calls=%async_computation.12 | async-start | bytes 5242880 | tf_op jit(solution)/shard_map/all_gather | solution.py:144
  8.7 126.1 %all-gather.7.cloned.1.call-start = ((), (), s32[]{:S(2)}) async-start(), calls=%async_computation.6 | async-start | bytes 5242880 | tf_op jit(solution)/shard_map/all_gather | solution.py:84
  17.1 220.2 %all-gather.9.cloned.1.call-start = ((), (), s32[]{:S(2)}) async-start(), calls=%async_computation.7 | async-start | bytes 7077888 | tf_op jit(solution)/shard_map/all_gather | solution.py:86
  19.4 343.0 %all-gather.13.cloned.1.call-start = ((), (), s32[]{:S(2)}) async-start(), calls=%async_computation.9 | async-start | bytes 9437184 | tf_op jit(solution)/shard_map/all_gather | solution.py:88
  20.0 467.9 %all-gather.15.cloned.1.call-start = ((), (), s32[]{:S(2)}) async-start(), calls=%async_computation.10 | async-start | bytes 9437184 | tf_op jit(solution)/shard_map/all_gather | solution.py:89
  20.6 582.1 %reduce-scatter.9.cloned.1.call-start = ((), (), s32[]{:S(2)}) async-start(), calls=%async_computation.13 | async-start | bytes 10485760 | tf_op jit(solution)/shard_map/reduce_scatter | solution.py:197
  21.8 226.6 %copy-start.22 = (f32[1024,32]{0,1:T(8,128)}, f32[1024,32]{0,1:T(8,128)S(1)}, u32[]{:S(2)}) copy-start(f32[1024,32]{0,1:T(8,128)S(1)} %get-tuple-element.70) | copy-start | bytes 393220
  21.8 226.6 %copy-start.24 = (f32[1024,32]{0,1:T(8,128)}, f32[1024,32]{0,1:T(8,128)S(1)}, u32[]{:S(2)}) copy-start(f32[1024,32]{0,1:T(8,128)S(1)} %get-tuple-element.71) | copy-start | bytes 393220
  247.5 38.0 %copy-start.4 = (bf16[1,1024,512]{1,2,0:T(8,128)(2,1)}, bf16[1,1024,512]{1,2,0:T(8,128)(2,1)S(1)}, u32[]{:S(2)}) copy-start(bf16[1,1024,512]{1,2,0:T(8,128)(2,1)S(1)} %slice.162) | copy-start | bytes 3145732
  248.3 7.5 copy-start.7
  249.0 6.7 copy-start.9
  252.2 19.1 %copy-start = (f32[8,512,1024]{2,1,0:T(8,128)}, f32[8,512,1024]{2,1,0:T(8,128)S(1)}, u32[]{:S(2)}) copy-start(f32[8,512,1024]{2,1,0:T(8,128)S(1)} %get-tuple-element.77) | copy-start | bytes 50331652
  255.7 7.7 copy-start.34
  263.5 7.8 copy-start.36
  263.5 7.8 copy-start.14
  298.8 16.6 copy-start.10
  298.8 25.3 %slice-start = ((s8[16777216]{0:T(1024)(128)(4,1)}), s8[4194304]{0:T(1024)(128)(4,1)S(1)}, s32[]{:S(2)}) async-start(s8[16777216]{0:T(1024)(128)(4,1)} %bitcast.75), calls=%async_computation.19 | async-start | bytes 8388608
  298.8 25.3 %slice-start.1 = ((s8[16777216]{0:T(1024)(128)(4,1)}), s8[4194304]{0:T(1024)(128)(4,1)S(1)}, s32[]{:S(2)}) async-start(s8[16777216]{0:T(1024)(128)(4,1)} %bitcast.75), calls=%async_computation.20 | async-start | bytes 8388608
  298.8 25.3 %slice-start.2 = ((s8[16777216]{0:T(1024)(128)(4,1)}), s8[4194304]{0:T(1024)(128)(4,1)S(1)}, s32[]{:S(2)}) async-start(s8[16777216]{0:T(1024)(128)(4,1)} %bitcast.75), calls=%async_computation.21 | async-start | bytes 8388608
  315.4 8.7 slice-start.3
  356.2 163.3 %copy-start.18 = (bf16[1,1024,512]{2,1,0:T(8,128)(2,1)}, bf16[1,1024,512]{2,1,0:T(8,128)(2,1)S(1)}, u32[]{:S(2)}) copy-start(bf16[1,1024,512]{2,1,0:T(8,128)(2,1)S(1)} %copy.34) | copy-start | bytes 3145732
  358.9 160.7 %copy-start.19 = (bf16[1,1024,512]{2,1,0:T(8,128)(2,1)}, bf16[1,1024,512]{2,1,0:T(8,128)(2,1)S(1)}, u32[]{:S(2)}) copy-start(bf16[1,1024,512]{2,1,0:T(8,128)(2,1)S(1)} %copy.33) | copy-start | bytes 3145732
  487.9 20.4 %copy-start.50 = (bf16[2048,2048]{1,0:T(8,128)(2,1)S(1)}, bf16[2048,2048]{1,0:T(8,128)(2,1)}, u32[]{:S(2)}) copy-start(bf16[2048,2048]{1,0:T(8,128)(2,1)} %all-gather.13.cloned.1.call-done) | copy-start | bytes 25165828
  508.3 11.3 copy-start.51
  508.3 11.2 copy-start.17
  532.5 10.9 copy-start.37
  532.5 10.9 copy-start.39
  532.6 144.6 %reduce-scatter.7.cloned.1.call-start = ((), (), s32[]{:S(2)}) async-start(), calls=%async_computation.11 | async-start | bytes 10485760 | tf_op jit(solution)/shard_map/reduce_scatter | solution.py:142
  533.7 18.4 %slice-start.4 = ((s8[8388608]{0:T(1024)(128)(4,1)}), s8[4194304]{0:T(1024)(128)(4,1)S(1)}, s32[]{:S(2)}) async-start(s8[8388608]{0:T(1024)(128)(4,1)} %bitcast.99), calls=%async_computation.23 | async-start | bytes 8388608
  543.5 8.6 slice-start.5
  552.1 12.5 copy-start.20
  570.3 32.4 %copy-start.3 = (bf16[256,2048]{1,0:T(8,128)(2,1)S(1)}, bf16[256,2048]{1,0:T(8,128)(2,1)}, u32[]{:S(2)}) copy-start(bf16[256,2048]{1,0:T(8,128)(2,1)} %param.13) | copy-start | bytes 3145732
  570.3 32.4 %copy-start.28 = (f32[2048]{0:T(1024)S(1)}, f32[2048]{0:T(1024)}, u32[]{:S(2)}) copy-start(f32[2048]{0:T(1024)} %copy-done.27) | copy-start | bytes 24580
  570.3 32.4 %copy-start.41 = (f32[256]{0:T(256)S(1)}, f32[256]{0:T(256)}, u32[]{:S(2)}) copy-start(f32[256]{0:T(256)} %copy-done.40) | copy-start | bytes 3076
  570.3 35.0 %copy-start.45 = (f32[256]{0:T(256)S(1)}, f32[256]{0:T(256)}, u32[]{:S(2)}) copy-start(f32[256]{0:T(256)} %copy-done.44) | copy-start | bytes 3076
  570.3 35.0 %copy-start.43 = (f32[256]{0:T(256)S(1)}, f32[256]{0:T(256)}, u32[]{:S(2)}) copy-start(f32[256]{0:T(256)} %copy-done.42) | copy-start | bytes 3076
  570.3 106.8 %copy-start.16 = (bf16[256,2048]{1,0:T(8,128)(2,1)S(1)}, bf16[256,2048]{1,0:T(8,128)(2,1)}, u32[]{:S(2)}) copy-start(bf16[256,2048]{1,0:T(8,128)(2,1)} %param.25) | copy-start | bytes 3145732
  570.4 236.7 %all-reduce.11.cloned.1.call-start = ((), (), s32[]{:S(2)}) async-start(), calls=%async_computation.18 | async-start | bytes 180224 | tf_op jit(solution)/shard_map/psum | solution.py:220
  573.4 109.8 %copy-start.32 = (f32[3,2048]{1,0:T(4,128)}, f32[3,2048]{1,0:T(4,128)S(1)}, u32[]{:S(2)}) copy-start(f32[3,2048]{1,0:T(4,128)S(1)} %constant_dynamic-update-slice_fusion) | copy-start | bytes 73732
  573.9 109.2 %copy-start.31 = (f32[8192]{0:T(1024)}, f32[8192]{0:T(1024)S(1)}, u32[]{:S(2)}) copy-start(f32[8192]{0:T(1024)S(1)} %dynamic_update_slice.7) | copy-start | bytes 98308
  683.2 336.4 %reduce-scatter.11.cloned.1.call-start = ((), (), s32[]{:S(2)}) async-start(), calls=%async_computation.14 | async-start | bytes 14155776 | tf_op jit(solution)/shard_map/reduce_scatter | solution.py:201
  695.8 415.6 %reduce-scatter.13.cloned.1.call-start = ((), (), s32[]{:S(2)}) async-start(), calls=%async_computation.15 | async-start | bytes 4718592 | tf_op jit(solution)/shard_map/reduce_scatter | solution.py:202
  702.4 696.2 %reduce-scatter.17.cloned.1.call-start = ((), (), s32[]{:S(2)}) async-start(), calls=%async_computation.17 | async-start | bytes 18874368 | tf_op jit(solution)/shard_map/reduce_scatter | solution.py:204
  720.0 964.7 %reduce-scatter.15.cloned.1.call-start = ((), (), s32[]{:S(2)}) async-start(), calls=%async_computation.16 | async-start | bytes 18874368 | tf_op jit(solution)/shard_map/reduce_scatter | solution.py:203
  (23 other events, 59.9 us)
Sparse Core Ops, SparseCore 0:
  10.1 53.7 all-gather.10
  65.4 32.6 all-gather.16
  100.3 34.4 all-gather.6
  137.3 99.9 all-gather.8
  239.2 123.1 all-gather.12
  364.3 123.5 all-gather.14
  532.7 69.9 reduce-scatter.8
  605.4 71.7 reduce-scatter.6
  684.7 122.3 all-reduce.10
  810.6 208.9 reduce-scatter.10
  1023.8 87.5 reduce-scatter.12
  1116.1 282.5 reduce-scatter.16
  1403.0 281.6 reduce-scatter.14
where the time goes:
time: 1710 us; the launch traced here: 1700 us
  waiting for transfers between devices  1370 us (80%)
  matrix products  225 us (13%)
  other arithmetic  63.4 us (4%)
  local copies, waits for them, and re-layouts  27 us (2%)
    reduce_scatter x1, waiting for transfers between devices, local(): lax.psum_scatter(grad_w_fc2, 'fsdp', scatter_dimension=1, tiled=True)  287 us
    reduce_scatter x1, waiting for transfers between devices, local(): lax.psum_scatter(grad_w_fc1, 'fsdp', scatter_dimension=0, tiled=True)  286 us
    reduce_scatter x1, waiting for transfers between devices, local(): lax.psum_scatter(grad_w_qkv, 'fsdp', scatter_dimension=1, tiled=True)  212 us
    all_gather x1, waiting for transfers between devices, local(): lax.all_gather(w_fc2, 'fsdp', axis=1, tiled=True)  111 us
    all_gather x1, waiting for transfers between devices, local(): lax.all_gather(w_qkv, 'fsdp', axis=1, tiled=True)  102 us
    reduce_scatter x1, waiting for transfers between devices, local(): lax.psum_scatter(grad_w_out, 'fsdp', scatter_dimension=1, tiled=True)  88.8 us
    psum x1, waiting for transfers between devices, local(): lax.psum((bias_qkv_full, bias_fc1_full, grad_gain, grad_offset, cotangent...  71.7 us
    reduce_scatter x1, waiting for transfers between devices, local(): lax.psum_scatter(branches, 'tp', scatter_dimension=0, tiled=True)  68.7 us
  transfers between devices with their start and end apart: 13, of which 13 were waited for; matrix products, arithmetic and copies ran while one was open for 15% of the time, Pallas kernels for 0%

commit v1 on v0

v1 whole, which is shorter than its diff:
```python
import functools
import math

import jax
import jax.numpy as jnp
from jax import lax
from jax.experimental import pallas as pl
from jax.experimental.pallas import tpu as pltpu
from jax.sharding import PartitionSpec as P

D = 2048
HEAD_DIM = 64
ROT = 32
FF = 8192
MIB = 1 << 20

wide = jnp.float32
narrow = jnp.bfloat16
norm_epsilon = 1e-05
masked_score = -1e30


def gelu_tanh(values):
    return (
        0.5
        * values
        * (1.0 + jnp.tanh(0.7978845608028654 * (values + 0.044715 * values * values * values)))
    )


def layer_norm(tokens_in, gain, offset):
    centre = jnp.mean(tokens_in, axis=-1, keepdims=True)
    centred = tokens_in - centre
    spread = jnp.mean(centred * centred, axis=-1, keepdims=True)
    return centred * lax.rsqrt(spread + norm_epsilon) * gain + offset


def openings(segment_rows):
    places = jnp.broadcast_to(
        jnp.arange(segment_rows.shape[1], dtype=jnp.int32)[None], segment_rows.shape
    )
    opened = jnp.concatenate(
        [
            jnp.ones((segment_rows.shape[0], 1), dtype=jnp.bool_),
            segment_rows[:, 1:] != segment_rows[:, :-1],
        ],
        axis=1,
    )
    return lax.cummax(jnp.where(opened, places, jnp.zeros_like(places)), axis=1)


def rotary_tables(opening):
    length = opening.shape[1]
    places = jnp.arange(length, dtype=jnp.int32)[None]
    frequency = jnp.exp(jnp.arange(0, ROT, 2, dtype=jnp.float32) * (-math.log(10000.0) / ROT))
    angles = (places - opening).astype(jnp.float32)[:, :, None] * frequency
    cosine, sine = jnp.cos(angles), jnp.sin(angles)
    ones = jnp.ones(angles.shape[:2] + (HEAD_DIM - ROT,), wide)
    cos_head = jnp.concatenate([cosine, cosine, ones], axis=-1)
    sin_head = jnp.concatenate([-sine, sine, 0.0 * ones], axis=-1)
    return (
        jnp.concatenate([cos_head, cos_head], axis=-1),
        jnp.concatenate([sin_head, sin_head], axis=-1),
    )


def nt(a, b):
    return lax.dot_general(a, b, (((1,), (1,)), ((), ())), preferred_element_type=wide)


def nn(a, b):
    return lax.dot_general(a, b, (((1,), (0,)), ((), ())), preferred_element_type=wide)


def tn(a, b):
    return lax.dot_general(a, b, (((0,), (0,)), ((), ())), preferred_element_type=wide)


def attention_kernel(
    rows,
    open_ref,
    cos_ref,
    sin_ref,
    q_ref,
    k_ref,
    v_ref,
    do_ref,
    attn_ref,
    gq_ref,
    gk_ref,
    gv_ref,
    kb_ref,
    vb_ref,
    dk_ref,
    dv_ref,
):
    length = q_ref.shape[0]
    lanes = 2 * HEAD_DIM
    place = lax.broadcasted_iota(jnp.int32, (1, lanes), 1)
    low_half = (place % HEAD_DIM) < (ROT // 2)
    scale = HEAD_DIM**-0.5

    def partner(u):
        return jnp.where(
            low_half, pltpu.roll(u, lanes - ROT // 2, 1), pltpu.roll(u, ROT // 2, 1)
        )

    def turn(u, cosine, sine):
        return u * cosine + partner(u) * sine

    def turn_back(u, cosine, sine):
        return u * cosine - partner(u) * sine

    kb_ref[...] = turn(k_ref[...], cos_ref[...], sin_ref[...]).astype(narrow)
    vb_ref[...] = v_ref[...].astype(narrow)
    dk_ref[...] = jnp.zeros_like(dk_ref)
    dv_ref[...] = jnp.zeros_like(dv_ref)
    for first in range(0, length, rows):
        seen = first + rows
        here = slice(first, seen)
        cosine, sine = cos_ref[here], sin_ref[here]
        q_both = (turn(q_ref[here], cosine, sine).astype(narrow) * scale).astype(narrow)
        row_place = first + lax.broadcasted_iota(jnp.int32, (rows, seen), 0)
        key_place = lax.broadcasted_iota(jnp.int32, (rows, seen), 1)
        allowed = (key_place <= row_place) & (key_place >= open_ref[here])
        attn_parts, dq_parts, dk_parts, dv_parts = [], [], [], []
        for head in range(2):
            cols = slice(head * HEAD_DIM, (head + 1) * HEAD_DIM)
            q = q_both[:, cols]
            k, v = kb_ref[0:seen, cols], vb_ref[0:seen, cols]
            do = do_ref[here, cols]
            scores = jnp.where(allowed, nt(q, k), masked_score)
            largest = jnp.max(scores, axis=-1, keepdims=True)
            exponent = jnp.exp(scores - largest)
            probs = exponent * (1.0 / jnp.sum(exponent, axis=-1, keepdims=True))
            probs_low = probs.astype(narrow)
            attn_parts.append(nn(probs_low, v))
            grad_probs = nt(do, v)
            inner = jnp.sum(probs * grad_probs, axis=-1, keepdims=True)
            grad_scores = (probs * (grad_probs - inner)).astype(narrow)
            dq_parts.append(nn(grad_scores, k))
            dk_parts.append(tn(grad_scores, q))
            dv_parts.append(tn(probs_low, do))
        attn_ref[here] = jnp.concatenate(attn_parts, axis=1).astype(narrow)
        dq = jnp.concatenate(dq_parts, axis=1) * scale
        gq_ref[here] = turn_back(dq, cosine, sine).astype(narrow)
        dk_ref[0:seen] += jnp.concatenate(dk_parts, axis=1)
        dv_ref[0:seen] += jnp.concatenate(dv_parts, axis=1)
    gk_ref[...] = turn_back(dk_ref[...], cos_ref[...], sin_ref[...]).astype(narrow)
    gv_ref[...] = dv_ref[...].astype(narrow)


def attention(opening, cosine, sine, projected, grad_attn, length):
    tokens, width = grad_attn.shape
    lanes = 2 * HEAD_DIM
    pairs = width // lanes
    rows = min(256, length)
    col = pl.BlockSpec((length, 1), lambda s, h: (s, 0))
    table = pl.BlockSpec((length, lanes), lambda s, h: (s, 0))
    block = pl.BlockSpec((length, lanes), lambda s, h: (s, h))
    k_block = pl.BlockSpec((length, lanes), lambda s, h: (s, pairs + h))
    v_block = pl.BlockSpec((length, lanes), lambda s, h: (s, 2 * pairs + h))
    out = jax.ShapeDtypeStruct((tokens, width), narrow)
    return pl.pallas_call(
        functools.partial(attention_kernel, rows),
        grid=(tokens // length, pairs),
        in_specs=[col, table, table, block, k_block, v_block, block],
        out_specs=[block] * 4,
        out_shape=[out] * 4,
        scratch_shapes=[
            pltpu.VMEM((length, lanes), narrow),
            pltpu.VMEM((length, lanes), narrow),
            pltpu.VMEM((length, lanes), wide),
            pltpu.VMEM((length, lanes), wide),
        ],
        compiler_params=pltpu.CompilerParams(vmem_limit_bytes=48 * MIB),
        cost_estimate=pl.CostEstimate(
            flops=tokens * length * width * 12, bytes_accessed=tokens * width * 32, transcendentals=0
        ),
        name="attention",
    )(opening.reshape(tokens, 1), cosine.reshape(tokens, lanes), sine.reshape(tokens, lanes),
      projected, projected, projected, grad_attn)


def after(value, *earlier):
    return lax.optimization_barrier((value,) + earlier)[0]


def solution(mesh):
    nf = mesh.shape["fsdp"]
    nt_axis = mesh.shape["tp"]
    planes = nf // 2
    swap_f = [(f, f ^ 1) for f in range(nf)]
    up = [(f, f + 2) for f in range(nf - 2)]
    down = [(f + 2, f) for f in range(nf - 2)]
    swap_core = [(t, t ^ 1) for t in range(nt_axis)]
    swap_chip = [(t, t ^ 2) for t in range(nt_axis)]

    def send_x(v):
        return lax.ppermute(v, "fsdp", swap_f)

    def send_y(v):
        return lax.ppermute(v, "tp", swap_chip)

    def send_core(v):
        return lax.ppermute(v, "tp", swap_core)

    def local(
        inputs,
        segments,
        ln_gain,
        ln_bias,
        w_qkv,
        b_qkv,
        w_out,
        b_out,
        w_fc1,
        b_fc1,
        w_fc2,
        b_fc2,
        cotangent,
    ):
        f_place = lax.axis_index("fsdp")
        t_place = lax.axis_index("tp")
        plane, side = f_place // 2, f_place % 2
        chip, core = t_place // 2, t_place % 2
        length = segments.shape[1]
        mine = inputs.shape[0]
        rows = w_fc1.shape[0]
        group = 2 * rows

        def relative(v):
            blocks = v.reshape(v.shape[:-1] + (planes, group))
            flipped = jnp.flip(blocks, axis=-2)
            twice = jnp.concatenate([flipped, flipped], axis=-2)
            cut = lax.dynamic_slice_in_dim(twice, planes - 1 - plane, planes, axis=twice.ndim - 2)
            return cut.reshape(v.shape)

        def pick(v, index, axis=0):
            return lax.dynamic_index_in_dim(v, index, axis, keepdims=False)

        half_qkv, half_ff = w_qkv.shape[2] // 2, w_fc1.shape[1] // 2
        qkv_halves = w_qkv.transpose(1, 0, 2).reshape(rows, 3, 2, half_qkv).transpose(2, 0, 1, 3)
        qkv_halves = qkv_halves.reshape(2, rows, 3 * half_qkv)
        out_halves = w_out.T.reshape(rows, 2, half_qkv).transpose(1, 0, 2)
        qo_halves = jnp.concatenate([qkv_halves, out_halves], axis=2)
        fc1_halves = w_fc1.reshape(rows, 2, half_ff).transpose(1, 0, 2)
        fc2_halves = w_fc2.T.reshape(rows, 2, half_ff).transpose(1, 0, 2)
        quarter = half_ff // 2

        def both_rows(kept, came):
            return jnp.where(
                side == 0, jnp.concatenate([kept, came], 0), jnp.concatenate([came, kept], 0)
            )

        token = [inputs]

        def gather_planes(halves):
            kept, sent = pick(halves, side), pick(halves, 1 - side)
            own = both_rows(kept, send_x(sent))
            ups, downs = [own], [own]
            for step in range(planes - 1):
                to_up, to_down, _ = lax.optimization_barrier((ups[-1], downs[-1], token[0]))
                ups.append(lax.ppermute(to_up, "fsdp", up))
                downs.append(lax.ppermute(to_down, "fsdp", down))
                token[0] = (ups[-1], downs[-1])
            blocks = [own] + [ups[d] + downs[planes - d] for d in range(1, planes)]
            return jnp.concatenate(blocks, axis=0)

        def scatter_planes(grads):
            low = grads.astype(narrow).reshape(planes, group, grads.shape[1])
            going_up = going_down = None
            for step in range(1, planes):
                up_part, down_part = low[step], low[planes - step]
                if going_up is not None:
                    up_part = (up_part.astype(wide) + going_up.astype(wide)).astype(narrow)
                    down_part = (down_part.astype(wide) + going_down.astype(wide)).astype(narrow)
                going_up = lax.ppermute(up_part, "fsdp", up)
                going_down = lax.ppermute(down_part, "fsdp", down)
            total = low[0].astype(wide)
            if going_up is not None:
                total = total + going_up.astype(wide) + going_down.astype(wide)
            parts = total.reshape(2, rows, grads.shape[1])
            came = send_x(pick(parts, 1 - side).astype(narrow)).astype(wide)
            kept = pick(parts, side)
            return jnp.where(side == 0, jnp.stack([kept, came]), jnp.stack([came, kept]))

        def gather_tokens(own, x_last):
            over_y = send_y(own)
            over_x = send_x(own)
            over_both = send_x(over_y) if x_last else send_y(over_x)
            spot = jnp.zeros((2, 2) + own.shape, own.dtype)
            for a, b, v in (
                (side, chip, own),
                (side, 1 - chip, over_y),
                (1 - side, chip, over_x),
                (1 - side, 1 - chip, over_both),
            ):
                spot = lax.dynamic_update_slice(spot, v[None, None], (a, b, 0, 0))
            other = send_core(spot)
            pair = jnp.where(
                core == 0, jnp.stack([spot, other], axis=2), jnp.stack([other, spot], axis=2)
            )
            return pair.reshape(8 * own.shape[0], own.shape[1])

        def scatter_tokens(total):
            parts = total.reshape(2, 2, 2, mine, D)
            came = send_core(pick(parts, 1 - core, 2).astype(narrow))
            summed = pick(parts, core, 2).astype(wide) + came.astype(wide)
            halves = []
            for number, columns in enumerate((summed[..., : D // 2], summed[..., D // 2 :])):
                if number == 0:
                    came = send_x(pick(columns, 1 - side, 0).astype(narrow))
                    part = pick(columns, side, 0) + came.astype(wide)
                    came = send_y(pick(part, 1 - chip, 0).astype(narrow))
                    part = pick(part, chip, 0) + came.astype(wide)
                else:
                    came = send_y(pick(columns, 1 - chip, 1).astype(narrow))
                    part = pick(columns, chip, 1) + came.astype(wide)
                    came = send_x(pick(part, 1 - side, 0).astype(narrow))
                    part = pick(part, side, 0) + came.astype(wide)
                halves.append(part)
            return relative(jnp.concatenate(halves, axis=1))

        def reduce_all(v):
            for axis, size in (("tp", nt_axis), ("fsdp", nf)):
                bit = 1
                while bit < size:
                    v = v + lax.ppermute(v, axis, [(i, i ^ bit) for i in range(size)])
                    bit *= 2
            return v

        tokens_in = inputs.astype(wide)
        normed_local, norm_back = jax.vjp(
            layer_norm, tokens_in, ln_gain.astype(wide), ln_bias.astype(wide)
        )
        normed = gather_tokens(relative(normed_local.astype(narrow)), True)
        grad_rows = gather_tokens(relative(cotangent), False)
        other_segments = send_x(segments)
        both_segments = jnp.where(
            side == 0,
            jnp.concatenate([segments, other_segments], 0),
            jnp.concatenate([other_segments, segments], 0),
        )
        opening = openings(both_segments)
        cosine, sine = rotary_tables(opening)

        full_qo = gather_planes(qo_halves)
        full_fc1a = gather_planes(fc1_halves[:, :, :quarter])
        full_fc2a = gather_planes(fc2_halves[:, :, :quarter])
        full_fc1b = gather_planes(fc1_halves[:, :, quarter:])
        full_fc2b = gather_planes(fc2_halves[:, :, quarter:])

        full_qkv, full_out = full_qo[:, : 3 * half_qkv], full_qo[:, 3 * half_qkv :]
        bias_qkv = lax.dynamic_slice_in_dim(b_qkv, side * half_qkv, half_qkv, axis=1)
        bias_fc1 = lax.dynamic_slice_in_dim(b_fc1, side * half_ff, half_ff, axis=0)

        projected = nn(normed, full_qkv) + bias_qkv.astype(wide).reshape(1, 3 * half_qkv)
        grad_mixed = nn(grad_rows, full_out).astype(narrow)
        mixed, grad_q, grad_k, grad_v = attention(
            opening, cosine, sine, projected, grad_mixed, length
        )
        grad_projected = jnp.concatenate([grad_q, grad_k, grad_v], axis=1)
        grad_qo = jnp.concatenate([tn(normed, grad_projected), tn(grad_rows, mixed)], axis=1)
        sum_qo = scatter_planes(grad_qo)

        sums_fc1, sums_fc2, hidden_sums = [], [], []
        branches = nt(mixed, full_out)
        grad_normed = nt(grad_projected, full_qkv)
        for number, (full_fc1, full_fc2) in enumerate(
            ((full_fc1a, full_fc2a), (full_fc1b, full_fc2b))
        ):
            bias = bias_fc1[number * quarter : (number + 1) * quarter].astype(wide)
            hidden = nn(normed, full_fc1) + bias
            active, gelu_back = jax.vjp(gelu_tanh, hidden)
            active_low = active.astype(narrow)
            sums_fc2.append(scatter_planes(tn(grad_rows, active_low)))
            grad_hidden = gelu_back(nn(grad_rows, full_fc2))[0].astype(narrow)
            sums_fc1.append(scatter_planes(tn(normed, grad_hidden)))
            hidden_sums.append(jnp.sum(grad_hidden.astype(wide), axis=0))
            branches = branches + nt(active_low, full_fc2)
            grad_normed = grad_normed + nt(grad_hidden, full_fc1)

        branch_local = scatter_tokens(branches)
        outputs = (tokens_in + branch_local + b_out.astype(wide) + b_fc2.astype(wide)).astype(narrow)
        grad_tokens, grad_gain, grad_offset = norm_back(scatter_tokens(grad_normed))
        grad_tokens = grad_tokens + cotangent.astype(wide)

        grad_w_qkv = sum_qo[:, :, : 3 * half_qkv].reshape(2, rows, 3, half_qkv)
        grad_w_qkv = grad_w_qkv.transpose(2, 1, 0, 3).reshape(3, rows, 2 * half_qkv)
        grad_w_out = sum_qo[:, :, 3 * half_qkv :].transpose(0, 2, 1).reshape(2 * half_qkv, rows)

        def joined(a, b):
            both = jnp.concatenate([a, b], axis=2)
            return both.transpose(1, 0, 2).reshape(rows, 2 * half_ff)

        grad_w_fc1 = joined(*sums_fc1)
        grad_w_fc2 = joined(*sums_fc2).T

        anchor = jnp.zeros((), jnp.int32)
        bias_qkv_full = lax.dynamic_update_slice(
            jnp.zeros((3, D), wide),
            jnp.sum(grad_projected.astype(wide), axis=0).reshape(3, half_qkv),
            (anchor, (2 * t_place + side) * half_qkv),
        )
        bias_fc1_full = lax.dynamic_update_slice(
            jnp.zeros((FF,), wide),
            jnp.concatenate(hidden_sums),
            ((2 * t_place + side) * half_ff,),
        )
        cotangent_sum = jnp.sum(cotangent.astype(wide), axis=0)
        small = reduce_all(
            jnp.concatenate(
                [bias_qkv_full.reshape(-1), bias_fc1_full, grad_gain, grad_offset, cotangent_sum]
            ).reshape(-1, 128)
        ).reshape(-1)
        total_qkv = small[: 3 * D].reshape(3, D)
        total_fc1 = small[3 * D : 3 * D + FF]
        total_gain, total_offset, total_out = small[3 * D + FF :].reshape(3, D)
        return (
            outputs,
            grad_tokens,
            total_gain,
            total_offset,
            grad_w_qkv,
            total_qkv,
            grad_w_out,
            total_out,
            grad_w_fc1,
            total_fc1,
            grad_w_fc2,
            total_out,
        )

    return jax.shard_map(
        local,
        mesh=mesh,
        in_specs=(
            P(("fsdp", "tp"), None),
            P("fsdp", None),
            P(),
            P(),
            P(None, "fsdp", "tp"),
            P(None, "tp"),
            P("tp", "fsdp"),
            P(),
            P("fsdp", "tp"),
            P("tp"),
            P("tp", "fsdp"),
            P(),
            P(("fsdp", "tp"), None),
        ),
        out_specs=(
            P(("fsdp", "tp"), None),
            P(("fsdp", "tp"), None),
            P(),
            P(),
            P(None, "fsdp", "tp"),
            P(),
            P("tp", "fsdp"),
            P(),
            P("fsdp", "tp"),
            P(),
            P("tp", "fsdp"),
            P(),
        ),
        check_vma=False,
    )
```

time: 1710 us -> 907 us (0.53)
  waiting for transfers between devices: 1370 us -> 238 us
  starting transfers between devices: 0.52 us -> 197 us
  local copies, waits for them, and re-layouts: 27 us -> 126 us
  matrix products: 225 us -> 165 us
  other arithmetic: 63.4 us -> 123 us
  Pallas kernels: 0 us -> 43.1 us
    reduce_scatter x6 -> x0, waiting for transfers between devices: 972 us -> none  [the longest x1 287 us: local(): lax.psum_scatter(grad_w_fc2, 'fsdp', scatter_dimension=1, tiled=True)]
    all_gather x6 -> x0, waiting for transfers between devices: 322 us -> none  [the longest x1 111 us: local(): lax.all_gather(w_fc2, 'fsdp', axis=1, tiled=True)]
    ppermute x0 -> x94, waiting for transfers between devices: none -> 238 us  [the longest x15 58.5 us: gather_planes(): downs.append(lax.ppermute(to_down, 'fsdp', down))]
    ppermute x0 -> x94, starting transfers between devices: none -> 197 us  [the longest x15 62.6 us: scatter_planes(): going_up = lax.ppermute(up_part, 'fsdp', up)]
    psum x1 -> x0, waiting for transfers between devices: 71.7 us -> none  [local(): lax.psum((bias_qkv_full, bias_fc1_full, grad_gain, grad_offset, cotangent...]
    dot_general x24 -> x18, matrix products: 225 us -> 165 us  [the longest x6 86.2 us: nt(): lax.dot_general(a, b, (((1,), (1,)), ((), ())), preferred_element_type=wide)]
    pallas_call x0 -> x1, Pallas kernels: none -> 43.1 us  [attention(): pl.pallas_call(functools.partial(attention_kernel, rows), grid=(tokens //...]
    add x2 -> x36, other arithmetic: 0.02 us -> 41.4 us  [the longest x15 13.7 us: gather_planes(): blocks = [own] + [ups[d] + downs[planes - d] for d in range(1, planes)]]
  transfers between devices with their start and end apart: 13 -> 94, of which waited for: 13 -> 43; matrix products, arithmetic and copies ran while one was open for 15% -> 45% of each run, Pallas kernels for 0% -> 5%
where the time goes in v1:
time: 907 us; the launch traced here: 895 us
  waiting for transfers between devices  238 us (26%)
  starting transfers between devices  197 us (22%)
  matrix products  165 us (18%)
  local copies, waits for them, and re-layouts  126 us (14%)
  other arithmetic  123 us (14%)
  Pallas kernels  43.1 us (5%)
    dot_general x6, matrix products, nt(): lax.dot_general(a, b, (((1,), (1,)), ((), ())), preferred_element_type=wide)  86.2 us
    ppermute x15, starting transfers between devices, scatter_planes(): going_up = lax.ppermute(up_part, 'fsdp', up)  62.6 us
    ppermute x15, starting transfers between devices, gather_planes(): ups.append(lax.ppermute(to_up, 'fsdp', up))  61.8 us
    ppermute x15, waiting for transfers between devices, gather_planes(): downs.append(lax.ppermute(to_down, 'fsdp', down))  58.5 us
    ppermute x15, waiting for transfers between devices, gather_planes(): ups.append(lax.ppermute(to_up, 'fsdp', up))  58 us
    dot_general x6, matrix products, nn(): lax.dot_general(a, b, (((1,), (0,)), ((), ())), preferred_element_type=wide)  43.4 us
    pallas_call x1, Pallas kernels, attention(): pl.pallas_call(functools.partial(attention_kernel, rows), grid=(tokens //...  43.1 us
    ppermute x18, waiting for transfers between devices, send_x(): return lax.ppermute(v, 'fsdp', swap_f)  42.3 us
  transfers between devices with their start and end apart: 94, of which 43 were waited for; matrix products, arithmetic and copies ran while one was open for 45% of the time, Pallas kernels for 5%

profile of v1, /device:TPU:0, one launch (start us, length us, event | category | flops | bytes accessed | tf_op | source)
XLA Modules:
  0.0 895.2 jit_solution(10819432385809141381)
XLA Ops:
  33.0 14.2 %collective-permute-done.5 = bf16[256,1024]{0,1:T(8,128)(2,1)} collective-permute-done((bf16[256,1024]{0,1:T(8,128)(2,1)}, bf16[256,1024]{0,1:T(8,128)(2,1)}, u32[]{:S(2)}, u32[]{:S(2)}) %collective-permute-start.5) | collective-permute-done | bytes 524320 | tf_op jit(solution)/shard_map/ppermute | solution.py:200
  68.2 5.1 collective-permute-done.6
  90.3 11.1 %collective-permute-done.8 = bf16[512,1024]{0,1:T(8,128)(2,1)S(1)} collective-permute-done((bf16[512,1024]{0,1:T(8,128)(2,1)}, bf16[512,1024]{0,1:T(8,128)(2,1)S(1)}, u32[]{:S(2)}, u32[]{:S(2)}) %collective-permute-start.8) | collective-permute-done | bytes 1048608 | tf_op jit(solution)/shard_map/ppermute | solution.py:264
  118.1 11.4 %collective-permute-done.10 = bf16[512,1024]{0,1:T(8,128)(2,1)S(1)} collective-permute-done((bf16[512,1024]{0,1:T(8,128)(2,1)S(1)}, bf16[512,1024]{0,1:T(8,128)(2,1)S(1)}, u32[]{:S(2)}, u32[]{:S(2)}) %collective-permute-start.10) | collective-permute-done | bytes 1048608 | tf_op jit(solution)/shard_map/ppermute | solution.py:265
  131.1 5.2 collective-permute-start.17
  178.9 5.2 collective-permute-start.24
  185.4 5.4 multiply_sine_fusion
  210.5 5.4 collective-permute-start.26
  222.6 10.1 %collective-permute-done.27 = bf16[512,512]{1,0:T(8,128)(2,1)} collective-permute-done((bf16[512,512]{1,0:T(8,128)(2,1)}, bf16[512,512]{1,0:T(8,128)(2,1)}, u32[]{:S(2)}, u32[]{:S(2)}) %collective-permute-start.27) | collective-permute-done | bytes 524320 | tf_op jit(solution)/shard_map/ppermute | solution.py:265
  234.0 5.4 collective-permute-start.29
  241.5 11.8 %maximum_select_fusion.1 = bf16[2,2,2,256,2048]{4,3,1,0,2:T(8,128)(2,1)} fusion(bf16[2,2,1,256,2048]{4,3,1,0,2:T(8,128)(2,1)} %bitcast.21, bf16[2,2,1,256,2048]{4,3,1,0,2:T(8,128)(2,1)} %bitcast.20, pred[]{:T(512)S(6)} %eq.8), kind=kLoop, calls=%fused_computation.3 | loop fusion | flops 12582912 | bytes 16777216 | tf_op jit(solution)/shard_map/jit(_where)/select_n | solution.py:301
  253.3 8.6 copy.79
  261.9 8.0 maximum_select_fusion
  275.4 8.6 broadcast_add_fusion.q_ref.k_ref.v_ref
  284.0 43.1 %attention.1 = (bf16[2048,256]{1,0:T(8,128)(2,1)S(1)}, bf16[2048,256]{1,0:T(8,128)(2,1)S(1)}, bf16[2048,256]{1,0:T(8,128)(2,1)S(1)}, bf16[2048,256]{1,0:T(8,128)(2,1)S(1)}) custom-call(s32[2048,1]{1,0:T(8,128)S(1)} %copy.80.open_ref, f32[2048,128]{1,0:T(8,128)} %concatenate.109.cos_ref, f32[2048,128]{1,0:T(8,128)} %concatenate.110.sin_ref, ...), custom_call_target="tpu_custom_call" | custom-call | flops 6442450944 | bytes 16777216 | tf_op jit(solution)/shard_map/attention/pallas_call | solution.py:164
  327.3 7.4 convolution_convert_fusion
  335.3 13.5 %fusion.18 = f32[2048,2048]{1,0:T(8,128)} fusion(bf16[2048,768]{1,0:T(8,128)(2,1)} %copy-done.15, bf16[2048,1024]{0,1:T(8,128)(2,1)S(1)} %copy-done.23), kind=kOutput, calls=%fused_computation.60 | convolution fusion | flops 6442450944 | bytes 23068672 | tf_op jit(solution)/shard_map/dot_general | solution.py:68
  348.8 5.7 fusion.67
  354.6 6.1 convolution_convert_fusion.2
  368.2 5.5 collective-permute-start.59
  374.4 8.2 fusion.97
  385.5 12.0 %convert_reduce_fusion.2 = (f32[512]{0:T(512)S(1)}, bf16[2048,512]{1,0:T(8,128)(2,1)S(1)}) fusion(bf16[2048,2048]{1,0:T(8,128)(2,1)} %bitcast.218, bf16[512,512]{1,0:T(8,128)(2,1)S(1)} %add.417, bf16[512,512]{1,0:T(8,128)(2,1)S(1)} %copy-done.60, bf16[512,512]{1,0:T(8,128)(2,1)S(1)} %add.415, bf16[512,512]{1,0:T(8,128)(2,1)} %maximum_select_fusion.9, ...), kind=kOutput, calls=%fused_computation.43 | convolution fusion | flops 4331666944 | bytes 16781312 | tf_op jit(solution)/shard_map/dot_general | solution.py:72
  397.5 9.5 %fusion.65 = f32[2048,2048]{1,0:T(8,128)} fusion(bf16[512,512]{1,0:T(8,128)(2,1)S(1)} %add.417, bf16[512,512]{1,0:T(8,128)(2,1)S(1)} %copy-done.60, bf16[512,512]{1,0:T(8,128)(2,1)S(1)} %add.415, bf16[512,512]{1,0:T(8,128)(2,1)} %maximum_select_fusion.9, f32[2048,512]{1,0:T(8,128)S(1)} %copy-done.86, f32[512]{0:T(512)S(1)} %get-tuple-element.164), kind=kOutput, calls=%fused_computation.195 | convolution fusion | flops 4313841664 | bytes 23070720 | tf_op jit(solution)/shard_map/dot_general | solution.py:68
  427.8 9.3 %fusion.66 = f32[2048,2048]{1,0:T(8,128)} fusion(bf16[2048,512]{1,0:T(8,128)(2,1)S(1)} %get-tuple-element.168, bf16[512,512]{1,0:T(8,128)(2,1)S(1)} %copy-done.55, bf16[512,512]{1,0:T(8,128)(2,1)S(1)} %copy-done.51, bf16[512,512]{1,0:T(8,128)(2,1)S(1)} %copy-done.53, bf16[512,512]{1,0:T(8,128)(2,1)} %maximum_select_fusion.8), kind=kOutput, calls=%fused_computation.196 | convolution fusion | flops 4303355904 | bytes 20971520 | tf_op jit(solution)/shard_map/dot_general | solution.py:68
  483.7 5.2 collective-permute-start.68
  491.6 18.9 %collective-permute-done.36 = bf16[512,512]{1,0:T(8,128)(2,1)S(1)} collective-permute-done((bf16[512,512]{1,0:T(8,128)(2,1)S(1)}, bf16[512,512]{1,0:T(8,128)(2,1)S(1)}, u32[]{:S(2)}, u32[]{:S(2)}) %collective-permute-start.36) | collective-permute-done | bytes 524320 | tf_op jit(solution)/shard_map/ppermute | solution.py:264
  515.4 5.7 convolution_convert_fusion.1
  537.2 10.6 %collective-permute-done.38 = bf16[512,512]{1,0:T(8,128)(2,1)S(1)} collective-permute-done((bf16[512,512]{1,0:T(8,128)(2,1)S(1)}, bf16[512,512]{1,0:T(8,128)(2,1)S(1)}, u32[]{:S(2)}, u32[]{:S(2)}) %collective-permute-start.38) | collective-permute-done | bytes 524320 | tf_op jit(solution)/shard_map/ppermute | solution.py:264
  567.1 5.4 collective-permute-start.61
  572.6 13.8 %collective-permute-done.41 = bf16[512,512]{1,0:T(8,128)(2,1)S(1)} collective-permute-done((bf16[512,512]{1,0:T(8,128)(2,1)S(1)}, bf16[512,512]{1,0:T(8,128)(2,1)S(1)}, u32[]{:S(2)}, u32[]{:S(2)}) %collective-permute-start.41) | collective-permute-done | bytes 524320 | tf_op jit(solution)/shard_map/ppermute | solution.py:265
  587.6 5.0 collective-permute-start.43
  605.8 9.2 %convert_reduce_fusion.1 = (f32[512]{0:T(512)S(1)}, bf16[2048,512]{1,0:T(8,128)(2,1)}) fusion(bf16[2048,2048]{1,0:T(8,128)(2,1)S(1)} %bitcast.227, bf16[512,512]{1,0:T(8,128)(2,1)S(1)} %add.428, bf16[512,512]{1,0:T(8,128)(2,1)S(1)} %add.427, bf16[512,512]{1,0:T(8,128)(2,1)S(1)} %add.426, bf16[512,512]{1,0:T(8,128)(2,1)S(1)} %copy-done.32, ...), kind=kOutput, calls=%fused_computation.42 | convolution fusion | flops 4331666944 | bytes 16781312 | tf_op jit(solution)/shard_map/dot_general | solution.py:72
  615.0 23.4 %add_add_fusion.1 = f32[2048,2048]{1,0:T(8,128)} fusion(f32[2048,2048]{1,0:T(8,128)} %fusion.97, f32[2048,2048]{1,0:T(8,128)} %fusion.65, bf16[512,512]{1,0:T(8,128)(2,1)S(1)} %add.428, bf16[512,512]{1,0:T(8,128)(2,1)S(1)} %add.427, bf16[512,512]{1,0:T(8,128)(2,1)S(1)} %add.426, bf16[512,512]{1,0:T(8,128)(2,1)S(1)} %copy-done.32, ...), kind=kOutput, calls=%fused_computation.1 | convolution fusion | flops 4322230272 | bytes 56625152 | tf_op jit(solution)/shard_map/dot_general | solution.py:68
  638.3 6.0 fusion.12
  644.4 22.4 %add_add_fusion = f32[2048,2048]{1,0:T(8,128)} fusion(f32[2048,2048]{1,0:T(8,128)} %fusion.18, f32[2048,2048]{1,0:T(8,128)} %fusion.66, bf16[2048,512]{1,0:T(8,128)(2,1)} %get-tuple-element.166, bf16[512,512]{1,0:T(8,128)(2,1)} %copy-done.30, bf16[512,512]{1,0:T(8,128)(2,1)} %copy-done.28, bf16[512,512]{1,0:T(8,128)(2,1)} %copy-done.29, ...), kind=kOutput, calls=%fused_computation | convolution fusion | flops 4311744512 | bytes 54525952 | tf_op jit(solution)/shard_map/dot_general | solution.py:68
  666.8 8.5 convolution_convert_fusion.3
  683.3 6.0 fusion.13
  704.8 6.6 collective-permute-done.74
  717.4 23.7 %collective-permute-done.77 = bf16[512,512]{1,0:T(8,128)(2,1)} collective-permute-done((bf16[512,512]{1,0:T(8,128)(2,1)}, bf16[512,512]{1,0:T(8,128)(2,1)}, u32[]{:S(2)}, u32[]{:S(2)}) %collective-permute-start.77) | collective-permute-done | bytes 524320 | tf_op jit(solution)/shard_map/ppermute | solution.py:279
  757.2 4.9 collective-permute-done.78
  766.1 5.9 bitcast_add_fusion.1
  776.9 5.9 bitcast_add_fusion
  791.9 9.2 %collective-permute-done.45 = bf16[2,256,1024]{2,1,0:T(8,128)(2,1)} collective-permute-done((bf16[2,256,1024]{2,1,0:T(8,128)(2,1)}, bf16[2,256,1024]{2,1,0:T(8,128)(2,1)}, u32[]{:S(2)}, u32[]{:S(2)}) %collective-permute-start.45) | collective-permute-done | bytes 1048608 | tf_op jit(solution)/shard_map/ppermute | solution.py:200
  806.3 17.2 %collective-permute-done.50 = bf16[2,256,1024]{2,1,0:T(8,128)(2,1)S(1)} collective-permute-done((bf16[2,256,1024]{2,1,0:T(8,128)(2,1)S(1)}, bf16[2,256,1024]{2,1,0:T(8,128)(2,1)S(1)}, u32[]{:S(2)}, u32[]{:S(2)}) %collective-permute-start.50) | collective-permute-done | bytes 1048608 | tf_op jit(solution)/shard_map/ppermute | solution.py:200
  828.0 8.3 collective-permute-done.46
  839.4 5.4 rev.16
  853.0 6.5 rev.17
  859.4 5.2 fusion.87
  (551 shorter events, 417.1 us)
Async XLA Ops:
  8.0 73.1 %collective-permute-start.12 = (bf16[256,2048]{1,0:T(8,128)(2,1)}, bf16[256,2048]{1,0:T(8,128)(2,1)}, u32[]{:S(2)}, u32[]{:S(2)}) collective-permute-start(bf16[256,2048]{1,0:T(8,128)(2,1)} %bitcast.109), channel_id=1, source_target_pairs={{0,2},{1,3},{2,0},{3,1},{4,6},{5,7},{6,4},{7,5},{8,10},{9,11},{10,... | collective-permute-start | bytes 3145736 | tf_op jit(solution)/shard_map/ppermute | solution.py:203
  11.0 54.3 %collective-permute-start.13 = (bf16[256,2048]{1,0:T(8,128)(2,1)}, bf16[256,2048]{1,0:T(8,128)(2,1)}, u32[]{:S(2)}, u32[]{:S(2)}) collective-permute-start(bf16[256,2048]{1,0:T(8,128)(2,1)} %bitcast.109), channel_id=1, source_target_pairs={{0,4},{4,0},{8,12},{12,8},{16,20},{20,16},{24,28},{28,24},{1,5},{5... | collective-permute-start | bytes 3145736 | tf_op jit(solution)/shard_map/ppermute | solution.py:200
  17.0 30.2 %collective-permute-start.5 = (bf16[256,1024]{0,1:T(8,128)(2,1)}, bf16[256,1024]{0,1:T(8,128)(2,1)}, u32[]{:S(2)}, u32[]{:S(2)}) collective-permute-start(bf16[256,1024]{0,1:T(8,128)(2,1)} %get-tuple-element.148), channel_id=1, source_target_pairs={{0,4},{4,0},{8,12},{12,8},{16,20},{20,16},{24,28},{28,24},{1,5},{5... | collective-permute-start | bytes 1572872 | tf_op jit(solution)/shard_map/ppermute | solution.py:200
  26.1 37.6 %collective-permute-start.1 = (bf16[256,2048]{1,0:T(8,128)(2,1)}, bf16[256,2048]{1,0:T(8,128)(2,1)}, u32[]{:S(2)}, u32[]{:S(2)}) collective-permute-start(bf16[256,2048]{1,0:T(8,128)(2,1)} %bitcast.107), channel_id=1, source_target_pairs={{0,2},{1,3},{2,0},{3,1},{4,6},{5,7},{6,4},{7,5},{8,10},{9,11},{10,... | collective-permute-start | bytes 3145736 | tf_op jit(solution)/shard_map/ppermute | solution.py:203
  53.1 25.4 %collective-permute-start.7 = (bf16[512,1024]{0,1:T(8,128)(2,1)S(1)}, bf16[512,1024]{0,1:T(8,128)(2,1)}, u32[]{:S(2)}, u32[]{:S(2)}) collective-permute-start(bf16[512,1024]{0,1:T(8,128)(2,1)S(1)} %maximum_select_fusion.3), channel_id=1, source_target_pairs={{8,0},{12,4},{16,8},{20,12},{24,16},{28,20},{9,1},{13,5},{17,9},{2... | collective-permute-start | bytes 3145736 | tf_op jit(solution)/shard_map/ppermute | solution.py:265
  63.8 43.4 %collective-permute-start.2 = (bf16[256,2048]{1,0:T(8,128)(2,1)}, bf16[256,2048]{1,0:T(8,128)(2,1)S(1)}, u32[]{:S(2)}, u32[]{:S(2)}) collective-permute-start(bf16[256,2048]{1,0:T(8,128)(2,1)} %bitcast.107), channel_id=1, source_target_pairs={{0,4},{4,0},{8,12},{12,8},{16,20},{20,16},{24,28},{28,24},{1,5},{5... | collective-permute-start | bytes 3145736 | tf_op jit(solution)/shard_map/ppermute | solution.py:200
  73.3 39.5 %collective-permute-start.3 = (bf16[256,2048]{1,0:T(8,128)(2,1)}, bf16[256,2048]{1,0:T(8,128)(2,1)S(1)}, u32[]{:S(2)}, u32[]{:S(2)}) collective-permute-start(bf16[256,2048]{1,0:T(8,128)(2,1)} %collective-permute-done.1), channel_id=1, source_target_pairs={{0,4},{4,0},{8,12},{12,8},{16,20},{20,16},{24,28},{28,24},{1,5},{5... | collective-permute-start | bytes 3145736 | tf_op jit(solution)/shard_map/ppermute | solution.py:200
  88.7 26.9 %collective-permute-start.16 = (bf16[256,512]{1,0:T(8,128)(2,1)S(1)}, bf16[256,512]{1,0:T(8,128)(2,1)S(1)}, u32[]{:S(2)}, u32[]{:S(2)}) collective-permute-start(bf16[256,512]{1,0:T(8,128)(2,1)S(1)} %bitcast.252), channel_id=1, source_target_pairs={{0,4},{4,0},{8,12},{12,8},{16,20},{20,16},{24,28},{28,24},{1,5},{5... | collective-permute-start | bytes 786440 | tf_op jit(solution)/shard_map/ppermute | solution.py:200
  101.3 140.1 %collective-permute-start.15 = (bf16[2,2,256,2048]{3,2,1,0:T(8,128)(2,1)}, bf16[2,2,256,2048]{3,2,1,0:T(8,128)(2,1)}, u32[]{:S(2)}, u32[]{:S(2)}) collective-permute-start(bf16[2,2,256,2048]{3,2,1,0:T(8,128)(2,1)} %bitcast_dynamic-update-slice_fusion), channel_id=1, source_target_pairs={{0,1},{1,0},{2,3},{3,2},{4,5},{5,4},{6,7},{7,6},{8,9},{9,8},{10,11... | collective-permute-start | bytes 12582920 | tf_op jit(solution)/shard_map/ppermute | solution.py:206
  113.9 148.0 %collective-permute-start.4 = (bf16[2,2,256,2048]{3,2,1,0:T(8,128)(2,1)}, bf16[2,2,256,2048]{3,2,1,0:T(8,128)(2,1)}, u32[]{:S(2)}, u32[]{:S(2)}) collective-permute-start(bf16[2,2,256,2048]{3,2,1,0:T(8,128)(2,1)} %bitcast_dynamic-update-slice_fusion.3), channel_id=1, source_target_pairs={{0,1},{1,0},{2,3},{3,2},{4,5},{5,4},{6,7},{7,6},{8,9},{9,8},{10,11... | collective-permute-start | bytes 12582920 | tf_op jit(solution)/shard_map/ppermute | solution.py:206
  115.6 40.9 %collective-permute-start = (s32[1,1024]{1,0:T(1,128)S(1)}, s32[1,1024]{1,0:T(1,128)S(1)}, u32[]{:S(2)}, u32[]{:S(2)}) collective-permute-start(s32[1,1024]{1,0:T(1,128)S(1)} %copy-done.82), channel_id=1, source_target_pairs={{0,4},{4,0},{8,12},{12,8},{16,20},{20,16},{24,28},{28,24},{1,5},{5... | collective-permute-start | bytes 12296 | tf_op jit(solution)/shard_map/ppermute | solution.py:200
  175.6 27.9 %collective-permute-start.37 = (bf16[256,512]{1,0:T(8,128)(2,1)}, bf16[256,512]{1,0:T(8,128)(2,1)}, u32[]{:S(2)}, u32[]{:S(2)}) collective-permute-start(bf16[256,512]{1,0:T(8,128)(2,1)} %get-tuple-element.152), channel_id=1, source_target_pairs={{0,4},{4,0},{8,12},{12,8},{16,20},{20,16},{24,28},{28,24},{1,5},{5... | collective-permute-start | bytes 786440 | tf_op jit(solution)/shard_map/ppermute | solution.py:200
  178.9 31.5 %collective-permute-start.24 = (bf16[512,512]{1,0:T(8,128)(2,1)}, bf16[512,512]{1,0:T(8,128)(2,1)}, u32[]{:S(2)}, u32[]{:S(2)}) collective-permute-start(bf16[512,512]{1,0:T(8,128)(2,1)} %maximum_select_fusion.9), channel_id=1, source_target_pairs={{0,8},{4,12},{8,16},{12,20},{16,24},{20,28},{1,9},{5,13},{9,17},{1... | collective-permute-start | bytes 1572872 | tf_op jit(solution)/shard_map/ppermute | solution.py:264
  184.1 26.3 %collective-permute-start.25 = (bf16[512,512]{1,0:T(8,128)(2,1)}, bf16[512,512]{1,0:T(8,128)(2,1)}, u32[]{:S(2)}, u32[]{:S(2)}) collective-permute-start(bf16[512,512]{1,0:T(8,128)(2,1)} %maximum_select_fusion.9), channel_id=1, source_target_pairs={{8,0},{12,4},{16,8},{20,12},{24,16},{28,20},{9,1},{13,5},{17,9},{2... | collective-permute-start | bytes 1572872 | tf_op jit(solution)/shard_map/ppermute | solution.py:265
  232.7 149.8 %collective-permute-start.28 = (bf16[512,512]{1,0:T(8,128)(2,1)}, bf16[512,512]{1,0:T(8,128)(2,1)}, u32[]{:S(2)}, u32[]{:S(2)}) collective-permute-start(bf16[512,512]{1,0:T(8,128)(2,1)} %collective-permute-done.27), channel_id=1, source_target_pairs={{8,0},{12,4},{16,8},{20,12},{24,16},{28,20},{9,1},{13,5},{17,9},{2... | collective-permute-start | bytes 1572872 | tf_op jit(solution)/shard_map/ppermute | solution.py:265
  234.0 150.0 %collective-permute-start.29 = (bf16[512,512]{1,0:T(8,128)(2,1)}, bf16[512,512]{1,0:T(8,128)(2,1)}, u32[]{:S(2)}, u32[]{:S(2)}) collective-permute-start(bf16[512,512]{1,0:T(8,128)(2,1)} %collective-permute-done.26), channel_id=1, source_target_pairs={{0,8},{4,12},{8,16},{12,20},{16,24},{20,28},{1,9},{5,13},{9,17},{1... | collective-permute-start | bytes 1572872 | tf_op jit(solution)/shard_map/ppermute | solution.py:264
  361.8 53.8 %collective-permute-start.80 = (bf16[512,512]{1,0:T(8,128)(2,1)}, bf16[512,512]{1,0:T(8,128)(2,1)S(1)}, u32[]{:S(2)}, u32[]{:S(2)}) collective-permute-start(bf16[512,512]{1,0:T(8,128)(2,1)} %get-tuple-element.120), channel_id=1, source_target_pairs={{0,8},{4,12},{8,16},{12,20},{16,24},{20,28},{1,9},{5,13},{9,17},{1... | collective-permute-start | bytes 1572872 | tf_op jit(solution)/shard_map/ppermute | solution.py:278
  363.1 57.2 %collective-permute-start.83 = (bf16[512,512]{1,0:T(8,128)(2,1)}, bf16[512,512]{1,0:T(8,128)(2,1)S(1)}, u32[]{:S(2)}, u32[]{:S(2)}) collective-permute-start(bf16[512,512]{1,0:T(8,128)(2,1)} %get-tuple-element.121), channel_id=1, source_target_pairs={{8,0},{12,4},{16,8},{20,12},{24,16},{28,20},{9,1},{13,5},{17,9},{2... | collective-permute-start | bytes 1572872 | tf_op jit(solution)/shard_map/ppermute | solution.py:279
  368.2 86.1 %collective-permute-start.59 = (bf16[512,1024]{0,1:T(8,128)(2,1)}, bf16[512,1024]{0,1:T(8,128)(2,1)}, u32[]{:S(2)}, u32[]{:S(2)}) collective-permute-start(bf16[512,1024]{0,1:T(8,128)(2,1)} %pad_maximum_fusion.7), channel_id=1, source_target_pairs={{0,8},{4,12},{8,16},{12,20},{16,24},{20,28},{1,9},{5,13},{9,17},{1... | collective-permute-start | bytes 3145736 | tf_op jit(solution)/shard_map/ppermute | solution.py:278
  415.6 32.5 %collective-permute-start.66 = (bf16[512,512]{1,0:T(8,128)(2,1)S(1)}, bf16[512,512]{1,0:T(8,128)(2,1)S(1)}, u32[]{:S(2)}, u32[]{:S(2)}) collective-permute-start(bf16[512,512]{1,0:T(8,128)(2,1)S(1)} %get-tuple-element.132), channel_id=1, source_target_pairs={{0,8},{4,12},{8,16},{12,20},{16,24},{20,28},{1,9},{5,13},{9,17},{1... | collective-permute-start | bytes 1572872 | tf_op jit(solution)/shard_map/ppermute | solution.py:278
  420.3 32.4 %collective-permute-start.69 = (bf16[512,512]{1,0:T(8,128)(2,1)S(1)}, bf16[512,512]{1,0:T(8,128)(2,1)S(1)}, u32[]{:S(2)}, u32[]{:S(2)}) collective-permute-start(bf16[512,512]{1,0:T(8,128)(2,1)S(1)} %get-tuple-element.133), channel_id=1, source_target_pairs={{8,0},{12,4},{16,8},{20,12},{24,16},{28,20},{9,1},{13,5},{17,9},{2... | collective-permute-start | bytes 1572872 | tf_op jit(solution)/shard_map/ppermute | solution.py:279
  454.3 26.7 %collective-permute-start.67 = (bf16[512,512]{1,0:T(8,128)(2,1)S(1)}, bf16[512,512]{1,0:T(8,128)(2,1)S(1)}, u32[]{:S(2)}, u32[]{:S(2)}) collective-permute-start(bf16[512,512]{1,0:T(8,128)(2,1)S(1)} %get-tuple-element.130), channel_id=1, source_target_pairs={{0,8},{4,12},{8,16},{12,20},{16,24},{20,28},{1,9},{5,13},{9,17},{1... | collective-permute-start | bytes 1572872 | tf_op jit(solution)/shard_map/ppermute | solution.py:278
  463.2 63.8 %collective-permute-start.60 = (bf16[512,1024]{0,1:T(8,128)(2,1)}, bf16[512,1024]{0,1:T(8,128)(2,1)S(1)}, u32[]{:S(2)}, u32[]{:S(2)}) collective-permute-start(bf16[512,1024]{0,1:T(8,128)(2,1)} %fusion.26), channel_id=1, source_target_pairs={{0,8},{4,12},{8,16},{12,20},{16,24},{20,28},{1,9},{5,13},{9,17},{1... | collective-permute-start | bytes 3145736 | tf_op jit(solution)/shard_map/ppermute | solution.py:278
  474.5 36.1 %collective-permute-start.36 = (bf16[512,512]{1,0:T(8,128)(2,1)S(1)}, bf16[512,512]{1,0:T(8,128)(2,1)S(1)}, u32[]{:S(2)}, u32[]{:S(2)}) collective-permute-start(bf16[512,512]{1,0:T(8,128)(2,1)S(1)} %collective-permute-done.33), channel_id=1, source_target_pairs={{0,8},{4,12},{8,16},{12,20},{16,24},{20,28},{1,9},{5,13},{9,17},{1... | collective-permute-start | bytes 1572872 | tf_op jit(solution)/shard_map/ppermute | solution.py:264
  483.7 47.9 %collective-permute-start.68 = (bf16[512,512]{1,0:T(8,128)(2,1)}, bf16[512,512]{1,0:T(8,128)(2,1)}, u32[]{:S(2)}, u32[]{:S(2)}) collective-permute-start(bf16[512,512]{1,0:T(8,128)(2,1)} %get-tuple-element.128), channel_id=1, source_target_pairs={{0,8},{4,12},{8,16},{12,20},{16,24},{20,28},{1,9},{5,13},{9,17},{1... | collective-permute-start | bytes 1572872 | tf_op jit(solution)/shard_map/ppermute | solution.py:278
  490.0 44.4 %collective-permute-start.71 = (bf16[512,512]{1,0:T(8,128)(2,1)}, bf16[512,512]{1,0:T(8,128)(2,1)}, u32[]{:S(2)}, u32[]{:S(2)}) collective-permute-start(bf16[512,512]{1,0:T(8,128)(2,1)} %get-tuple-element.129), channel_id=1, source_target_pairs={{8,0},{12,4},{16,8},{20,12},{24,16},{28,20},{9,1},{13,5},{17,9},{2... | collective-permute-start | bytes 1572872 | tf_op jit(solution)/shard_map/ppermute | solution.py:279
  521.3 33.5 %collective-permute-start.87 = (bf16[512,512]{1,0:T(8,128)(2,1)S(1)}, bf16[512,512]{1,0:T(8,128)(2,1)S(1)}, u32[]{:S(2)}, u32[]{:S(2)}) collective-permute-start(bf16[512,512]{1,0:T(8,128)(2,1)S(1)} %get-tuple-element.126), channel_id=1, source_target_pairs={{0,8},{4,12},{8,16},{12,20},{16,24},{20,28},{1,9},{5,13},{9,17},{1... | collective-permute-start | bytes 1572872 | tf_op jit(solution)/shard_map/ppermute | solution.py:278
  525.7 30.4 %collective-permute-start.90 = (bf16[512,512]{1,0:T(8,128)(2,1)S(1)}, bf16[512,512]{1,0:T(8,128)(2,1)S(1)}, u32[]{:S(2)}, u32[]{:S(2)}) collective-permute-start(bf16[512,512]{1,0:T(8,128)(2,1)S(1)} %get-tuple-element.127), channel_id=1, source_target_pairs={{8,0},{12,4},{16,8},{20,12},{24,16},{28,20},{9,1},{13,5},{17,9},{2... | collective-permute-start | bytes 1572872 | tf_op jit(solution)/shard_map/ppermute | solution.py:279
  534.3 53.3 %collective-permute-start.62 = (bf16[512,1024]{0,1:T(8,128)(2,1)S(1)}, bf16[512,1024]{0,1:T(8,128)(2,1)S(1)}, u32[]{:S(2)}, u32[]{:S(2)}) collective-permute-start(bf16[512,1024]{0,1:T(8,128)(2,1)S(1)} %get-tuple-element.107), channel_id=1, source_target_pairs={{8,0},{12,4},{16,8},{20,12},{24,16},{28,20},{9,1},{13,5},{17,9},{2... | collective-permute-start | bytes 3145736 | tf_op jit(solution)/shard_map/ppermute | solution.py:279
  554.8 31.5 %collective-permute-start.41 = (bf16[512,512]{1,0:T(8,128)(2,1)S(1)}, bf16[512,512]{1,0:T(8,128)(2,1)S(1)}, u32[]{:S(2)}, u32[]{:S(2)}) collective-permute-start(bf16[512,512]{1,0:T(8,128)(2,1)S(1)} %collective-permute-done.39), channel_id=1, source_target_pairs={{8,0},{12,4},{16,8},{20,12},{24,16},{28,20},{9,1},{13,5},{17,9},{2... | collective-permute-start | bytes 1572872 | tf_op jit(solution)/shard_map/ppermute | solution.py:265
  556.4 37.6 %collective-permute-start.88 = (bf16[512,512]{1,0:T(8,128)(2,1)S(1)}, bf16[512,512]{1,0:T(8,128)(2,1)S(1)}, u32[]{:S(2)}, u32[]{:S(2)}) collective-permute-start(bf16[512,512]{1,0:T(8,128)(2,1)S(1)} %get-tuple-element.124), channel_id=1, source_target_pairs={{0,8},{4,12},{8,16},{12,20},{16,24},{20,28},{1,9},{5,13},{9,17},{1... | collective-permute-start | bytes 1572872 | tf_op jit(solution)/shard_map/ppermute | solution.py:278
  561.0 36.6 %collective-permute-start.91 = (bf16[512,512]{1,0:T(8,128)(2,1)S(1)}, bf16[512,512]{1,0:T(8,128)(2,1)S(1)}, u32[]{:S(2)}, u32[]{:S(2)}) collective-permute-start(bf16[512,512]{1,0:T(8,128)(2,1)S(1)} %get-tuple-element.125), channel_id=1, source_target_pairs={{8,0},{12,4},{16,8},{20,12},{24,16},{28,20},{9,1},{13,5},{17,9},{2... | collective-permute-start | bytes 1572872 | tf_op jit(solution)/shard_map/ppermute | solution.py:279
  567.1 179.8 %collective-permute-start.61 = (bf16[512,1024]{0,1:T(8,128)(2,1)}, bf16[512,1024]{0,1:T(8,128)(2,1)}, u32[]{:S(2)}, u32[]{:S(2)}) collective-permute-start(bf16[512,1024]{0,1:T(8,128)(2,1)} %get-tuple-element.106), channel_id=1, source_target_pairs={{0,8},{4,12},{8,16},{12,20},{16,24},{20,28},{1,9},{5,13},{9,17},{1... | collective-permute-start | bytes 3145736 | tf_op jit(solution)/shard_map/ppermute | solution.py:278
  594.0 103.3 %collective-permute-start.63 = (bf16[512,1024]{0,1:T(8,128)(2,1)}, bf16[512,1024]{0,1:T(8,128)(2,1)}, u32[]{:S(2)}, u32[]{:S(2)}) collective-permute-start(bf16[512,1024]{0,1:T(8,128)(2,1)} %fusion.27), channel_id=1, source_target_pairs={{8,0},{12,4},{16,8},{20,12},{24,16},{28,20},{9,1},{13,5},{17,9},{2... | collective-permute-start | bytes 3145736 | tf_op jit(solution)/shard_map/ppermute | solution.py:279
  598.8 76.6 %collective-permute-start.89 = (bf16[512,512]{1,0:T(8,128)(2,1)}, bf16[512,512]{1,0:T(8,128)(2,1)}, u32[]{:S(2)}, u32[]{:S(2)}) collective-permute-start(bf16[512,512]{1,0:T(8,128)(2,1)} %get-tuple-element.122), channel_id=1, source_target_pairs={{0,8},{4,12},{8,16},{12,20},{16,24},{20,28},{1,9},{5,13},{9,17},{1... | collective-permute-start | bytes 1572872 | tf_op jit(solution)/shard_map/ppermute | solution.py:278
  604.2 76.1 %collective-permute-start.92 = (bf16[512,512]{1,0:T(8,128)(2,1)}, bf16[512,512]{1,0:T(8,128)(2,1)}, u32[]{:S(2)}, u32[]{:S(2)}) collective-permute-start(bf16[512,512]{1,0:T(8,128)(2,1)} %get-tuple-element.123), channel_id=1, source_target_pairs={{8,0},{12,4},{16,8},{20,12},{24,16},{28,20},{9,1},{13,5},{17,9},{2... | collective-permute-start | bytes 1572872 | tf_op jit(solution)/shard_map/ppermute | solution.py:279
  644.4 121.8 %collective-permute-start.44 = (bf16[2,2,256,2048]{3,2,1,0:T(8,128)(2,1)}, bf16[2,2,256,2048]{3,2,1,0:T(8,128)(2,1)}, u32[]{:S(2)}, u32[]{:S(2)}) collective-permute-start(bf16[2,2,256,2048]{3,2,1,0:T(8,128)(2,1)} %fusion.12), channel_id=1, source_target_pairs={{0,1},{1,0},{2,3},{3,2},{4,5},{5,4},{6,7},{7,6},{8,9},{9,8},{10,11... | collective-permute-start | bytes 12582920 | tf_op jit(solution)/shard_map/ppermute | solution.py:206
  696.2 80.7 %collective-permute-start.49 = (bf16[2,2,256,2048]{3,2,1,0:T(8,128)(2,1)}, bf16[2,2,256,2048]{3,2,1,0:T(8,128)(2,1)}, u32[]{:S(2)}, u32[]{:S(2)}) collective-permute-start(bf16[2,2,256,2048]{3,2,1,0:T(8,128)(2,1)} %fusion.13), channel_id=1, source_target_pairs={{0,1},{1,0},{2,3},{3,2},{4,5},{5,4},{6,7},{7,6},{8,9},{9,8},{10,11... | collective-permute-start | bytes 12582920 | tf_op jit(solution)/shard_map/ppermute | solution.py:206
  702.4 45.8 %collective-permute-start.64 = (bf16[512,1024]{0,1:T(8,128)(2,1)}, bf16[512,1024]{0,1:T(8,128)(2,1)}, u32[]{:S(2)}, u32[]{:S(2)}) collective-permute-start(bf16[512,1024]{0,1:T(8,128)(2,1)} %add_convert_fusion), channel_id=1, source_target_pairs={{8,0},{12,4},{16,8},{20,12},{24,16},{28,20},{9,1},{13,5},{17,9},{2... | collective-permute-start | bytes 3145736 | tf_op jit(solution)/shard_map/ppermute | solution.py:279
  711.4 29.7 %collective-permute-start.77 = (bf16[512,512]{1,0:T(8,128)(2,1)}, bf16[512,512]{1,0:T(8,128)(2,1)}, u32[]{:S(2)}, u32[]{:S(2)}) collective-permute-start(bf16[512,512]{1,0:T(8,128)(2,1)} %get-tuple-element.137), channel_id=1, source_target_pairs={{8,0},{12,4},{16,8},{20,12},{24,16},{28,20},{9,1},{13,5},{17,9},{2... | collective-permute-start | bytes 1572872 | tf_op jit(solution)/shard_map/ppermute | solution.py:279
  754.4 124.6 %collective-permute-start.65 = (bf16[256,1024]{1,0:T(8,128)(2,1)}, bf16[256,1024]{1,0:T(8,128)(2,1)}, u32[]{:S(2)}, u32[]{:S(2)}) collective-permute-start(bf16[256,1024]{1,0:T(8,128)(2,1)} %fusion.56), channel_id=1, source_target_pairs={{0,4},{4,0},{8,12},{12,8},{16,20},{20,16},{24,28},{28,24},{1,5},{5... | collective-permute-start | bytes 1572872 | tf_op jit(solution)/shard_map/ppermute | solution.py:200
  763.7 25.5 %collective-permute-start.79 = (bf16[256,512]{1,0:T(8,128)(2,1)S(1)}, bf16[256,512]{1,0:T(8,128)(2,1)S(1)}, u32[]{:S(2)}, u32[]{:S(2)}) collective-permute-start(bf16[256,512]{1,0:T(8,128)(2,1)S(1)} %fusion.70), channel_id=1, source_target_pairs={{0,4},{4,0},{8,12},{12,8},{16,20},{20,16},{24,28},{28,24},{1,5},{5... | collective-permute-start | bytes 786440 | tf_op jit(solution)/shard_map/ppermute | solution.py:200
  774.7 26.4 %collective-permute-start.45 = (bf16[2,256,1024]{2,1,0:T(8,128)(2,1)}, bf16[2,256,1024]{2,1,0:T(8,128)(2,1)}, u32[]{:S(2)}, u32[]{:S(2)}) collective-permute-start(bf16[2,256,1024]{2,1,0:T(8,128)(2,1)} %fusion.43), channel_id=1, source_target_pairs={{0,4},{4,0},{8,12},{12,8},{16,20},{20,16},{24,28},{28,24},{1,5},{5... | collective-permute-start | bytes 3145736 | tf_op jit(solution)/shard_map/ppermute | solution.py:200
  776.4 27.1 %collective-permute-start.47 = (bf16[2,256,1024]{2,1,0:T(8,128)(2,1)}, bf16[2,256,1024]{2,1,0:T(8,128)(2,1)}, u32[]{:S(2)}, u32[]{:S(2)}) collective-permute-start(bf16[2,256,1024]{2,1,0:T(8,128)(2,1)} %fusion.44), channel_id=1, source_target_pairs={{0,2},{1,3},{2,0},{3,1},{4,6},{5,7},{6,4},{7,5},{8,10},{9,11},{10,... | collective-permute-start | bytes 3145736 | tf_op jit(solution)/shard_map/ppermute | solution.py:203
  787.7 35.8 %collective-permute-start.50 = (bf16[2,256,1024]{2,1,0:T(8,128)(2,1)S(1)}, bf16[2,256,1024]{2,1,0:T(8,128)(2,1)S(1)}, u32[]{:S(2)}, u32[]{:S(2)}) collective-permute-start(bf16[2,256,1024]{2,1,0:T(8,128)(2,1)S(1)} %fusion.45), channel_id=1, source_target_pairs={{0,4},{4,0},{8,12},{12,8},{16,20},{20,16},{24,28},{28,24},{1,5},{5... | collective-permute-start | bytes 3145736 | tf_op jit(solution)/shard_map/ppermute | solution.py:200
  790.3 35.0 %collective-permute-start.52 = (bf16[2,256,1024]{2,1,0:T(8,128)(2,1)S(1)}, bf16[2,256,1024]{2,1,0:T(8,128)(2,1)S(1)}, u32[]{:S(2)}, u32[]{:S(2)}) collective-permute-start(bf16[2,256,1024]{2,1,0:T(8,128)(2,1)S(1)} %fusion.46), channel_id=1, source_target_pairs={{0,2},{1,3},{2,0},{3,1},{4,6},{5,7},{6,4},{7,5},{8,10},{9,11},{10,... | collective-permute-start | bytes 3145736 | tf_op jit(solution)/shard_map/ppermute | solution.py:203
  802.9 33.5 %collective-permute-start.46 = (bf16[256,1024]{1,0:T(8,128)(2,1)S(1)}, bf16[256,1024]{1,0:T(8,128)(2,1)S(1)}, u32[]{:S(2)}, u32[]{:S(2)}) collective-permute-start(bf16[256,1024]{1,0:T(8,128)(2,1)S(1)} %fusion.52), channel_id=1, source_target_pairs={{0,2},{1,3},{2,0},{3,1},{4,6},{5,7},{6,4},{7,5},{8,10},{9,11},{10,... | collective-permute-start | bytes 1572872 | tf_op jit(solution)/shard_map/ppermute | solution.py:203
  805.4 31.2 %collective-permute-start.48 = (bf16[256,1024]{1,0:T(8,128)(2,1)S(1)}, bf16[256,1024]{1,0:T(8,128)(2,1)S(1)}, u32[]{:S(2)}, u32[]{:S(2)}) collective-permute-start(bf16[256,1024]{1,0:T(8,128)(2,1)S(1)} %fusion.53), channel_id=1, source_target_pairs={{0,4},{4,0},{8,12},{12,8},{16,20},{20,16},{24,28},{28,24},{1,5},{5... | collective-permute-start | bytes 1572872 | tf_op jit(solution)/shard_map/ppermute | solution.py:200
  (139 other events, 2592.8 us)

commit v2 on v1

--- a/solution.py
+++ b/solution.py
@@ -182,17 +182,184 @@
       projected, projected, projected, grad_attn)
 
 
-def after(value, *earlier):
-    return lax.optimization_barrier((value,) + earlier)[0]
+MESH = pl.DeviceIdType.MESH
+
+
+def neighbours():
+    f_place, t_place = lax.axis_index("fsdp"), lax.axis_index("tp")
+    side, chip, core = f_place % 2, t_place // 2, t_place % 2
+    over_x = {"fsdp": f_place + 1 - 2 * side, "tp": t_place}
+    over_y = {"fsdp": f_place, "tp": t_place + 2 - 4 * chip}
+    over_core = {"fsdp": f_place, "tp": t_place + 1 - 2 * core}
+    return side, chip, core, over_x, over_y, over_core
+
+
+def greet(*others):
+    barrier = pltpu.get_barrier_semaphore()
+    for other in others:
+        pl.semaphore_signal(barrier, inc=1, device_id=other, device_id_type=MESH)
+    pl.semaphore_wait(barrier, len(others))
+
+
+class Copies:
+    def __init__(self, send_sems, recv_sems):
+        self.send_sems, self.recv_sems, self.count, self.started = send_sems, recv_sems, 0, []
+
+    def remote(self, source, target, device):
+        copy = pltpu.make_async_remote_copy(
+            src_ref=source,
+            dst_ref=target,
+            send_sem=self.send_sems.at[self.count],
+            recv_sem=self.recv_sems.at[self.count],
+            device_id=device,
+            device_id_type=MESH,
+        )
+        self.count += 1
+        copy.start()
+        self.started.append(copy)
+        return copy
+
+    def local(self, source, target):
+        copy = pltpu.make_async_copy(source, target, self.send_sems.at[self.count])
+        self.count += 1
+        copy.start()
+        return copy
+
+
+def half(ref, which, width):
+    return pl.ds(pl.multiple_of(which * width, 128), width)
+
+
+def exchange_qo_kernel(qkv_ref, out_ref, block_ref, send_sems, recv_sems):
+    side, _, _, over_x, _, _ = neighbours()
+    width = out_ref.shape[1] // 2
+    greet(over_x)
+    copies = Copies(send_sems, recv_sems)
+    kept = []
+    for part in range(4):
+        source = qkv_ref.at[part] if part < 3 else out_ref
+        target = block_ref.at[side, :, pl.ds(part * width, width)]
+        copies.remote(source.at[:, half(source, 1 - side, width)], target, over_x)
+        kept.append(copies.local(source.at[:, half(source, side, width)], target))
+    for copy in kept + copies.started:
+        copy.wait()
+
+
+def exchange_qo(w_qkv, w_out_rows):
+    rows, columns = w_out_rows.shape
+    return pl.pallas_call(
+        exchange_qo_kernel,
+        in_specs=[pl.BlockSpec(memory_space=pl.ANY)] * 2,
+        out_specs=pl.BlockSpec(memory_space=pl.ANY),
+        out_shape=jax.ShapeDtypeStruct((2, rows, 2 * columns), narrow),
+        scratch_shapes=[pltpu.SemaphoreType.DMA((8,)), pltpu.SemaphoreType.DMA((8,))],
+        compiler_params=pltpu.CompilerParams(collective_id=0, has_side_effects=True),
+        name="exchange_qo",
+    )(w_qkv, w_out_rows)
+
+
+def gather_kernel(
+    normed_ref, given_ref, fc1_ref, fc2_ref, normed_all, given_all, fc1_block, fc2_block, send_sems, recv_sems
+):
+    side, chip, core, over_x, over_y, over_core = neighbours()
+    rows = normed_ref.shape[0]
+    cut = rows // 2
+    width = fc1_ref.shape[1] // 2
+    greet(over_x, over_y, over_core)
+    copies = Copies(send_sems, recv_sems)
+    waits = []
+    arrays = ((normed_ref, normed_all), (given_ref, given_all))
+    first = []
+    for own, whole in arrays:
+        mine = whole.at[side, chip, core]
+        first.append((copies.remote(own, mine, over_y), copies.remote(own, mine, over_x)))
+        waits.append(copies.local(own, mine))
+        copies.remote(own, mine, over_core)
+    for weight, block in ((fc1_ref, fc1_block), (fc2_ref, fc2_block)):
+        copies.remote(weight.at[:, half(weight, 1 - side, width)], block.at[side], over_x)
+        waits.append(copies.local(weight.at[:, half(weight, side, width)], block.at[side]))
+    corner = []
+    for number, (_, whole) in enumerate(arrays):
+        from_y, from_x = first[number]
+        y_slot, x_slot = whole.at[side, 1 - chip, core], whole.at[1 - side, chip, core]
+        from_y.wait_recv()
+        if number == 0:
+            part = y_slot.at[pl.ds(0, cut)]
+            a = copies.remote(part, part, over_x)
+        copies.remote(y_slot, y_slot, over_core)
+        from_x.wait_recv()
+        if number == 0:
+            part = x_slot.at[pl.ds(cut, rows - cut)]
+            b = copies.remote(part, part, over_y)
+            corner.append((a, b))
+        else:
+            corner.append((copies.remote(x_slot, x_slot, over_y),))
+        copies.remote(x_slot, x_slot, over_core)
+    for number, (_, whole) in enumerate(arrays):
+        for copy in corner[number]:
+            copy.wait_recv()
+        slot = whole.at[1 - side, 1 - chip, core]
+        copies.remote(slot, slot, over_core)
+    done = [copy for pair in first for copy in pair] + [copy for group in corner for copy in group]
+    for copy in waits:
+        copy.wait()
+    for copy in copies.started:
+        copy.wait_send()
+        if not any(copy is other for other in done):
+            copy.wait_recv()
+
+
+def gather_tokens(normed, given, fc1, fc2_rows):
+    mine, rows = normed.shape[0], fc1.shape[0]
+    whole = jax.ShapeDtypeStruct((2, 2, 2, mine, D), narrow)
+    block = jax.ShapeDtypeStruct((2, rows, fc1.shape[1] // 2), narrow)
+    normed_all, given_all, fc1_block, fc2_block = pl.pallas_call(
+        gather_kernel,
+        in_specs=[pl.BlockSpec(memory_space=pl.ANY)] * 4,
+        out_specs=[pl.BlockSpec(memory_space=pl.ANY)] * 4,
+        out_shape=[whole, whole, block, block],
+        scratch_shapes=[pltpu.SemaphoreType.DMA((24,)), pltpu.SemaphoreType.DMA((24,))],
+        compiler_params=pltpu.CompilerParams(collective_id=1, has_side_effects=True),
+        name="gather_tokens",
+    )(normed, given, fc1, fc2_rows)
+    return normed_all.reshape(8 * mine, D), given_all.reshape(8 * mine, D), fc1_block, fc2_block
+
+
+def product_kernel(count, *refs):
+    total = nt(refs[0][...], refs[count][...])
+    for number in range(1, count):
+        total += nt(refs[number][...], refs[count + number][...])
+    refs[2 * count][...] = total.astype(narrow)
+
+
+def sum_of_products(pairs):
+    tokens = pairs[0][0].shape[0]
+    block = min(256, tokens)
+    left = [pl.BlockSpec((block, a.shape[1]), lambda i: (i, 0)) for a, _, _ in pairs]
+    right = [
+        pl.BlockSpec((w.shape[0], a.shape[1]), functools.partial(lambda c, i: (0, c), c))
+        for a, w, c in pairs
+    ]
+    depth = sum(a.shape[1] for a, _, _ in pairs)
+    return pl.pallas_call(
+        functools.partial(product_kernel, len(pairs)),
+        grid=(tokens // block,),
+        in_specs=left + right,
+        out_specs=pl.BlockSpec((block, D), lambda i: (i, 0)),
+        out_shape=jax.ShapeDtypeStruct((tokens, D), narrow),
+        compiler_params=pltpu.CompilerParams(vmem_limit_bytes=48 * MIB),
+        cost_estimate=pl.CostEstimate(
+            flops=2 * tokens * depth * D, bytes_accessed=2 * depth * (tokens + D), transcendentals=0
+        ),
+        name="sum_of_products",
+    )(*[a for a, _, _ in pairs], *[w for _, w, _ in pairs])
 
 
 def solution(mesh):
     nf = mesh.shape["fsdp"]
     nt_axis = mesh.shape["tp"]
-    planes = nf // 2
+    columns_of_planes = [list(range(side, nf, 2)) for side in range(2)]
     swap_f = [(f, f ^ 1) for f in range(nf)]
-    up = [(f, f + 2) for f in range(nf - 2)]
-    down = [(f + 2, f) for f in range(nf - 2)]
     swap_core = [(t, t ^ 1) for t in range(nt_axis)]
     swap_chip = [(t, t ^ 2) for t in range(nt_axis)]
 
@@ -204,6 +371,12 @@
 
     def send_core(v):
         return lax.ppermute(v, "tp", swap_core)
+
+    def gather_planes(block):
+        block = block.reshape(block.shape[0] * block.shape[1], block.shape[2])
+        return lax.all_gather(
+            block, "fsdp", axis=0, tiled=True, axis_index_groups=columns_of_planes
+        )
 
     def local(
         inputs,
@@ -222,86 +395,30 @@
     ):
         f_place = lax.axis_index("fsdp")
         t_place = lax.axis_index("tp")
-        plane, side = f_place // 2, f_place % 2
+        side = f_place % 2
         chip, core = t_place // 2, t_place % 2
         length = segments.shape[1]
         mine = inputs.shape[0]
         rows = w_fc1.shape[0]
-        group = 2 * rows
-
-        def relative(v):
-            blocks = v.reshape(v.shape[:-1] + (planes, group))
-            flipped = jnp.flip(blocks, axis=-2)
-            twice = jnp.concatenate([flipped, flipped], axis=-2)
-            cut = lax.dynamic_slice_in_dim(twice, planes - 1 - plane, planes, axis=twice.ndim - 2)
-            return cut.reshape(v.shape)
+        half_qkv, half_ff = w_qkv.shape[2] // 2, w_fc1.shape[1] // 2
 
         def pick(v, index, axis=0):
             return lax.dynamic_index_in_dim(v, index, axis, keepdims=False)
 
-        half_qkv, half_ff = w_qkv.shape[2] // 2, w_fc1.shape[1] // 2
-        qkv_halves = w_qkv.transpose(1, 0, 2).reshape(rows, 3, 2, half_qkv).transpose(2, 0, 1, 3)
-        qkv_halves = qkv_halves.reshape(2, rows, 3 * half_qkv)
-        out_halves = w_out.T.reshape(rows, 2, half_qkv).transpose(1, 0, 2)
-        qo_halves = jnp.concatenate([qkv_halves, out_halves], axis=2)
-        fc1_halves = w_fc1.reshape(rows, 2, half_ff).transpose(1, 0, 2)
-        fc2_halves = w_fc2.T.reshape(rows, 2, half_ff).transpose(1, 0, 2)
-        quarter = half_ff // 2
-
-        def both_rows(kept, came):
-            return jnp.where(
-                side == 0, jnp.concatenate([kept, came], 0), jnp.concatenate([came, kept], 0)
+        def in_order(kept, came):
+            return jnp.where(side == 0, jnp.stack([kept, came]), jnp.stack([came, kept]))
+
+        def scatter_planes(grads):
+            total = lax.psum_scatter(
+                grads.astype(narrow),
+                "fsdp",
+                scatter_dimension=0,
+                tiled=True,
+                axis_index_groups=columns_of_planes,
             )
-
-        token = [inputs]
-
-        def gather_planes(halves):
-            kept, sent = pick(halves, side), pick(halves, 1 - side)
-            own = both_rows(kept, send_x(sent))
-            ups, downs = [own], [own]
-            for step in range(planes - 1):
-                to_up, to_down, _ = lax.optimization_barrier((ups[-1], downs[-1], token[0]))
-                ups.append(lax.ppermute(to_up, "fsdp", up))
-                downs.append(lax.ppermute(to_down, "fsdp", down))
-                token[0] = (ups[-1], downs[-1])
-            blocks = [own] + [ups[d] + downs[planes - d] for d in range(1, planes)]
-            return jnp.concatenate(blocks, axis=0)
-
-        def scatter_planes(grads):
-            low = grads.astype(narrow).reshape(planes, group, grads.shape[1])
-            going_up = going_down = None
-            for step in range(1, planes):
-                up_part, down_part = low[step], low[planes - step]
-                if going_up is not None:
-                    up_part = (up_part.astype(wide) + going_up.astype(wide)).astype(narrow)
-                    down_part = (down_part.astype(wide) + going_down.astype(wide)).astype(narrow)
-                going_up = lax.ppermute(up_part, "fsdp", up)
-                going_down = lax.ppermute(down_part, "fsdp", down)
-            total = low[0].astype(wide)
-            if going_up is not None:
-                total = total + going_up.astype(wide) + going_down.astype(wide)
             parts = total.reshape(2, rows, grads.shape[1])
-            came = send_x(pick(parts, 1 - side).astype(narrow)).astype(wide)
-            kept = pick(parts, side)
-            return jnp.where(side == 0, jnp.stack([kept, came]), jnp.stack([came, kept]))
-
-        def gather_tokens(own, x_last):
-            over_y = send_y(own)
-            over_x = send_x(own)
-            over_both = send_x(over_y) if x_last else send_y(over_x)
-            spot = jnp.zeros((2, 2) + own.shape, own.dtype)
-            for a, b, v in (
-                (side, chip, own),
-                (side, 1 - chip, over_y),
-                (1 - side, chip, over_x),
-                (1 - side, 1 - chip, over_both),
-            ):
-                spot = lax.dynamic_update_slice(spot, v[None, None], (a, b, 0, 0))
-            other = send_core(spot)
-            pair = jnp.where(
-                core == 0, jnp.stack([spot, other], axis=2), jnp.stack([other, spot], axis=2)
-            )
-            return pair.reshape(8 * own.shape[0], own.shape[1])
+            came = send_x(pick(parts, 1 - side))
+            return in_order(pick(parts, side), came).astype(wide)
 
         def scatter_tokens(total):
             parts = total.reshape(2, 2, 2, mine, D)
@@ -320,7 +437,7 @@
                     came = send_x(pick(part, 1 - side, 0).astype(narrow))
                     part = pick(part, side, 0) + came.astype(wide)
                 halves.append(part)
-            return relative(jnp.concatenate(halves, axis=1))
+            return jnp.concatenate(halves, axis=1)
 
         def reduce_all(v):
             for axis, size in (("tp", nt_axis), ("fsdp", nf)):
@@ -330,26 +447,19 @@
                     bit *= 2
             return v
 
+        full_qo = gather_planes(exchange_qo(w_qkv, w_out.T))
+
         tokens_in = inputs.astype(wide)
         normed_local, norm_back = jax.vjp(
             layer_norm, tokens_in, ln_gain.astype(wide), ln_bias.astype(wide)
         )
-        normed = gather_tokens(relative(normed_local.astype(narrow)), True)
-        grad_rows = gather_tokens(relative(cotangent), False)
-        other_segments = send_x(segments)
-        both_segments = jnp.where(
-            side == 0,
-            jnp.concatenate([segments, other_segments], 0),
-            jnp.concatenate([other_segments, segments], 0),
-        )
+        normed, grad_rows, fc1_block, fc2_block = gather_tokens(
+            normed_local.astype(narrow), cotangent, w_fc1, w_fc2.T
+        )
+        full_fc1, full_fc2 = gather_planes(fc1_block), gather_planes(fc2_block)
+        both_segments = in_order(segments[0], send_x(segments)[0])
         opening = openings(both_segments)
         cosine, sine = rotary_tables(opening)
-
-        full_qo = gather_planes(qo_halves)
-        full_fc1a = gather_planes(fc1_halves[:, :, :quarter])
-        full_fc2a = gather_planes(fc2_halves[:, :, :quarter])
-        full_fc1b = gather_planes(fc1_halves[:, :, quarter:])
-        full_fc2b = gather_planes(fc2_halves[:, :, quarter:])
 
         full_qkv, full_out = full_qo[:, : 3 * half_qkv], full_qo[:, 3 * half_qkv :]
         bias_qkv = lax.dynamic_slice_in_dim(b_qkv, side * half_qkv, half_qkv, axis=1)
@@ -361,41 +471,34 @@
             opening, cosine, sine, projected, grad_mixed, length
         )
         grad_projected = jnp.concatenate([grad_q, grad_k, grad_v], axis=1)
-        grad_qo = jnp.concatenate([tn(normed, grad_projected), tn(grad_rows, mixed)], axis=1)
+        grad_qo = jnp.concatenate(
+            [tn(normed, grad_projected).astype(narrow), tn(grad_rows, mixed).astype(narrow)], axis=1
+        )
         sum_qo = scatter_planes(grad_qo)
 
-        sums_fc1, sums_fc2, hidden_sums = [], [], []
-        branches = nt(mixed, full_out)
-        grad_normed = nt(grad_projected, full_qkv)
-        for number, (full_fc1, full_fc2) in enumerate(
-            ((full_fc1a, full_fc2a), (full_fc1b, full_fc2b))
-        ):
-            bias = bias_fc1[number * quarter : (number + 1) * quarter].astype(wide)
-            hidden = nn(normed, full_fc1) + bias
-            active, gelu_back = jax.vjp(gelu_tanh, hidden)
-            active_low = active.astype(narrow)
-            sums_fc2.append(scatter_planes(tn(grad_rows, active_low)))
-            grad_hidden = gelu_back(nn(grad_rows, full_fc2))[0].astype(narrow)
-            sums_fc1.append(scatter_planes(tn(normed, grad_hidden)))
-            hidden_sums.append(jnp.sum(grad_hidden.astype(wide), axis=0))
-            branches = branches + nt(active_low, full_fc2)
-            grad_normed = grad_normed + nt(grad_hidden, full_fc1)
-
-        branch_local = scatter_tokens(branches)
+        hidden = nn(normed, full_fc1) + bias_fc1.astype(wide)
+        active, gelu_back = jax.vjp(gelu_tanh, hidden)
+        active_low = active.astype(narrow)
+        sum_fc2 = scatter_planes(tn(grad_rows, active_low))
+        grad_hidden = gelu_back(nn(grad_rows, full_fc2))[0].astype(narrow)
+        sum_fc1 = scatter_planes(tn(normed, grad_hidden))
+        grad_normed = scatter_tokens(
+            sum_of_products(
+                [(grad_q, full_qo, 0), (grad_k, full_qo, 1), (grad_v, full_qo, 2), (grad_hidden, full_fc1, 0)]
+            )
+        )
+        branch_local = scatter_tokens(
+            sum_of_products([(mixed, full_qo, 3), (active_low, full_fc2, 0)])
+        )
         outputs = (tokens_in + branch_local + b_out.astype(wide) + b_fc2.astype(wide)).astype(narrow)
-        grad_tokens, grad_gain, grad_offset = norm_back(scatter_tokens(grad_normed))
+        grad_tokens, grad_gain, grad_offset = norm_back(grad_normed)
         grad_tokens = grad_tokens + cotangent.astype(wide)
 
         grad_w_qkv = sum_qo[:, :, : 3 * half_qkv].reshape(2, rows, 3, half_qkv)
         grad_w_qkv = grad_w_qkv.transpose(2, 1, 0, 3).reshape(3, rows, 2 * half_qkv)
         grad_w_out = sum_qo[:, :, 3 * half_qkv :].transpose(0, 2, 1).reshape(2 * half_qkv, rows)
-
-        def joined(a, b):
-            both = jnp.concatenate([a, b], axis=2)
-            return both.transpose(1, 0, 2).reshape(rows, 2 * half_ff)
-
-        grad_w_fc1 = joined(*sums_fc1)
-        grad_w_fc2 = joined(*sums_fc2).T
+        grad_w_fc1 = sum_fc1.transpose(1, 0, 2).reshape(rows, 2 * half_ff)
+        grad_w_fc2 = sum_fc2.transpose(0, 2, 1).reshape(2 * half_ff, rows)
 
         anchor = jnp.zeros((), jnp.int32)
         bias_qkv_full = lax.dynamic_update_slice(
@@ -405,7 +508,7 @@
         )
         bias_fc1_full = lax.dynamic_update_slice(
             jnp.zeros((FF,), wide),
-            jnp.concatenate(hidden_sums),
+            jnp.sum(grad_hidden.astype(wide), axis=0),
             ((2 * t_place + side) * half_ff,),
         )
         cotangent_sum = jnp.sum(cotangent.astype(wide), axis=0)

time: 907 us -> 581 us (0.64)
  starting transfers between devices: 197 us -> 17.8 us
  Pallas kernels: 43.1 us -> 199 us
  waiting for transfers between devices: 238 us -> 140 us
  other arithmetic: 123 us -> 34.6 us
  matrix products: 165 us -> 96.6 us
  local copies, waits for them, and re-layouts: 126 us -> 74 us
  between operations: 3.61 us -> 15.3 us
    ppermute x60 -> x0, waiting for transfers between devices: 176 us -> none  [the longest x15 58.5 us: gather_planes(): downs.append(lax.ppermute(to_down, 'fsdp', down))]
    ppermute x60 -> x0, starting transfers between devices: 164 us -> none  [the longest x15 62.6 us: scatter_planes(): going_up = lax.ppermute(up_part, 'fsdp', up)]
    pallas_call x0 -> x4, Pallas kernels: none -> 156 us  [the longest x1 98.4 us: gather_tokens(): pl.pallas_call(gather_kernel, in_specs=[pl.BlockSpec(memory_space=pl.ANY)...]
    dot_general x6 -> x0, matrix products: 86.2 us -> none  [nt(): lax.dot_general(a, b, (((1,), (1,)), ((), ())), preferred_element_type=wide)]
    all_gather x0 -> x3, waiting for transfers between devices: none -> 48.9 us  [gather_planes(): lax.all_gather(block, 'fsdp', axis=0, tiled=True, axis_index_groups=colum...]
    select_n x13 -> x1, other arithmetic: 30.1 us -> 0.02 us  [in_order(): jnp.where(side == 0, jnp.stack([kept, came]), jnp.stack([came, kept]))]
    add x20 -> x0, other arithmetic: 21.8 us -> none  [the longest x15 13.7 us: gather_planes(): blocks = [own] + [ups[d] + downs[planes - d] for d in range(1, planes)]]
    ppermute x5, waiting for transfers between devices: 9.91 us -> 27.6 us  [reduce_all(): v = v + lax.ppermute(v, axis, [(i, i ^ bit) for i in range(size)])]
  transfers between devices with their start and end apart: 94 -> 25, of which waited for: 43 -> 12; matrix products, arithmetic and copies ran while one was open for 45% -> 33% of each run, Pallas kernels for 5% -> 31%
where the time goes in v2:
time: 581 us; the launch traced here: 578 us
  Pallas kernels  199 us (34%)
  waiting for transfers between devices  140 us (24%)
  matrix products  96.6 us (17%)
  local copies, waits for them, and re-layouts  74 us (13%)
  other arithmetic  34.6 us (6%)
  starting transfers between devices  17.8 us (3%)
  between operations  15.3 us (3%)
    pallas_call x1, Pallas kernels, gather_tokens(): pl.pallas_call(gather_kernel, in_specs=[pl.BlockSpec(memory_space=pl.ANY)...  98.4 us
    dot_general x4, matrix products, nn(): lax.dot_general(a, b, (((1,), (0,)), ((), ())), preferred_element_type=wide)  54.2 us
    all_gather x3, waiting for transfers between devices, gather_planes(): lax.all_gather(block, 'fsdp', axis=0, tiled=True, axis_index_groups=colum...  48.9 us
    pallas_call x1, Pallas kernels, attention(): pl.pallas_call(functools.partial(attention_kernel, rows), grid=(tokens //...  43.2 us
    dot_general x4, matrix products, tn(): lax.dot_general(a, b, (((0,), (0,)), ((), ())), preferred_element_type=wide)  42.4 us
    ppermute x8, waiting for transfers between devices, send_x(): return lax.ppermute(v, 'fsdp', swap_f)  38.2 us
    pallas_call x2, Pallas kernels, sum_of_products(): pl.pallas_call(functools.partial(product_kernel, len(pairs)), grid=(token...  37.3 us
    ppermute x5, waiting for transfers between devices, reduce_all(): v = v + lax.ppermute(v, axis, [(i, i ^ bit) for i in range(size)])  27.6 us
  transfers between devices with their start and end apart: 25, of which 12 were waited for; matrix products, arithmetic and copies ran while one was open for 33% of the time, Pallas kernels for 31%

profile of v2, /device:TPU:0, one launch (start us, length us, event | category | flops | bytes accessed | tf_op | source)
XLA Modules:
  0.0 577.6 jit_solution(6867987947629575810)
XLA Ops:
  7.2 1.9 copy.81
  9.2 20.1 %exchange_qo.1 = bf16[2,256,1024]{2,1,0:T(8,128)(2,1)} custom-call(bf16[3,256,512]{2,1,0:T(8,128)(2,1)} %qkv_ref.1, bf16[256,512]{1,0:T(8,128)(2,1)} %bitcast.136), custom_call_target="tpu_custom_call" | custom-call | tf_op jit(solution)/shard_map/exchange_qo/pallas_call | solution.py:250
  34.3 98.4 %gather_tokens.1 = (bf16[2,2,2,256,2048]{4,3,2,1,0:T(8,128)(2,1)}, bf16[2,2,2,256,2048]{4,3,2,1,0:T(8,128)(2,1)}, bf16[2,256,1024]{2,1,0:T(8,128)(2,1)}, bf16[2,256,1024]{2,1,0:T(8,128)(2,1)}) custom-call(bf16[256,2048]{1,0:T(8,128)(2,1)} %fusion.18.normed_ref, bf16[256,2048]{1,0:T(8,128)(2,1)} %given_ref.1, bf16[256,2048]{1,0:T(8,128)(2,1)} %fc1_ref.1, ...), custom_call_target="tpu_custom_call" | custom-call | tf_op jit(solution)/shard_map/gather_tokens/pallas_call | solution.py:316
  133.8 2.7 collective-permute-done
  139.1 3.7 multiply_sine_fusion
  143.8 4.5 concatenate.31.cos_ref
  148.4 3.0 concatenate.32.sin_ref
  151.3 7.1 %convolution_convert_fusion.4.do_ref = bf16[2048,256]{1,0:T(8,128)(2,1)} fusion(bf16[2048,2048]{1,0:T(8,128)(2,1)} %bitcast.143, bf16[2048,1024]{1,0:T(8,128)(2,1)} %all-gather.4.cloned.1.call-done.refs_2_.refs_4_.refs_5_.refs_6_), kind=kOutput, calls=%fused_computation.37 | convolution fusion | flops 2148007936 | bytes 10485760 | tf_op jit(solution)/shard_map/dot_general | solution.py:72
  158.5 10.9 %fusion.8.q_ref.k_ref.v_ref = f32[2048,768]{1,0:T(8,128)} fusion(bf16[2048,2048]{1,0:T(8,128)(2,1)} %bitcast.147, bf16[2048,1024]{1,0:T(8,128)(2,1)S(1)} %copy-done.32, f32[768]{0:T(1024)S(1)} %reshape.255), kind=kOutput, calls=%fused_computation.25 | convolution fusion | flops 6444023808 | bytes 17829888 | tf_op jit(solution)/shard_map/dot_general | solution.py:72
  169.4 43.2 %attention.1 = (bf16[2048,256]{1,0:T(8,128)(2,1)S(1)}, bf16[2048,256]{1,0:T(8,128)(2,1)S(1)}, bf16[2048,256]{1,0:T(8,128)(2,1)S(1)}, bf16[2048,256]{1,0:T(8,128)(2,1)S(1)}) custom-call(s32[2048,1]{1,0:T(8,128)S(1)} %copy-done, f32[2048,128]{1,0:T(8,128)} %concatenate.31.cos_ref, f32[2048,128]{1,0:T(8,128)} %concatenate.32.sin_ref, ...), custom_call_target="tpu_custom_call" | custom-call | flops 6442450944 | bytes 16777216 | tf_op jit(solution)/shard_map/attention/pallas_call | solution.py:164
  212.9 7.2 %convolution_convert_fusion.3 = bf16[2048,256]{0,1:T(8,128)(2,1)S(1)} fusion(bf16[2048,2048]{1,0:T(8,128)(2,1)} %bitcast.144, bf16[2048,256]{1,0:T(8,128)(2,1)S(1)} %get-tuple-element.22.refs_0_), kind=kOutput, calls=%fused_computation.36 | convolution fusion | flops 2148007936 | bytes 10485760 | tf_op jit(solution)/shard_map/dot_general | solution.py:76
  220.1 8.0 %convolution_convert_fusion.2 = bf16[2048,768]{0,1:T(8,128)(2,1)S(1)} fusion(bf16[2048,2048]{1,0:T(8,128)(2,1)S(1)} %bitcast.152, bf16[2048,768]{1,0:T(8,128)(2,1)S(1)} %constant_dynamic-update-slice_fusion), kind=kOutput, calls=%fused_computation.22 | convolution fusion | flops 6444023808 | bytes 14680064 | tf_op jit(solution)/shard_map/dot_general | solution.py:76
  228.1 2.6 pad_maximum_fusion
  231.4 14.5 %fusion.45 = f32[2048,1024]{1,0:T(8,128)} fusion(bf16[2048,2048]{1,0:T(8,128)(2,1)} %bitcast.148, bf16[2048,1024]{1,0:T(8,128)(2,1)} %all-gather.6.cloned.1.call-done.refs_7_), kind=kOutput, calls=%fused_computation.131 | convolution fusion | flops 8589934592 | bytes 20971520 | tf_op jit(solution)/shard_map/dot_general | solution.py:72
  245.9 48.9 %all-gather.8.cloned.1.call-done.refs_3_ = bf16[2048,1024]{1,0:T(8,128)(2,1)} async-done(((bf16[512,1024]{1,0:T(8,128)(2,1)}), bf16[2048,1024]{1,0:T(8,128)(2,1)}) %all-gather.8.cloned.1.call-update) | async-done | bytes 4194320 | tf_op jit(solution)/shard_map/all_gather | solution.py:377
  294.8 21.7 %convert_reduce_fusion = (f32[1024]{0:T(1024)S(1)}, bf16[2048,1024]{1,0:T(8,128)(2,1)S(1)}, bf16[2048,1024]{1,0:T(8,128)(2,1)}) fusion(f32[2048,1024]{1,0:T(8,128)} %fusion.45, f32[1024]{0:T(1024)S(1)} %dynamic-slice_convert_fusion.8, bf16[2048,2048]{1,0:T(8,128)(2,1)} %bitcast.145, bf16[2048,1024]{1,0:T(8,128)(2,1)} %all-gather.8.cloned.1.call-done.refs_3_), kind=kOutput, calls=%fused_computation.12 | convolution fusion | flops 8650750976 | bytes 29368320 | tf_op jit(solution)/shard_map/dot_general | solution.py:72
  316.5 2.0 copy-done.33
  318.5 13.0 %convolution_convert_fusion.1 = bf16[2048,1024]{1,0:T(8,128)(2,1)} fusion(bf16[2048,2048]{1,0:T(8,128)(2,1)} %bitcast.149, bf16[2048,1024]{1,0:T(8,128)(2,1)S(1)} %get-tuple-element.68.refs_3_), kind=kOutput, calls=%fused_computation.21 | convolution fusion | flops 8592031744 | bytes 16777216 | tf_op jit(solution)/shard_map/dot_general | solution.py:76
  332.9 2.2 copy-done.3
  335.1 16.1 %sum_of_products.2 = bf16[2048,2048]{1,0:T(8,128)(2,1)} custom-call(bf16[2048,256]{1,0:T(8,128)(2,1)S(1)} %copy-done.2, bf16[2048,1024]{1,0:T(8,128)(2,1)S(1)} %copy-done.3, bf16[2048,1024]{1,0:T(8,128)(2,1)} %all-gather.4.cloned.1.call-done.refs_2_.refs_4_.refs_5_.refs_6_, bf16[2048,1024]{1,0:T(8,128)(2,1)} %all-gather.8.cloned.1.call-done.refs_3_), custom_call_target="tpu_custom_call" | custom-call | flops 10737418240 | bytes 10485760 | tf_op jit(solution)/shard_map/sum_of_products/pallas_call | solution.py:344
  351.2 21.2 %sum_of_products.3 = bf16[2048,2048]{1,0:T(8,128)(2,1)} custom-call(bf16[2048,256]{1,0:T(8,128)(2,1)S(1)} %get-tuple-element.25.refs_0_, bf16[2048,256]{1,0:T(8,128)(2,1)S(1)} %get-tuple-element.26.refs_1_, bf16[2048,256]{1,0:T(8,128)(2,1)S(1)} %get-tuple-element.27.refs_2_, bf16[2048,1024]{1,0:T(8,128)(2,1)} %copy-done.33, ...), custom_call_target="tpu_custom_call" | custom-call | flops 15032385536 | bytes 14680064 | tf_op jit(solution)/shard_map/sum_of_products/pallas_call | solution.py:344
  372.4 9.6 %constant_dynamic-slice_fusion.4 = (bf16[2,2,1,256,2048]{4,3,2,1,0:T(8,128)(2,1)}, bf16[2,2,1,256,2048]{4,3,2,1,0:T(8,128)(2,1)S(1)}, bf16[2,2,1,256,2048]{4,3,2,1,0:T(8,128)(2,1)S(1)}, bf16[2,2,1,256,2048]{4,3,2,1,0:T(8,128)(2,1)}) fusion(bf16[2,2,2,256,2048]{4,3,2,1,0:T(8,128)(2,1)} %bitcast.124, s32[]{:T(128)S(6)} %select_n.105, s32[]{:T(128)S(6)} %select_n.106, ...), kind=kLoop, calls=%fused_computation.110 | loop fusion | bytes 33554440 | tf_op jit(solution)/shard_map/jit(dynamic_index_in_dim)/dynamic_slice | solution.py:406
  382.0 2.3 copy.112
  384.3 2.3 copy.111
  387.1 14.3 %convolution_convert_fusion = bf16[2048,1024]{1,0:T(8,128)(2,1)} fusion(bf16[2048,2048]{1,0:T(8,128)(2,1)} %bitcast.146, bf16[2048,1024]{1,0:T(8,128)(2,1)} %get-tuple-element.71.refs_1_), kind=kOutput, calls=%fused_computation.20 | convolution fusion | flops 8592031744 | bytes 16777216 | tf_op jit(solution)/shard_map/dot_general | solution.py:76
  401.4 5.4 convert_add_fusion.1
  406.8 3.2 fusion.44
  411.8 4.0 convert_add_fusion
  415.7 3.2 fusion.43
  418.9 2.0 copy-done.11
  423.3 1.9 fusion.27
  426.8 1.9 fusion.25
  429.3 7.1 %collective-permute-done.4 = bf16[2,256,1024]{2,1,0:T(8,128)(2,1)} collective-permute-done((bf16[2,256,1024]{2,1,0:T(8,128)(2,1)S(1)}, bf16[2,256,1024]{2,1,0:T(8,128)(2,1)}, u32[]{:S(2)}, u32[]{:S(2)}) %collective-permute-start.4) | collective-permute-done | bytes 1048608 | tf_op jit(solution)/shard_map/ppermute | solution.py:370
  439.7 18.2 %collective-permute-done.9 = bf16[2,256,1024]{2,1,0:T(8,128)(2,1)} collective-permute-done((bf16[2,256,1024]{2,1,0:T(8,128)(2,1)S(1)}, bf16[2,256,1024]{2,1,0:T(8,128)(2,1)}, u32[]{:S(2)}, u32[]{:S(2)}) %collective-permute-start.9) | collective-permute-done | bytes 1048608 | tf_op jit(solution)/shard_map/ppermute | solution.py:370
  463.4 10.4 %collective-permute-done.2 = bf16[2,256,1024]{2,1,0:T(8,128)(2,1)S(1)} collective-permute-done((bf16[2,256,1024]{2,1,0:T(8,128)(2,1)S(1)}, bf16[2,256,1024]{2,1,0:T(8,128)(2,1)S(1)}, u32[]{:S(2)}, u32[]{:S(2)}) %collective-permute-start.2) | collective-permute-done | bytes 1048608 | tf_op jit(solution)/shard_map/ppermute | solution.py:367
  475.1 19.9 %collective-permute-done.10 = bf16[256,1024]{1,0:T(8,128)(2,1)S(1)} collective-permute-done((bf16[256,1024]{1,0:T(8,128)(2,1)S(1)}, bf16[256,1024]{1,0:T(8,128)(2,1)S(1)}, u32[]{:S(2)}, u32[]{:S(2)}) %collective-permute-start.10) | collective-permute-done | bytes 524320 | tf_op jit(solution)/shard_map/ppermute | solution.py:367
  497.3 3.1 convert_reduce_fusion.3
  502.3 4.0 collective-permute-done.12
  507.9 3.0 collective-permute-done.13
  511.0 9.6 %collective-permute-done.14 = f32[160,128]{1,0:T(8,128)S(1)} collective-permute-done((f32[160,128]{1,0:T(8,128)S(1)}, f32[160,128]{1,0:T(8,128)S(1)}, u32[]{:S(2)}, u32[]{:S(2)}) %collective-permute-start.14) | collective-permute-done | bytes 81952 | tf_op jit(solution)/shard_map/ppermute | solution.py:446
  520.6 9.7 %collective-permute-done.15 = f32[160,128]{1,0:T(8,128)S(1)} collective-permute-done((f32[160,128]{1,0:T(8,128)S(1)}, f32[160,128]{1,0:T(8,128)S(1)}, u32[]{:S(2)}, u32[]{:S(2)}) %collective-permute-start.15) | collective-permute-done | bytes 81952 | tf_op jit(solution)/shard_map/ppermute | solution.py:446
  535.4 2.3 constant_dynamic-slice_fusion.1
  538.2 2.1 constant_dynamic-slice_fusion
  541.7 5.2 collective-permute-done.16
  550.5 3.0 copy.89
  553.5 2.7 copy.90
  556.2 3.0 copy.94
  563.8 2.9 copy.95
  (194 shorter events, 53.2 us)
Async XLA Ops:
  7.2 23.5 %copy-start.16 = (bf16[2048,256]{1,0:T(8,128)(2,1)S(1)}, bf16[2048,256]{1,0:T(8,128)(2,1)}, u32[]{:S(2)}) copy-start(bf16[2048,256]{1,0:T(8,128)(2,1)} %param.23) | copy-start | bytes 3145732
  7.2 25.0 %copy-start.4 = (bf16[256,2048]{1,0:T(8,128)(2,1)S(1)}, bf16[256,2048]{1,0:T(8,128)(2,1)}, u32[]{:S(2)}) copy-start(bf16[256,2048]{1,0:T(8,128)(2,1)} %param.13) | copy-start | bytes 3145732
  7.2 144.1 %all-gather.4.cloned.1.call-start = ((), (), s32[]{:S(2)}) async-start(), calls=%async_computation.3 | async-start | bytes 5242880 | tf_op jit(solution)/shard_map/all_gather | solution.py:377
  29.3 202.1 %all-gather.6.cloned.1.call-start = ((), (), s32[]{:S(2)}) async-start(), calls=%async_computation.4 | async-start | bytes 5242880 | tf_op jit(solution)/shard_map/all_gather | solution.py:377
  30.0 102.7 %copy-start.18 = (f32[2048]{0:T(1024)}, f32[2048]{0:T(1024)S(1)}, u32[]{:S(2)}) copy-start(f32[2048]{0:T(1024)S(1)} %convert_element_type.160) | copy-start | bytes 24580
  32.4 100.3 %copy-start.20 = (f32[256]{0:T(256)}, f32[256]{0:T(256)S(1)}, u32[]{:S(2)}) copy-start(f32[256]{0:T(256)S(1)} %broadcast_multiply_fusion) | copy-start | bytes 3076
  32.4 100.4 %copy-start.29 = (s32[1,1024]{1,0:T(1,128)S(1)}, s32[1,1024]{1,0:T(1,128)}, u32[]{:S(2)}) copy-start(s32[1,1024]{1,0:T(1,128)} %param.14) | copy-start | bytes 12292
  32.8 100.7 %copy-start.25 = (f32[256]{0:T(256)}, f32[256]{0:T(256)S(1)}, u32[]{:S(2)}) copy-start(f32[256]{0:T(256)S(1)} %fusion.20) | copy-start | bytes 3076
  32.8 100.6 %copy-start.23 = (f32[256]{0:T(256)}, f32[256]{0:T(256)S(1)}, u32[]{:S(2)}) copy-start(f32[256]{0:T(256)S(1)} %fusion.40) | copy-start | bytes 3076
  32.9 100.9 %copy-start.30 = (bf16[3,512]{1,0:T(4,128)(2,1)S(1)}, bf16[3,512]{1,0:T(4,128)(2,1)}, u32[]{:S(2)}) copy-start(bf16[3,512]{1,0:T(4,128)(2,1)} %param.18) | copy-start | bytes 9220
  132.7 162.1 %all-gather.8.cloned.1.call-start = ((), (), s32[]{:S(2)}) async-start(), calls=%async_computation.5 | async-start | bytes 5242880 | tf_op jit(solution)/shard_map/all_gather | solution.py:377
  132.8 3.7 collective-permute-start
  133.5 396.9 %reduce-scatter.4.cloned.1.call-start = ((), (), s32[]{:S(2)}) async-start(), calls=%async_computation.6 | async-start | bytes 5242880 | tf_op jit(solution)/shard_map/reduce_scatter | solution.py:412
  158.5 10.9 %copy-start = (s32[2048,1]{1,0:T(8,128)S(1)}, s32[2048,1]{1,0:T(8,128)}, u32[]{:S(2)}) copy-start(s32[2048,1]{1,0:T(8,128)} %copy.82.open_ref) | copy-start | bytes 24580
  212.6 7.4 %copy-start.1 = (bf16[2048,256]{1,0:T(8,128)(2,1)}, bf16[2048,256]{1,0:T(8,128)(2,1)S(1)}, u32[]{:S(2)}) copy-start(bf16[2048,256]{1,0:T(8,128)(2,1)S(1)} %get-tuple-element.22.refs_0_) | copy-start | bytes 3145732
  212.8 7.3 %slice-start = ((s8[8388608]{0:T(1024)(128)(4,1)}), s8[4194304]{0:T(1024)(128)(4,1)S(1)}, s32[]{:S(2)}) async-start(s8[8388608]{0:T(1024)(128)(4,1)} %bitcast.150), calls=%async_computation.9 | async-start | bytes 8388608
  212.9 7.2 %copy-start.13 = (bf16[2048,768]{1,0:T(8,128)(2,1)}, bf16[2048,768]{1,0:T(8,128)(2,1)S(1)}, u32[]{:S(2)}) copy-start(bf16[2048,768]{1,0:T(8,128)(2,1)S(1)} %constant_dynamic-update-slice_fusion) | copy-start | bytes 9437188
  212.9 7.2 %slice-start.1 = ((s8[8388608]{0:T(1024)(128)(4,1)}), s8[4194304]{0:T(1024)(128)(4,1)S(1)}, s32[]{:S(2)}) async-start(s8[8388608]{0:T(1024)(128)(4,1)} %bitcast.150), calls=%async_computation.10 | async-start | bytes 8388608
  230.7 304.7 %reduce-scatter.6.cloned.1.call-start = ((), (), s32[]{:S(2)}) async-start(), calls=%async_computation.7 | async-start | bytes 5242880 | tf_op jit(solution)/shard_map/reduce_scatter | solution.py:412
  331.6 206.6 %reduce-scatter.8.cloned.1.call-start = ((), (), s32[]{:S(2)}) async-start(), calls=%async_computation.8 | async-start | bytes 5242880 | tf_op jit(solution)/shard_map/reduce_scatter | solution.py:412
  384.3 17.1 %collective-permute-start.1 = (bf16[2,2,256,2048]{3,2,0,1:T(8,128)(2,1)}, bf16[2,2,256,2048]{3,2,0,1:T(8,128)(2,1)}, u32[]{:S(2)}, u32[]{:S(2)}) collective-permute-start(bf16[2,2,256,2048]{3,2,0,1:T(8,128)(2,1)} %bitcast.120), channel_id=1, source_target_pairs={{0,1},{1,0},{2,3},{3,2},{4,5},{5,4},{6,7},{7,6},{8,9},{9,8},{10,11... | collective-permute-start | bytes 12582920 | tf_op jit(solution)/shard_map/ppermute | solution.py:373
  386.6 25.2 %collective-permute-start.6 = (bf16[2,2,256,2048]{3,2,0,1:T(8,128)(2,1)}, bf16[2,2,256,2048]{3,2,0,1:T(8,128)(2,1)}, u32[]{:S(2)}, u32[]{:S(2)}) collective-permute-start(bf16[2,2,256,2048]{3,2,0,1:T(8,128)(2,1)} %bitcast.119), channel_id=1, source_target_pairs={{0,1},{1,0},{2,3},{3,2},{4,5},{5,4},{6,7},{7,6},{8,9},{9,8},{10,11... | collective-permute-start | bytes 12582920 | tf_op jit(solution)/shard_map/ppermute | solution.py:373
  410.2 26.2 %collective-permute-start.4 = (bf16[2,256,1024]{2,1,0:T(8,128)(2,1)S(1)}, bf16[2,256,1024]{2,1,0:T(8,128)(2,1)}, u32[]{:S(2)}, u32[]{:S(2)}) collective-permute-start(bf16[2,256,1024]{2,1,0:T(8,128)(2,1)S(1)} %fusion.26), channel_id=1, source_target_pairs={{0,2},{1,3},{2,0},{3,1},{4,6},{5,7},{6,4},{7,5},{8,10},{9,11},{10,... | collective-permute-start | bytes 3145736 | tf_op jit(solution)/shard_map/ppermute | solution.py:370
  421.1 36.9 %collective-permute-start.9 = (bf16[2,256,1024]{2,1,0:T(8,128)(2,1)S(1)}, bf16[2,256,1024]{2,1,0:T(8,128)(2,1)}, u32[]{:S(2)}, u32[]{:S(2)}) collective-permute-start(bf16[2,256,1024]{2,1,0:T(8,128)(2,1)S(1)} %fusion.28), channel_id=1, source_target_pairs={{0,2},{1,3},{2,0},{3,1},{4,6},{5,7},{6,4},{7,5},{8,10},{9,11},{10,... | collective-permute-start | bytes 3145736 | tf_op jit(solution)/shard_map/ppermute | solution.py:370
  423.0 13.4 %copy-start.10 = (f32[2,2,256,1024]{3,2,0,1:T(8,128)S(1)}, f32[2,2,256,1024]{3,2,0,1:T(8,128)}, u32[]{:S(2)}) copy-start(f32[2,2,256,1024]{3,2,0,1:T(8,128)} %copy-done.9) | copy-start | bytes 12582916
  425.2 36.1 %collective-permute-start.7 = (bf16[2,256,1024]{2,1,0:T(8,128)(2,1)S(1)}, bf16[2,256,1024]{2,1,0:T(8,128)(2,1)S(1)}, u32[]{:S(2)}, u32[]{:S(2)}) collective-permute-start(bf16[2,256,1024]{2,1,0:T(8,128)(2,1)S(1)} %fusion.27), channel_id=1, source_target_pairs={{0,4},{4,0},{8,12},{12,8},{16,20},{20,16},{24,28},{28,24},{1,5},{5... | collective-permute-start | bytes 3145736 | tf_op jit(solution)/shard_map/ppermute | solution.py:367
  426.8 31.2 %copy-start.12 = (f32[2,2,256,1024]{3,2,0,1:T(8,128)S(1)}, f32[2,2,256,1024]{3,2,0,1:T(8,128)}, u32[]{:S(2)}) copy-start(f32[2,2,256,1024]{3,2,0,1:T(8,128)} %copy-done.11) | copy-start | bytes 12582916
  428.7 45.1 %collective-permute-start.2 = (bf16[2,256,1024]{2,1,0:T(8,128)(2,1)S(1)}, bf16[2,256,1024]{2,1,0:T(8,128)(2,1)S(1)}, u32[]{:S(2)}, u32[]{:S(2)}) collective-permute-start(bf16[2,256,1024]{2,1,0:T(8,128)(2,1)S(1)} %fusion.25), channel_id=1, source_target_pairs={{0,4},{4,0},{8,12},{12,8},{16,20},{20,16},{24,28},{28,24},{1,5},{5... | collective-permute-start | bytes 3145736 | tf_op jit(solution)/shard_map/ppermute | solution.py:367
  438.1 23.2 %copy-start.8 = (f32[2,2,256,1024]{3,2,0,1:T(8,128)S(1)}, f32[2,2,256,1024]{3,2,0,1:T(8,128)}, u32[]{:S(2)}) copy-start(f32[2,2,256,1024]{3,2,0,1:T(8,128)} %get-tuple-element.72) | copy-start | bytes 12582916
  438.2 58.8 %collective-permute-start.5 = (bf16[256,1024]{1,0:T(8,128)(2,1)S(1)}, bf16[256,1024]{1,0:T(8,128)(2,1)S(1)}, u32[]{:S(2)}, u32[]{:S(2)}) collective-permute-start(bf16[256,1024]{1,0:T(8,128)(2,1)S(1)} %fusion.33), channel_id=1, source_target_pairs={{0,4},{4,0},{8,12},{12,8},{16,20},{20,16},{24,28},{28,24},{1,5},{5... | collective-permute-start | bytes 1572872 | tf_op jit(solution)/shard_map/ppermute | solution.py:367
  459.7 14.2 %copy-start.7 = (f32[2,2,256,1024]{3,2,0,1:T(8,128)S(1)}, f32[2,2,256,1024]{3,2,0,1:T(8,128)}, u32[]{:S(2)}) copy-start(f32[2,2,256,1024]{3,2,0,1:T(8,128)} %get-tuple-element.76) | copy-start | bytes 12582916
  459.8 35.3 %collective-permute-start.10 = (bf16[256,1024]{1,0:T(8,128)(2,1)S(1)}, bf16[256,1024]{1,0:T(8,128)(2,1)S(1)}, u32[]{:S(2)}, u32[]{:S(2)}) collective-permute-start(bf16[256,1024]{1,0:T(8,128)(2,1)S(1)} %fusion.35), channel_id=1, source_target_pairs={{0,4},{4,0},{8,12},{12,8},{16,20},{20,16},{24,28},{28,24},{1,5},{5... | collective-permute-start | bytes 1572872 | tf_op jit(solution)/shard_map/ppermute | solution.py:367
  461.8 33.4 %collective-permute-start.8 = (bf16[256,1024]{1,0:T(8,128)(2,1)S(1)}, bf16[256,1024]{1,0:T(8,128)(2,1)S(1)}, u32[]{:S(2)}, u32[]{:S(2)}) collective-permute-start(bf16[256,1024]{1,0:T(8,128)(2,1)S(1)} %fusion.34), channel_id=1, source_target_pairs={{0,2},{1,3},{2,0},{3,1},{4,6},{5,7},{6,4},{7,5},{8,10},{9,11},{10,... | collective-permute-start | bytes 1572872 | tf_op jit(solution)/shard_map/ppermute | solution.py:370
  474.1 21.2 %copy-start.5 = (bf16[256,2048]{1,0:T(8,128)(2,1)S(1)}, bf16[256,2048]{1,0:T(8,128)(2,1)}, u32[]{:S(2)}) copy-start(bf16[256,2048]{1,0:T(8,128)(2,1)} %param.13) | copy-start | bytes 3145732
  474.1 21.2 %copy-start.19 = (f32[2048]{0:T(1024)S(1)}, f32[2048]{0:T(1024)}, u32[]{:S(2)}) copy-start(f32[2048]{0:T(1024)} %copy-done.18) | copy-start | bytes 24580
  474.1 21.2 %copy-start.21 = (f32[256]{0:T(256)S(1)}, f32[256]{0:T(256)}, u32[]{:S(2)}) copy-start(f32[256]{0:T(256)} %copy-done.20) | copy-start | bytes 3076
  474.2 21.6 %copy-start.26 = (f32[256]{0:T(256)S(1)}, f32[256]{0:T(256)}, u32[]{:S(2)}) copy-start(f32[256]{0:T(256)} %copy-done.25) | copy-start | bytes 3076
  474.2 21.6 %copy-start.24 = (f32[256]{0:T(256)S(1)}, f32[256]{0:T(256)}, u32[]{:S(2)}) copy-start(f32[256]{0:T(256)} %copy-done.23) | copy-start | bytes 3076
  474.3 22.9 %collective-permute-start.3 = (bf16[256,1024]{1,0:T(8,128)(2,1)S(1)}, bf16[256,1024]{1,0:T(8,128)(2,1)S(1)}, u32[]{:S(2)}, u32[]{:S(2)}) collective-permute-start(bf16[256,1024]{1,0:T(8,128)(2,1)S(1)} %fusion.32), channel_id=1, source_target_pairs={{0,2},{1,3},{2,0},{3,1},{4,6},{5,7},{6,4},{7,5},{8,10},{9,11},{10,... | collective-permute-start | bytes 1572872 | tf_op jit(solution)/shard_map/ppermute | solution.py:370
  500.4 1.3 collective-permute-start.11
  501.8 4.6 collective-permute-start.12
  506.4 4.5 collective-permute-start.13
  510.9 9.6 %collective-permute-start.14 = (f32[160,128]{1,0:T(8,128)S(1)}, f32[160,128]{1,0:T(8,128)S(1)}, u32[]{:S(2)}, u32[]{:S(2)}) collective-permute-start(f32[160,128]{1,0:T(8,128)S(1)} %add.235), channel_id=1, source_target_pairs={{0,8},{4,12},{8,0},{12,4},{16,24},{20,28},{24,16},{28,20},{1,9},{5... | collective-permute-start | bytes 245768 | tf_op jit(solution)/shard_map/ppermute | solution.py:446
  520.5 9.8 %collective-permute-start.15 = (f32[160,128]{1,0:T(8,128)S(1)}, f32[160,128]{1,0:T(8,128)S(1)}, u32[]{:S(2)}, u32[]{:S(2)}) collective-permute-start(f32[160,128]{1,0:T(8,128)S(1)} %add.236), channel_id=1, source_target_pairs={{0,16},{4,20},{8,24},{12,28},{16,0},{20,4},{24,8},{28,12},{1,17},{... | collective-permute-start | bytes 245768 | tf_op jit(solution)/shard_map/ppermute | solution.py:446
  532.0 14.9 %collective-permute-start.16 = (bf16[256,1024]{1,0:T(8,128)(2,1)S(1)}, bf16[256,1024]{1,0:T(8,128)(2,1)S(1)}, u32[]{:S(2)}, u32[]{:S(2)}) collective-permute-start(bf16[256,1024]{1,0:T(8,128)(2,1)S(1)} %get-tuple-element.85), channel_id=1, source_target_pairs={{0,4},{4,0},{8,12},{12,8},{16,20},{20,16},{24,28},{28,24},{1,5},{5... | collective-permute-start | bytes 1572872 | tf_op jit(solution)/shard_map/ppermute | solution.py:367
  534.1 35.8 %copy-start.22 = (f32[2048]{0:T(1024)}, f32[2048]{0:T(1024)S(1)}, u32[]{:S(2)}) copy-start(f32[2048]{0:T(1024)S(1)} %get-tuple-element.120) | copy-start | bytes 24580
  537.6 22.7 %collective-permute-start.17 = (bf16[256,1024]{1,0:T(8,128)(2,1)}, bf16[256,1024]{1,0:T(8,128)(2,1)}, u32[]{:S(2)}, u32[]{:S(2)}) collective-permute-start(bf16[256,1024]{1,0:T(8,128)(2,1)} %get-tuple-element.83), channel_id=1, source_target_pairs={{0,4},{4,0},{8,12},{12,8},{16,20},{20,16},{24,28},{28,24},{1,5},{5... | collective-permute-start | bytes 1572872 | tf_op jit(solution)/shard_map/ppermute | solution.py:367
  540.3 26.4 %collective-permute-start.18 = (bf16[256,1024]{1,0:T(8,128)(2,1)}, bf16[256,1024]{1,0:T(8,128)(2,1)}, u32[]{:S(2)}, u32[]{:S(2)}) collective-permute-start(bf16[256,1024]{1,0:T(8,128)(2,1)} %get-tuple-element.81), channel_id=1, source_target_pairs={{0,4},{4,0},{8,12},{12,8},{16,20},{20,16},{24,28},{28,24},{1,5},{5... | collective-permute-start | bytes 1572872 | tf_op jit(solution)/shard_map/ppermute | solution.py:367
  (13 other events, 40.4 us)
Sparse Core Ops, SparseCore 0:
  29.4 81.0 all-gather.3
  132.8 81.0 all-gather.5
  215.5 79.2 all-gather.7
  297.0 75.2 reduce-scatter.3
  374.5 77.2 reduce-scatter.5
  454.0 80.7 reduce-scatter.7

commit v3 on v2

--- a/solution.py
+++ b/solution.py
@@ -35,33 +35,13 @@
     return centred * lax.rsqrt(spread + norm_epsilon) * gain + offset
 
 
-def openings(segment_rows):
-    places = jnp.broadcast_to(
-        jnp.arange(segment_rows.shape[1], dtype=jnp.int32)[None], segment_rows.shape
-    )
-    opened = jnp.concatenate(
-        [
-            jnp.ones((segment_rows.shape[0], 1), dtype=jnp.bool_),
-            segment_rows[:, 1:] != segment_rows[:, :-1],
-        ],
-        axis=1,
-    )
-    return lax.cummax(jnp.where(opened, places, jnp.zeros_like(places)), axis=1)
-
-
-def rotary_tables(opening):
-    length = opening.shape[1]
-    places = jnp.arange(length, dtype=jnp.int32)[None]
-    frequency = jnp.exp(jnp.arange(0, ROT, 2, dtype=jnp.float32) * (-math.log(10000.0) / ROT))
-    angles = (places - opening).astype(jnp.float32)[:, :, None] * frequency
-    cosine, sine = jnp.cos(angles), jnp.sin(angles)
-    ones = jnp.ones(angles.shape[:2] + (HEAD_DIM - ROT,), wide)
-    cos_head = jnp.concatenate([cosine, cosine, ones], axis=-1)
-    sin_head = jnp.concatenate([-sine, sine, 0.0 * ones], axis=-1)
-    return (
-        jnp.concatenate([cos_head, cos_head], axis=-1),
-        jnp.concatenate([sin_head, sin_head], axis=-1),
-    )
+def lane_constants():
+    place = jnp.arange(2 * HEAD_DIM, dtype=jnp.int32) % HEAD_DIM
+    turned = (place % (ROT // 2)).astype(wide) * 2.0
+    frequency = jnp.exp(turned * (-math.log(10000.0) / ROT))
+    sign = jnp.where(place < ROT // 2, -1.0, 1.0)
+    inside = place < ROT
+    return jnp.stack([jnp.where(inside, frequency, 0.0), jnp.where(inside, sign, 0.0)])
 
 
 def nt(a, b):
@@ -78,7 +58,7 @@
 
 def attention_kernel(
     rows,
-    open_ref,
+    bound_ref,
     cos_ref,
     sin_ref,
     q_ref,
@@ -111,6 +91,7 @@
     def turn_back(u, cosine, sine):
         return u * cosine - partner(u) * sine
 
+    bound = bound_ref[0, 0:1, 0:1].astype(jnp.int32)
     kb_ref[...] = turn(k_ref[...], cos_ref[...], sin_ref[...]).astype(narrow)
     vb_ref[...] = v_ref[...].astype(narrow)
     dk_ref[...] = jnp.zeros_like(dk_ref)
@@ -122,7 +103,9 @@
         q_both = (turn(q_ref[here], cosine, sine).astype(narrow) * scale).astype(narrow)
         row_place = first + lax.broadcasted_iota(jnp.int32, (rows, seen), 0)
         key_place = lax.broadcasted_iota(jnp.int32, (rows, seen), 1)
-        allowed = (key_place <= row_place) & (key_place >= open_ref[here])
+        row_start = first + lax.broadcasted_iota(jnp.int32, (rows, 1), 0)
+        opening = jnp.where(row_start >= bound, bound, 0)
+        allowed = (key_place <= row_place) & (key_place >= opening)
         attn_parts, dq_parts, dk_parts, dv_parts = [], [], [], []
         for head in range(2):
             cols = slice(head * HEAD_DIM, (head + 1) * HEAD_DIM)
@@ -150,12 +133,12 @@
     gv_ref[...] = dv_ref[...].astype(narrow)
 
 
-def attention(opening, cosine, sine, projected, grad_attn, length):
+def attention(bounds, cosine, sine, projected, grad_attn, length):
     tokens, width = grad_attn.shape
     lanes = 2 * HEAD_DIM
     pairs = width // lanes
     rows = min(256, length)
-    col = pl.BlockSpec((length, 1), lambda s, h: (s, 0))
+    bound = pl.BlockSpec((1, 8, 128), lambda s, h: (s, 0, 0))
     table = pl.BlockSpec((length, lanes), lambda s, h: (s, 0))
     block = pl.BlockSpec((length, lanes), lambda s, h: (s, h))
     k_block = pl.BlockSpec((length, lanes), lambda s, h: (s, pairs + h))
@@ -164,7 +147,7 @@
     return pl.pallas_call(
         functools.partial(attention_kernel, rows),
         grid=(tokens // length, pairs),
-        in_specs=[col, table, table, block, k_block, v_block, block],
+        in_specs=[bound, table, table, block, k_block, v_block, block],
         out_specs=[block] * 4,
         out_shape=[out] * 4,
         scratch_shapes=[
@@ -178,8 +161,7 @@
             flops=tokens * length * width * 12, bytes_accessed=tokens * width * 32, transcendentals=0
         ),
         name="attention",
-    )(opening.reshape(tokens, 1), cosine.reshape(tokens, lanes), sine.reshape(tokens, lanes),
-      projected, projected, projected, grad_attn)
+    )(bounds, cosine, sine, projected, projected, projected, grad_attn)
 
 
 MESH = pl.DeviceIdType.MESH
@@ -196,9 +178,19 @@
 
 def greet(*others):
     barrier = pltpu.get_barrier_semaphore()
-    for other in others:
-        pl.semaphore_signal(barrier, inc=1, device_id=other, device_id_type=MESH)
-    pl.semaphore_wait(barrier, len(others))
+    count = 0
+    for other, there in others:
+        if there is True:
+            pl.semaphore_signal(barrier, inc=1, device_id=other, device_id_type=MESH)
+            count = count + 1
+        else:
+
+            @pl.when(there)
+            def _():
+                pl.semaphore_signal(barrier, inc=1, device_id=other, device_id_type=MESH)
+
+            count = count + there.astype(jnp.int32)
+    pl.semaphore_wait(barrier, count)
 
 
 class Copies:
@@ -226,103 +218,586 @@
         return copy
 
 
-def half(ref, which, width):
+def half(which, width):
     return pl.ds(pl.multiple_of(which * width, 128), width)
 
 
-def exchange_qo_kernel(qkv_ref, out_ref, block_ref, send_sems, recv_sems):
-    side, _, _, over_x, _, _ = neighbours()
+def chain(planes):
+    f_place, t_place = lax.axis_index("fsdp"), lax.axis_index("tp")
+    plane = f_place // 2
+    above = {"fsdp": f_place + 2, "tp": t_place}
+    below = {"fsdp": f_place - 2, "tp": t_place}
+    return plane, above, below, plane < planes - 1, plane > 0
+
+
+class PlaneGather:
+    def __init__(self, planes, whole, send_sems, recv_sems):
+        self.planes, self.whole, self.send_sems, self.recv_sems = planes, whole, send_sems, recv_sems
+        self.plane, above, below, has_above, has_below = chain(planes)
+        self.side = lax.axis_index("fsdp") % 2
+        self.devices, self.has_after = (above, below), (has_above, has_below)
+
+    def spot(self, plane, piece):
+        return self.whole.at[plane, self.side if piece == 0 else 1 - self.side]
+
+    def copy(self, way, step, piece, back):
+        ref = self.spot(self.plane - back if way == 0 else self.plane + back, piece)
+        return pltpu.make_async_remote_copy(
+            src_ref=ref,
+            dst_ref=ref,
+            send_sem=self.send_sems.at[way, step, piece],
+            recv_sem=self.recv_sems.at[way, step, piece],
+            device_id=self.devices[way],
+            device_id_type=MESH,
+        )
+
+    def exists(self, way, back):
+        return self.plane >= back if way == 0 else self.plane + back < self.planes
+
+    def send(self, step, piece):
+        for way in range(2):
+
+            @pl.when(self.has_after[way] & self.exists(way, step - 1))
+            def _():
+                self.copy(way, step, piece, step - 1).start()
+
+    def receive(self, step, piece):
+        for way in range(2):
+
+            @pl.when(self.exists(way, step))
+            def _():
+                self.copy(way, step, piece, step).wait_recv()
+
+    def drain(self):
+        for step in range(1, self.planes):
+            for piece in range(2):
+                for way in range(2):
+
+                    @pl.when(self.has_after[way] & self.exists(way, step - 1))
+                    def _():
+                        self.copy(way, step, piece, step - 1).wait_send()
+
+
+def gather_kernel(
+    planes,
+    input_ref,
+    segment_ref,
+    gain_ref,
+    bias_ref,
+    w_out_ref,
+    w_fc2_ref,
+    lane_ref,
+    given_ref,
+    qkv_ref,
+    fc1_ref,
+    normed_all,
+    given_all,
+    qo_all,
+    fc1_block,
+    fc2_ref,
+    bound_ref,
+    cos_ref,
+    sin_ref,
+    normed_ref,
+    out_ref,
+    send_sems,
+    recv_sems,
+    plane_send_sems,
+    plane_recv_sems,
+):
+    side, chip, core, over_x, over_y, over_core = neighbours()
+    plane, above, below, has_above, has_below = chain(planes)
+    rows = input_ref.shape[0]
+    cut = rows // 2
+    length = segment_ref.shape[1]
+    out_ref[...] = w_out_ref[...].T
+    zeros = length - jnp.sum(segment_ref[...], axis=1, keepdims=True)
+    bound_ref[side] = jnp.broadcast_to(zeros.astype(wide), bound_ref.shape[1:])
+    greet(
+        (over_x, True), (over_y, True), (over_core, True), (above, has_above), (below, has_below)
+    )
+    copies = Copies(send_sems, recv_sems)
+
     width = out_ref.shape[1] // 2
-    greet(over_x)
-    copies = Copies(send_sems, recv_sems)
-    kept = []
+    qo = PlaneGather(planes, qo_all, plane_send_sems, plane_recv_sems)
+    qo_kept, qo_came = [], []
     for part in range(4):
         source = qkv_ref.at[part] if part < 3 else out_ref
-        target = block_ref.at[side, :, pl.ds(part * width, width)]
-        copies.remote(source.at[:, half(source, 1 - side, width)], target, over_x)
-        kept.append(copies.local(source.at[:, half(source, side, width)], target))
-    for copy in kept + copies.started:
+        target = qo_all.at[plane, side, :, pl.ds(part * width, width)]
+        qo_kept.append(copies.local(source.at[:, half(side, width)], target))
+        qo_came.append(copies.remote(source.at[:, half(1 - side, width)], target, over_x))
+    bounds = copies.remote(bound_ref.at[side], bound_ref.at[side], over_x)
+    mine = [whole.at[side, chip, core] for whole in (normed_all, given_all)]
+    y_given = copies.remote(given_ref, mine[1], over_y)
+    for copy in qo_kept:
         copy.wait()
-
-
-def exchange_qo(w_qkv, w_out_rows):
-    rows, columns = w_out_rows.shape
-    return pl.pallas_call(
-        exchange_qo_kernel,
-        in_specs=[pl.BlockSpec(memory_space=pl.ANY)] * 2,
-        out_specs=pl.BlockSpec(memory_space=pl.ANY),
-        out_shape=jax.ShapeDtypeStruct((2, rows, 2 * columns), narrow),
-        scratch_shapes=[pltpu.SemaphoreType.DMA((8,)), pltpu.SemaphoreType.DMA((8,))],
-        compiler_params=pltpu.CompilerParams(collective_id=0, has_side_effects=True),
-        name="exchange_qo",
-    )(w_qkv, w_out_rows)
-
-
-def gather_kernel(
-    normed_ref, given_ref, fc1_ref, fc2_ref, normed_all, given_all, fc1_block, fc2_block, send_sems, recv_sems
-):
-    side, chip, core, over_x, over_y, over_core = neighbours()
-    rows = normed_ref.shape[0]
-    cut = rows // 2
-    width = fc1_ref.shape[1] // 2
-    greet(over_x, over_y, over_core)
-    copies = Copies(send_sems, recv_sems)
-    waits = []
-    arrays = ((normed_ref, normed_all), (given_ref, given_all))
-    first = []
-    for own, whole in arrays:
-        mine = whole.at[side, chip, core]
-        first.append((copies.remote(own, mine, over_y), copies.remote(own, mine, over_x)))
-        waits.append(copies.local(own, mine))
-        copies.remote(own, mine, over_core)
-    for weight, block in ((fc1_ref, fc1_block), (fc2_ref, fc2_block)):
-        copies.remote(weight.at[:, half(weight, 1 - side, width)], block.at[side], over_x)
-        waits.append(copies.local(weight.at[:, half(weight, side, width)], block.at[side]))
-    corner = []
-    for number, (_, whole) in enumerate(arrays):
-        from_y, from_x = first[number]
-        y_slot, x_slot = whole.at[side, 1 - chip, core], whole.at[1 - side, chip, core]
-        from_y.wait_recv()
-        if number == 0:
-            part = y_slot.at[pl.ds(0, cut)]
-            a = copies.remote(part, part, over_x)
-        copies.remote(y_slot, y_slot, over_core)
-        from_x.wait_recv()
-        if number == 0:
-            part = x_slot.at[pl.ds(cut, rows - cut)]
-            b = copies.remote(part, part, over_y)
-            corner.append((a, b))
-        else:
-            corner.append((copies.remote(x_slot, x_slot, over_y),))
-        copies.remote(x_slot, x_slot, over_core)
-    for number, (_, whole) in enumerate(arrays):
-        for copy in corner[number]:
+    qo.send(1, 0)
+
+    tokens = input_ref[...].astype(wide)
+    normed_ref[...] = layer_norm(tokens, gain_ref[...], bias_ref[...]).astype(narrow)
+    x_normed = copies.remote(normed_ref, mine[0], over_x)
+    y_normed = copies.remote(normed_ref, mine[0], over_y)
+    kept = [copies.local(normed_ref, mine[0]), copies.local(given_ref, mine[1])]
+    last = [
+        copies.remote(normed_ref, mine[0], over_core),
+        copies.remote(given_ref, mine[1], over_core),
+    ]
+    for copy in qo_came:
+        copy.wait_recv()
+    qo.send(1, 1)
+    x_given = copies.remote(given_ref, mine[1], over_x)
+    ff_width = fc1_ref.shape[1] // 2
+    kept.append(copies.local(fc1_ref.at[:, half(side, ff_width)], fc1_block.at[side]))
+
+    bounds.wait_recv()
+    step = min(256, length)
+
+    def tables(i, carry):
+        here = pl.ds(pl.multiple_of(i * step, 8), step)
+        sequence, first = i // (length // step), (i % (length // step)) * step
+        place = (first + lax.broadcasted_iota(jnp.int32, (step, 1), 0)).astype(wide)
+        bound = bound_ref[sequence, 0:1, 0:1]
+        angles = (place - jnp.where(place >= bound, bound, 0.0)) * lane_ref[0:1]
+        cos_ref[here] = jnp.cos(angles)
+        sin_ref[here] = jnp.sin(angles) * lane_ref[1:2]
+        return carry
+
+    lax.fori_loop(0, 2 * length // step, tables, 0)
+
+    def forward(step):
+        for piece in range(2):
+            qo.receive(step - 1, piece)
+            qo.send(step, piece)
+
+    if planes > 2:
+        forward(2)
+    fc2_ref[...] = w_fc2_ref[...].T
+    y_slot = [whole.at[side, 1 - chip, core] for whole in (normed_all, given_all)]
+    x_slot = [whole.at[1 - side, chip, core] for whole in (normed_all, given_all)]
+    x_normed.wait_recv()
+    corner = [[copies.remote(x_slot[0], x_slot[0], over_y)]]
+    last.append(copies.remote(x_slot[0], x_slot[0], over_core))
+    y_given.wait_recv()
+    part = y_slot[1].at[pl.ds(0, cut)]
+    corner.append([copies.remote(part, part, over_x)])
+    last.append(
+        copies.remote(fc1_ref.at[:, half(1 - side, ff_width)], fc1_block.at[side], over_x)
+    )
+    last.append(copies.remote(y_slot[1], y_slot[1], over_core))
+    for k in range(3, planes):
+        forward(k)
+    y_normed.wait_recv()
+    last.append(copies.remote(y_slot[0], y_slot[0], over_core))
+    x_given.wait_recv()
+    part = x_slot[1].at[pl.ds(cut, rows - cut)]
+    corner[1].append(copies.remote(part, part, over_y))
+    last.append(copies.remote(x_slot[1], x_slot[1], over_core))
+    for whole, parts in zip((normed_all, given_all), corner):
+        for copy in parts:
             copy.wait_recv()
         slot = whole.at[1 - side, 1 - chip, core]
-        copies.remote(slot, slot, over_core)
-    done = [copy for pair in first for copy in pair] + [copy for group in corner for copy in group]
-    for copy in waits:
+        last.append(copies.remote(slot, slot, over_core))
+    for piece in range(2):
+        qo.receive(planes - 1, piece)
+    for copy in kept:
         copy.wait()
     for copy in copies.started:
         copy.wait_send()
-        if not any(copy is other for other in done):
-            copy.wait_recv()
-
-
-def gather_tokens(normed, given, fc1, fc2_rows):
-    mine, rows = normed.shape[0], fc1.shape[0]
+    qo.drain()
+    for copy in last:
+        copy.wait_recv()
+
+
+def gather_tokens(planes, inputs, segments, gain, bias, given, w_qkv, w_out, fc1, w_fc2):
+    mine, rows, lanes = inputs.shape[0], fc1.shape[0], 2 * HEAD_DIM
+    tokens, length = 8 * mine, segments.shape[1]
+    columns = 2 * w_out.shape[0]
     whole = jax.ShapeDtypeStruct((2, 2, 2, mine, D), narrow)
     block = jax.ShapeDtypeStruct((2, rows, fc1.shape[1] // 2), narrow)
-    normed_all, given_all, fc1_block, fc2_block = pl.pallas_call(
-        gather_kernel,
-        in_specs=[pl.BlockSpec(memory_space=pl.ANY)] * 4,
-        out_specs=[pl.BlockSpec(memory_space=pl.ANY)] * 4,
-        out_shape=[whole, whole, block, block],
-        scratch_shapes=[pltpu.SemaphoreType.DMA((24,)), pltpu.SemaphoreType.DMA((24,))],
-        compiler_params=pltpu.CompilerParams(collective_id=1, has_side_effects=True),
+    table = jax.ShapeDtypeStruct((2 * length, lanes), wide)
+    weights = jax.ShapeDtypeStruct((planes, 2, rows, columns), narrow)
+    anywhere, vmem = pl.BlockSpec(memory_space=pl.ANY), pl.BlockSpec(memory_space=pltpu.VMEM)
+    normed_all, given_all, qo_all, fc1_block, fc2_rows, bounds, cosine, sine = pl.pallas_call(
+        functools.partial(gather_kernel, planes),
+        in_specs=[vmem] * 7 + [anywhere] * 3,
+        out_specs=[anywhere] * 4 + [vmem] * 4,
+        out_shape=[
+            whole,
+            whole,
+            weights,
+            block,
+            jax.ShapeDtypeStruct((rows, w_fc2.shape[0]), narrow),
+            jax.ShapeDtypeStruct((2, 8, 128), wide),
+            table,
+            table,
+        ],
+        scratch_shapes=[
+            pltpu.VMEM((mine, D), narrow),
+            pltpu.VMEM((rows, w_out.shape[0]), narrow),
+            pltpu.SemaphoreType.DMA((32,)),
+            pltpu.SemaphoreType.DMA((32,)),
+            pltpu.SemaphoreType.DMA((2, planes, 2)),
+            pltpu.SemaphoreType.DMA((2, planes, 2)),
+        ],
+        compiler_params=pltpu.CompilerParams(
+            collective_id=1, has_side_effects=True, vmem_limit_bytes=32 * MIB
+        ),
         name="gather_tokens",
-    )(normed, given, fc1, fc2_rows)
-    return normed_all.reshape(8 * mine, D), given_all.reshape(8 * mine, D), fc1_block, fc2_block
+    )(inputs, segments, gain, bias, w_out, w_fc2, lane_constants(), given, w_qkv, fc1)
+    return (
+        normed_all.reshape(tokens, D),
+        given_all.reshape(tokens, D),
+        qo_all.reshape(D, columns),
+        fc1_block,
+        fc2_rows,
+        bounds,
+        cosine,
+        sine,
+    )
+
+
+def scatter_kernel(planes, which, *refs):
+    lefts = sorted(set(which))
+    n_left, n_right = len(lefts), len(which)
+    left_refs, right_refs = refs[:n_left], refs[n_left : n_left + n_right]
+    (
+        fc1_ref,
+        bias_ref,
+        weight_ref,
+        out_ref,
+        weight_all,
+        active_all,
+        slope_all,
+        grad_all,
+        left_vmem,
+        turned,
+        going,
+        came,
+        active_stage,
+        slope_stage,
+        grad_stage,
+        load_sems,
+        send_sems,
+        recv_sems,
+        x_send_sems,
+        x_recv_sems,
+        store_sems,
+    ) = refs[n_left + n_right :]
+    side, _, _, over_x, _, _ = neighbours()
+    plane, above, below, has_above, has_below = chain(planes)
+    devices, has_after, has_before = (above, below), (has_above, has_below), (has_below, has_above)
+    group, width = out_ref.shape[1], right_refs[0].shape[1]
+    tokens = right_refs[0].shape[0]
+    own = out_ref
+
+    def load(j):
+        return [
+            pltpu.make_async_copy(
+                left_refs[i].at[:, pl.ds(pl.multiple_of(j * group, 128), group)],
+                left_vmem.at[i, j],
+                load_sems.at[i, j],
+            )
+            for i in range(n_left)
+        ]
+
+    def order(k):
+        return jnp.where(plane < planes // 2, planes - 1 - k, k)
+
+    for k in range(planes):
+        for copy in load(order(k)):
+            copy.start()
+    greet((over_x, True), (above, has_above), (below, has_below))
+    copies = Copies(x_send_sems, x_recv_sems)
+    columns = weight_ref.shape[1] // 2
+    kept = copies.local(weight_ref.at[:, half(side, columns)], weight_all.at[plane, side])
+    other = copies.remote(
+        weight_ref.at[:, half(1 - side, columns)], weight_all.at[plane, side], over_x
+    )
+
+    def depth(way):
+        return plane if way == 0 else planes - 1 - plane
+
+    def named(way, block):
+        return block if way == 0 else planes - 1 - block
+
+    def is_weight(at, number):
+        return (number <= at) | (number == at + 2)
+
+    def weight_block(at, number):
+        return jnp.where(number <= at, at - number + 1, 0)
+
+    def sum_block(at, number):
+        return jnp.where(number == at + 1, planes - 1, planes + 1 + at - number)
+
+    def weight_copies(way, number, at, pieces=(0, 1)):
+        j = named(way, weight_block(at, number))
+        return [
+            pltpu.make_async_remote_copy(
+                src_ref=weight_all.at[j, piece_side],
+                dst_ref=weight_all.at[j, piece_side],
+                send_sem=send_sems.at[way, number, piece],
+                recv_sem=recv_sems.at[way, number, piece],
+                device_id=devices[way],
+                device_id_type=MESH,
+            )
+            for piece, piece_side in enumerate((side, 1 - side))
+            if piece in pieces
+        ]
+
+    def landing(way, j, receiver):
+        return j if way == 0 else jnp.where(j == receiver, planes, j)
+
+    def sum_copy(way, number, at, receiver, arriving):
+        j = named(way, sum_block(at, number))
+        spot = landing(way, j, receiver)
+        return j, spot, pltpu.make_async_remote_copy(
+            src_ref=came.at[spot] if arriving else going.at[j],
+            dst_ref=came.at[spot],
+            send_sem=send_sems.at[way, number, 2],
+            recv_sem=recv_sems.at[way, number, 2],
+            device_id=devices[way],
+            device_id_type=MESH,
+        )
+
+    def next_plane(way):
+        return plane + 1 if way == 0 else plane - 1
+
+    def finish_send(way, number):
+        at = depth(way)
+
+        @pl.when(has_after[way] & is_weight(at, number))
+        def _():
+            for copy in weight_copies(way, number, at):
+                copy.wait_send()
+
+        @pl.when(has_after[way] & jnp.logical_not(is_weight(at, number)))
+        def _():
+            sum_copy(way, number, at, next_plane(way), False)[2].wait_send()
+
+    def take(way, number):
+        at = depth(way) - 1
+
+        @pl.when(has_before[way] & is_weight(at, number))
+        def _():
+            for copy in weight_copies(way, number, at):
+                copy.wait_recv()
+
+        @pl.when(has_before[way] & jnp.logical_not(is_weight(at, number)))
+        def _():
+            j, spot, copy = sum_copy(way, number, at, plane, True)
+            copy.wait_recv()
+
+            @pl.when(j == plane)
+            def _():
+                own[...] += came[spot].astype(wide)
+
+            @pl.when(j != plane)
+            def _():
+                going[j] = (going[j].astype(wide) + came[spot].astype(wide)).astype(narrow)
+
+    def give(way, number):
+        at = depth(way)
+
+        @pl.when(has_after[way] & is_weight(at, number))
+        def _():
+            for copy in weight_copies(way, number, at):
+                copy.start()
+
+        @pl.when(has_after[way] & jnp.logical_not(is_weight(at, number)))
+        def _():
+            sum_copy(way, number, at, next_plane(way), False)[2].start()
+
+    step = slope_stage.shape[1]
+    blocks = tokens // step
+
+    def turn(i, carry):
+        here = pl.ds(pl.multiple_of(i * step, 128), step)
+        for number, right_ref in enumerate(right_refs):
+            turned[number * width : (number + 1) * width, here] = right_ref[here].T
+        return carry
+
+    def multiply(k):
+        j = order(k)
+        for copy in load(j):
+            copy.wait()
+        for i in range(n_left):
+            numbers = [number for number, left in enumerate(which) if left == lefts[i]]
+            here = slice(numbers[0] * width, (numbers[-1] + 1) * width)
+            block = nn(turned[here], left_vmem[i, j])
+            going[j, here] = block.astype(narrow)
+
+            @pl.when(j == plane)
+            def _():
+                own[here] = block
+
+    def store_hidden(i, slot):
+        here = pl.ds(pl.multiple_of(i * step, 16), step)
+        return [
+            pltpu.make_async_copy(slope_stage.at[slot], slope_all.at[here], store_sems.at[0, slot]),
+            pltpu.make_async_copy(active_stage.at[slot], active_all.at[here], store_sems.at[1, slot]),
+        ]
+
+    def hidden_units(i, carry):
+        here = pl.ds(pl.multiple_of(i * step, 128), step)
+        slot = i % 2
+        hidden = bias_ref[...] + nn(left_vmem[0, 0, here], fc1_ref[0:group])
+        for j in range(1, planes):
+            hidden += nn(left_vmem[0, j, here], fc1_ref[j * group : (j + 1) * group])
+        squared = hidden * hidden
+        inner = jnp.tanh(0.7978845608028654 * hidden * (1.0 + 0.044715 * squared))
+        half_sum = 0.5 * (1.0 + inner)
+        active = (hidden * half_sum).astype(narrow)
+
+        @pl.when(i >= 2)
+        def _():
+            for copy in store_hidden(i - 2, slot):
+                copy.wait()
+
+        active_stage[slot] = active
+        slope_stage[slot] = half_sum + hidden * (0.5 * (1.0 - inner * inner)) * (
+            0.7978845608028654 * (1.0 + 3.0 * 0.044715 * squared)
+        )
+        for copy in store_hidden(i, slot):
+            copy.start()
+        turned[:, here] = active.T
+        return carry
+
+    def store_grad(j, slot):
+        return pltpu.make_async_copy(grad_stage.at[slot], grad_all.at[j], store_sems.at[2, slot])
+
+    def fc2_gradient(j, carry):
+        slot = j % 2
+
+        @pl.when(j >= 2)
+        def _():
+            store_grad(j - 2, slot).wait()
+
+        grad_stage[slot] = nn(turned[...], left_vmem[n_left - 1, j]).astype(narrow)
+        store_grad(j, slot).start()
+        return carry
+
+    kept.wait()
+    for way in range(2):
+
+        @pl.when(has_after[way] & (depth(way) > 0))
+        def _():
+            weight_copies(way, 1, depth(way), (0,))[0].start()
+
+    lax.fori_loop(0, blocks, turn, 0)
+    multiply(0)
+    for way in range(2):
+
+        @pl.when(has_after[way] & (depth(way) == 0))
+        def _():
+            sum_copy(way, 1, 0, next_plane(way), False)[2].start()
+
+    other.wait_recv()
+    for way in range(2):
+
+        @pl.when(has_after[way] & (depth(way) > 0))
+        def _():
+            weight_copies(way, 1, depth(way), (1,))[0].start()
+
+    for k in range(1, planes):
+        multiply(k)
+
+    lax.fori_loop(0, blocks // 2, hidden_units, 0)
+    for number in range(2, planes + 1):
+        for way in range(2):
+            take(way, number - 1)
+            finish_send(way, number - 1)
+            give(way, number)
+        if number == 2:
+            lax.fori_loop(blocks // 2, blocks, hidden_units, 0)
+            lax.fori_loop(0, planes // 2, fc2_gradient, 0)
+        if number == min(3, planes):
+            lax.fori_loop(planes // 2, planes, fc2_gradient, 0)
+    for way in range(2):
+        take(way, planes)
+    for way in range(2):
+        finish_send(way, planes)
+    for slot in range(2):
+        for copy in store_hidden(blocks - 2 + slot, slot) + [store_grad(planes - 2 + slot, slot)]:
+            copy.wait()
+    for copy in copies.started:
+        copy.wait_send()
+
+
+def backward_step(planes, lefts, rights, which, fc1, bias, weight, collective_id):
+    tokens, width = rights[0].shape
+    group, columns, hidden = D // planes, width * len(rights), fc1.shape[1]
+    rows, step = group // 2, min(256, tokens // 2)
+    anywhere, vmem = pl.BlockSpec(memory_space=pl.ANY), pl.BlockSpec(memory_space=pltpu.VMEM)
+    total, weight_all, active, slope, grad = pl.pallas_call(
+        functools.partial(scatter_kernel, planes, which),
+        in_specs=[anywhere] * len(lefts) + [vmem] * (len(rights) + 2) + [anywhere],
+        out_specs=[vmem] + [anywhere] * 4,
+        out_shape=[
+            jax.ShapeDtypeStruct((columns, group), wide),
+            jax.ShapeDtypeStruct((planes, 2, rows, weight.shape[1] // 2), narrow),
+            jax.ShapeDtypeStruct((tokens, hidden), narrow),
+            jax.ShapeDtypeStruct((tokens, hidden), wide),
+            jax.ShapeDtypeStruct((planes, hidden, group), narrow),
+        ],
+        scratch_shapes=[
+            pltpu.VMEM((len(lefts), planes, tokens, group), narrow),
+            pltpu.VMEM((columns, tokens), narrow),
+            pltpu.VMEM((planes, columns, group), narrow),
+            pltpu.VMEM((planes + 1, columns, group), narrow),
+            pltpu.VMEM((2, step, hidden), narrow),
+            pltpu.VMEM((2, step, hidden), wide),
+            pltpu.VMEM((2, hidden, group), narrow),
+            pltpu.SemaphoreType.DMA((len(lefts), planes)),
+            pltpu.SemaphoreType.DMA((2, planes + 1, 3)),
+            pltpu.SemaphoreType.DMA((2, planes + 1, 3)),
+            pltpu.SemaphoreType.DMA((2,)),
+            pltpu.SemaphoreType.DMA((2,)),
+            pltpu.SemaphoreType.DMA((3, 2)),
+        ],
+        compiler_params=pltpu.CompilerParams(
+            collective_id=collective_id, has_side_effects=True, vmem_limit_bytes=62 * MIB
+        ),
+        cost_estimate=pl.CostEstimate(
+            flops=40 * tokens * D * columns, bytes_accessed=2 * tokens * D, transcendentals=0
+        ),
+        name="backward_step",
+    )(*lefts, *rights, fc1, bias, weight)
+    return total, weight_all.reshape(D, weight.shape[1] // 2), active, slope, grad
+
+
+def project_kernel(normed_ref, given_ref, in_ref, out_ref, bias_ref, projected_ref, given_attn_ref):
+    projected_ref[...] = nn(normed_ref[...], in_ref[...]) + bias_ref[...]
+    given_attn_ref[...] = nn(given_ref[...], out_ref[...]).astype(narrow)
+
+
+def project(normed, given, weights, bias):
+    tokens, width = normed.shape[0], weights.shape[1] // 4
+    block = min(256, tokens)
+    row = pl.BlockSpec((block, D), lambda i: (i, 0))
+    return pl.pallas_call(
+        project_kernel,
+        grid=(tokens // block,),
+        in_specs=[
+            row,
+            row,
+            pl.BlockSpec((D, 3 * width), lambda i: (0, 0)),
+            pl.BlockSpec((D, width), lambda i: (0, 3)),
+            pl.BlockSpec((1, 3 * width), lambda i: (0, 0)),
+        ],
+        out_specs=[
+            pl.BlockSpec((block, 3 * width), lambda i: (i, 0)),
+            pl.BlockSpec((block, width), lambda i: (i, 0)),
+        ],
+        out_shape=[
+            jax.ShapeDtypeStruct((tokens, 3 * width), wide),
+            jax.ShapeDtypeStruct((tokens, width), narrow),
+        ],
+        compiler_params=pltpu.CompilerParams(vmem_limit_bytes=48 * MIB),
+        cost_estimate=pl.CostEstimate(
+            flops=8 * tokens * D * width, bytes_accessed=8 * tokens * D, transcendentals=0
+        ),
+        name="project",
+    )(normed, given, weights, weights, bias)
 
 
 def product_kernel(count, *refs):
@@ -408,17 +883,21 @@
         def in_order(kept, came):
             return jnp.where(side == 0, jnp.stack([kept, came]), jnp.stack([came, kept]))
 
-        def scatter_planes(grads):
-            total = lax.psum_scatter(
+        def sum_planes(grads):
+            return lax.psum_scatter(
                 grads.astype(narrow),
                 "fsdp",
                 scatter_dimension=0,
                 tiled=True,
                 axis_index_groups=columns_of_planes,
             )
-            parts = total.reshape(2, rows, grads.shape[1])
-            came = send_x(pick(parts, 1 - side))
-            return in_order(pick(parts, side), came).astype(wide)
+
+        def halves_of(kept, came):
+            return in_order(kept, came).astype(wide)
+
+        def scatter_sides(total):
+            parts = total.astype(narrow).reshape(total.shape[0], 2, rows)
+            return halves_of(pick(parts, side, 1), send_x(pick(parts, 1 - side, 1)))
 
         def scatter_tokens(total):
             parts = total.reshape(2, 2, 2, mine, D)
@@ -447,41 +926,49 @@
                     bit *= 2
             return v
 
-        full_qo = gather_planes(exchange_qo(w_qkv, w_out.T))
-
+        normed, grad_rows, full_qo, fc1_block, fc2_rows, bounds, cosine, sine = gather_tokens(
+            nf // 2,
+            inputs,
+            segments,
+            ln_gain.astype(wide).reshape(1, D),
+            ln_bias.astype(wide).reshape(1, D),
+            cotangent,
+            w_qkv,
+            w_out,
+            w_fc1,
+            w_fc2,
+        )
+        full_fc1 = gather_planes(fc1_block)
         tokens_in = inputs.astype(wide)
-        normed_local, norm_back = jax.vjp(
+        _, norm_back = jax.vjp(
             layer_norm, tokens_in, ln_gain.astype(wide), ln_bias.astype(wide)
         )
-        normed, grad_rows, fc1_block, fc2_block = gather_tokens(
-            normed_local.astype(narrow), cotangent, w_fc1, w_fc2.T
-        )
-        full_fc1, full_fc2 = gather_planes(fc1_block), gather_planes(fc2_block)
-        both_segments = in_order(segments[0], send_x(segments)[0])
-        opening = openings(both_segments)
-        cosine, sine = rotary_tables(opening)
-
-        full_qkv, full_out = full_qo[:, : 3 * half_qkv], full_qo[:, 3 * half_qkv :]
+
         bias_qkv = lax.dynamic_slice_in_dim(b_qkv, side * half_qkv, half_qkv, axis=1)
         bias_fc1 = lax.dynamic_slice_in_dim(b_fc1, side * half_ff, half_ff, axis=0)
 
-        projected = nn(normed, full_qkv) + bias_qkv.astype(wide).reshape(1, 3 * half_qkv)
-        grad_mixed = nn(grad_rows, full_out).astype(narrow)
+        projected, grad_mixed = project(
+            normed, grad_rows, full_qo, bias_qkv.astype(wide).reshape(1, 3 * half_qkv)
+        )
         mixed, grad_q, grad_k, grad_v = attention(
-            opening, cosine, sine, projected, grad_mixed, length
-        )
+            bounds, cosine, sine, projected, grad_mixed, length
+        )
+        sum_qo, full_fc2, active_low, slope, grad_w2 = backward_step(
+            nf // 2,
+            [normed, grad_rows],
+            [grad_q, grad_k, grad_v, mixed],
+            (0, 0, 0, 1),
+            full_fc1,
+            bias_fc1.astype(wide).reshape(1, half_ff),
+            fc2_rows,
+            2,
+        )
+        sum_fc2 = scatter_sides(sum_planes(grad_w2.reshape(-1, grad_w2.shape[2])))
+        grad_hidden = (nn(grad_rows, full_fc2) * slope).astype(narrow)
+        grad_w1 = tn(normed, grad_hidden).astype(narrow)
+        total_fc1 = sum_planes(grad_w1)
+        grad_hidden, mixed, grad_w1 = lax.optimization_barrier((grad_hidden, mixed, grad_w1))
         grad_projected = jnp.concatenate([grad_q, grad_k, grad_v], axis=1)
-        grad_qo = jnp.concatenate(
-            [tn(normed, grad_projected).astype(narrow), tn(grad_rows, mixed).astype(narrow)], axis=1
-        )
-        sum_qo = scatter_planes(grad_qo)
-
-        hidden = nn(normed, full_fc1) + bias_fc1.astype(wide)
-        active, gelu_back = jax.vjp(gelu_tanh, hidden)
-        active_low = active.astype(narrow)
-        sum_fc2 = scatter_planes(tn(grad_rows, active_low))
-        grad_hidden = gelu_back(nn(grad_rows, full_fc2))[0].astype(narrow)
-        sum_fc1 = scatter_planes(tn(normed, grad_hidden))
         grad_normed = scatter_tokens(
             sum_of_products(
                 [(grad_q, full_qo, 0), (grad_k, full_qo, 1), (grad_v, full_qo, 2), (grad_hidden, full_fc1, 0)]
@@ -494,11 +981,11 @@
         grad_tokens, grad_gain, grad_offset = norm_back(grad_normed)
         grad_tokens = grad_tokens + cotangent.astype(wide)
 
-        grad_w_qkv = sum_qo[:, :, : 3 * half_qkv].reshape(2, rows, 3, half_qkv)
-        grad_w_qkv = grad_w_qkv.transpose(2, 1, 0, 3).reshape(3, rows, 2 * half_qkv)
-        grad_w_out = sum_qo[:, :, 3 * half_qkv :].transpose(0, 2, 1).reshape(2 * half_qkv, rows)
-        grad_w_fc1 = sum_fc1.transpose(1, 0, 2).reshape(rows, 2 * half_ff)
-        grad_w_fc2 = sum_fc2.transpose(0, 2, 1).reshape(2 * half_ff, rows)
+        sum_qo = scatter_sides(sum_qo)
+        grad_w_qkv = sum_qo[:, : 3 * half_qkv].reshape(2, 3, half_qkv, rows)
+        grad_w_qkv = grad_w_qkv.transpose(1, 3, 0, 2).reshape(3, rows, 2 * half_qkv)
+        grad_w_out = sum_qo[:, 3 * half_qkv :].reshape(2 * half_qkv, rows)
+        grad_w_fc2 = sum_fc2.reshape(2 * half_ff, rows)
 
         anchor = jnp.zeros((), jnp.int32)
         bias_qkv_full = lax.dynamic_update_slice(
@@ -517,8 +1004,20 @@
                 [bias_qkv_full.reshape(-1), bias_fc1_full, grad_gain, grad_offset, cotangent_sum]
             ).reshape(-1, 128)
         ).reshape(-1)
+        total_fc1, outputs, grad_tokens, small, grad_w_qkv, grad_w_out, grad_w_fc2 = (
+            lax.optimization_barrier(
+                (total_fc1, outputs, grad_tokens, small, grad_w_qkv, grad_w_out, grad_w_fc2)
+            )
+        )
+        parts = total_fc1.reshape(2, rows, total_fc1.shape[1])
+        kept, came = pick(parts, side).astype(wide), send_x(pick(parts, 1 - side)).astype(wide)
+        grad_w_fc1 = jnp.where(
+            side == 0,
+            jnp.concatenate([kept, came], axis=1),
+            jnp.concatenate([came, kept], axis=1),
+        )
         total_qkv = small[: 3 * D].reshape(3, D)
-        total_fc1 = small[3 * D : 3 * D + FF]
+        total_b_fc1 = small[3 * D : 3 * D + FF]
         total_gain, total_offset, total_out = small[3 * D + FF :].reshape(3, D)
         return (
             outputs,
@@ -530,7 +1029,7 @@
             grad_w_out,
             total_out,
             grad_w_fc1,
-            total_fc1,
+            total_b_fc1,
             grad_w_fc2,
             total_out,
         )

time: 581 us -> 567 us (0.976)
  Pallas kernels: 199 us -> 304 us
  matrix products: 96.6 us -> 26.9 us
  waiting for transfers between devices: 140 us -> 94.1 us
    pallas_call x2 -> x3, Pallas kernels: 118 us -> 223 us  [the longest x1 121 us: backward_step(): pl.pallas_call(functools.partial(scatter_kernel, planes, which), in_specs...]
    dot_general x4 -> x1, matrix products: 54.2 us -> 14 us  [nn(): lax.dot_general(a, b, (((1,), (0,)), ((), ())), preferred_element_type=wide)]
    all_gather x3 -> x1, waiting for transfers between devices: 48.9 us -> 15.7 us  [gather_planes(): lax.all_gather(block, 'fsdp', axis=0, tiled=True, axis_index_groups=colum...]
    dot_general x4 -> x1, matrix products: 42.4 us -> 12.9 us  [tn(): lax.dot_general(a, b, (((0,), (0,)), ((), ())), preferred_element_type=wide)]
    ppermute x5, waiting for transfers between devices: 27.6 us -> 16.8 us  [reduce_all(): v = v + lax.ppermute(v, axis, [(i, i ^ bit) for i in range(size)])]
    unnamed x85 -> x88, local copies, waits for them, and re-layouts: 19 us -> 28.2 us
    concatenate x3 -> x0, local copies, waits for them, and re-layouts: 7.49 us -> none  [the longest x1 4.47 us: rotary_tables(): jnp.concatenate([cos_head, cos_head], axis=-1)]
    dynamic_slice x6 -> x8, local copies, waits for them, and re-layouts: 18.6 us -> 22.7 us  [pick(): return lax.dynamic_index_in_dim(v, index, axis, keepdims=False)]
  transfers between devices with their start and end apart: 25 -> 21, of which waited for: 12 -> 11; matrix products, arithmetic and copies ran while one was open for 33% -> 18% of each run, Pallas kernels for 31% -> 17%
where the time goes in v3:
time: 567 us; the launch traced here: 564 us
  Pallas kernels  304 us (54%)
  waiting for transfers between devices  94.1 us (17%)
  local copies, waits for them, and re-layouts  79.3 us (14%)
  other arithmetic  32 us (6%)
  matrix products  26.9 us (5%)
  between operations  14.7 us (3%)
  starting transfers between devices  12.9 us (2%)
    pallas_call x1, Pallas kernels, backward_step(): pl.pallas_call(functools.partial(scatter_kernel, planes, which), in_specs...  121 us
    pallas_call x1, Pallas kernels, gather_tokens(): pl.pallas_call(functools.partial(gather_kernel, planes), in_specs=[vmem]...  87.5 us
    pallas_call x1, Pallas kernels, attention(): pl.pallas_call(functools.partial(attention_kernel, rows), grid=(tokens //...  42.7 us
    pallas_call x2, Pallas kernels, sum_of_products(): pl.pallas_call(functools.partial(product_kernel, len(pairs)), grid=(token...  37.5 us
    ppermute x7, waiting for transfers between devices, send_x(): return lax.ppermute(v, 'fsdp', swap_f)  36.6 us
    unnamed x88, local copies, waits for them, and re-layouts  28.2 us
    ppermute x4, waiting for transfers between devices, send_y(): return lax.ppermute(v, 'tp', swap_chip)  25 us
    dynamic_slice x8, local copies, waits for them, and re-layouts, pick(): return lax.dynamic_index_in_dim(v, index, axis, keepdims=False)  22.7 us
  transfers between devices with their start and end apart: 21, of which 11 were waited for; matrix products, arithmetic and copies ran while one was open for 18% of the time, Pallas kernels for 17%

profile of v3, /device:TPU:0, one launch (start us, length us, event | category | flops | bytes accessed | tf_op | source)
XLA Modules:
  0.0 563.6 jit_solution(7235773987603191513)
XLA Ops:
  16.3 87.5 %gather_tokens.1 = (bf16[2,2,2,256,2048]{4,3,2,1,0:T(8,128)(2,1)S(1)}, bf16[2,2,2,256,2048]{4,3,2,1,0:T(8,128)(2,1)}, bf16[4,2,256,1024]{3,2,1,0:T(8,128)(2,1)S(...) custom-call(bf16[256,2048]{1,0:T(8,128)(2,1)S(1)} %copy-done, ...), custom_call_target="tpu_custom_call" | custom-call | tf_op jit(solution)/shard_map/gather_tokens/pallas_call | solution.py:420
  103.8 3.3 copy-done.17
  107.1 2.0 copy-done.18
  112.0 2.2 copy-done.19
  114.2 14.8 %project.1 = (f32[2048,768]{1,0:T(8,128)}, bf16[2048,256]{1,0:T(8,128)(2,1)S(1)}) custom-call(bf16[2048,2048]{1,0:T(8,128)(2,1)} %bitcast.100, bf16[2048,2048]{1,0:T(8,128)(2,1)} %bitcast.124, bf16[2048,1024]{1,0:T(8,128)(2,1)S(1)} %bitcast.107, bf16[2048,1024]{1,0:T(8,128)(2,1)S(1)} %bitcast.108, f32[1,768]{1,0:T(1,128)S(1)} %bitcast.99), custom_call_target="tpu_custom_call" | custom-call | flops 8589934592 | bytes 33554432 | tf_op jit(solution)/shard_map/project/pallas_call | solution.py:777
  130.0 42.7 %attention.1 = (bf16[2048,256]{1,0:T(8,128)(2,1)S(1)}, bf16[2048,256]{1,0:T(8,128)(2,1)S(1)}, bf16[2048,256]{1,0:T(8,128)(2,1)S(1)}, bf16[2048,256]{1,0:T(8,128)(2,1)S(1)}) custom-call(f32[2,8,128]{2,1,0:T(8,128)S(1)} %get-tuple-element.42.bound_ref, f32[2048,128]{1,0:T(8,128)S(1)} %get-tuple-element.43.cos_ref, f32[2048,128]{1,0:T(8,128)} %copy-done.21, ...), custom_call_target="tpu_custom_call" | custom-call | flops 6442450944 | bytes 16777216 | tf_op jit(solution)/shard_map/attention/pallas_call | solution.py:147
  176.6 15.7 %all-gather.2.cloned.1.call-done.refs_6_.refs_7_ = bf16[2048,1024]{1,0:T(8,128)(2,1)} async-done(((bf16[512,1024]{1,0:T(8,128)(2,1)}), bf16[2048,1024]{1,0:T(8,128)(2,1)}) %all-gather.2.cloned.1.call-update) | async-done | bytes 4194320 | tf_op jit(solution)/shard_map/all_gather | solution.py:852
  192.2 121.2 %backward_step.1 = (f32[1024,512]{1,0:T(8,128)}, bf16[4,2,256,1024]{3,2,1,0:T(8,128)(2,1)}, bf16[2048,1024]{1,0:T(8,128)(2,1)}, f32[2048,1024]{1,0:T(8,128)}, bf16[4,1024,512]{2,1,0:T(8,128)(2,1)}) custom-call(bf16[2048,2048]{1,0:T(8,128)(2,1)} %bitcast.101, bf16[2048,2048]{1,0:T(8,128)(2,1)} %bitcast.125, bf16[2048,256]{1,0:T(8,128)(2,1)} %copy-done.6, ...), custom_call_target="tpu_custom_call" | custom-call | flops 171798691840 | bytes 8388608 | tf_op jit(solution)/shard_map/backward_step/pallas_call | solution.py:731
  313.4 6.4 %copy.44 = bf16[4096,512]{0,1:T(8,128)(2,1)} copy(bf16[4096,512]{1,0:T(8,128)(2,1)} %bitcast.112) | data formatting | bytes 8388608 | tf_op jit(solution)/shard_map/reshape | solution.py:966
  320.1 14.0 %multiply_convert_fusion.refs_3_ = bf16[2048,1024]{1,0:T(8,128)(2,1)S(1)} fusion(f32[2048,1024]{1,0:T(8,128)} %get-tuple-element.55, bf16[2048,2048]{1,0:T(8,128)(2,1)} %bitcast.126, bf16[2048,1024]{1,0:T(8,128)(2,1)} %bitcast.127), kind=kOutput, calls=%fused_computation.3 | convolution fusion | flops 8594128896 | bytes 25165824 | tf_op jit(solution)/shard_map/dot_general | solution.py:52
  334.1 1.9 copy-done.33
  336.0 12.9 %convolution_convert_fusion = bf16[2048,1024]{1,0:T(8,128)(2,1)} fusion(bf16[2048,2048]{1,0:T(8,128)(2,1)} %bitcast.102, bf16[2048,1024]{1,0:T(8,128)(2,1)S(1)} %multiply_convert_fusion.refs_3_), kind=kOutput, calls=%fused_computation.9 | convolution fusion | flops 8592031744 | bytes 16777216 | tf_op jit(solution)/shard_map/dot_general | solution.py:56
  348.9 21.2 %sum_of_products.3 = bf16[2048,2048]{1,0:T(8,128)(2,1)} custom-call(bf16[2048,256]{1,0:T(8,128)(2,1)S(1)} %copy-done.7, bf16[2048,256]{1,0:T(8,128)(2,1)S(1)} %copy-done.9, bf16[2048,256]{1,0:T(8,128)(2,1)S(1)} %copy-done.11, bf16[2048,1024]{1,0:T(8,128)(2,1)} %copy-done.33, bf16[2048,1024]{1,0:T(8,128)(2,1)} %bitcast.103, bf16[2048,1024]{1,0:T(8,128)(2,1)} %bitcast.104, ...), custom_call_target="tpu_custom_call" | custom-call | flops 15032385536 | bytes 14680064 | tf_op jit(solution)/shard_map/sum_of_products/pallas_call | solution.py:819
  370.1 7.1 %constant_dynamic-slice_fusion.5 = (bf16[2,2,1,256,2048]{4,3,2,1,0:T(8,128)(2,1)}, bf16[2,2,1,256,2048]{4,3,2,1,0:T(8,128)(2,1)S(1)}) fusion(bf16[2,2,2,256,2048]{4,3,2,1,0:T(8,128)(2,1)} %bitcast.110, s32[]{:T(128)S(6)} %select_n.165, s32[]{:T(128)S(6)} %select_n.166), kind=kLoop, calls=%fused_computation.69 | loop fusion | bytes 16777224 | tf_op jit(solution)/shard_map/jit(dynamic_index_in_dim)/dynamic_slice | solution.py:881
  377.3 2.7 copy.62
  380.0 1.3 copy-done.25
  381.4 16.3 %sum_of_products.2 = bf16[2048,2048]{1,0:T(8,128)(2,1)} custom-call(bf16[2048,256]{1,0:T(8,128)(2,1)S(1)} %copy-done.23, bf16[2048,1024]{1,0:T(8,128)(2,1)S(1)} %copy-done.25, bf16[2048,1024]{1,0:T(8,128)(2,1)} %bitcast.106, bf16[2048,1024]{1,0:T(8,128)(2,1)} %bitcast.128), custom_call_target="tpu_custom_call" | custom-call | flops 10737418240 | bytes 10485760 | tf_op jit(solution)/shard_map/sum_of_products/pallas_call | solution.py:819
  397.6 6.7 %constant_dynamic-slice_fusion.7 = (bf16[2,2,1,256,2048]{4,3,2,1,0:T(8,128)(2,1)}, bf16[2,2,1,256,2048]{4,3,2,1,0:T(8,128)(2,1)S(1)}) fusion(bf16[2,2,2,256,2048]{4,3,2,1,0:T(8,128)(2,1)} %bitcast.109, s32[]{:T(128)S(6)} %select_n.165, s32[]{:T(128)S(6)} %select_n.166), kind=kLoop, calls=%fused_computation.71 | loop fusion | bytes 16777224 | tf_op jit(solution)/shard_map/jit(dynamic_index_in_dim)/dynamic_slice | solution.py:881
  404.3 2.3 copy.63
  406.6 1.7 convert_reduce_fusion.1
  408.7 3.0 convert_reduce_fusion
  412.2 4.7 convert_add_fusion
  416.9 3.3 fusion.27
  420.1 4.3 fusion.14
  426.7 4.0 convert_add_fusion.1
  430.7 3.2 fusion.28
  433.9 2.1 copy-done.31
  438.8 1.8 fusion.11
  440.6 2.1 collective-permute-start.1
  442.7 8.1 %collective-permute-done.8 = bf16[2,256,1024]{2,1,0:T(8,128)(2,1)} collective-permute-done((bf16[2,256,1024]{2,1,0:T(8,128)(2,1)}, bf16[2,256,1024]{2,1,0:T(8,128)(2,1)}, u32[]{:S(2)}, u32[]{:S(2)}) %collective-permute-start.8) | collective-permute-done | bytes 1048608 | tf_op jit(solution)/shard_map/ppermute | solution.py:845
  450.8 2.2 bitcast_add_fusion
  453.2 1.8 bitcast_add_fusion.1
  456.2 17.0 %collective-permute-done.3 = bf16[2,256,1024]{2,1,0:T(8,128)(2,1)} collective-permute-done((bf16[2,256,1024]{2,1,0:T(8,128)(2,1)}, bf16[2,256,1024]{2,1,0:T(8,128)(2,1)}, u32[]{:S(2)}, u32[]{:S(2)}) %collective-permute-start.3) | collective-permute-done | bytes 1048608 | tf_op jit(solution)/shard_map/ppermute | solution.py:845
  473.2 1.7 bitcast_add_fusion.2
  476.8 9.8 %collective-permute-done.9 = bf16[256,1024]{1,0:T(8,128)(2,1)S(1)} collective-permute-done((bf16[256,1024]{1,0:T(8,128)(2,1)S(1)}, bf16[256,1024]{1,0:T(8,128)(2,1)S(1)}, u32[]{:S(2)}, u32[]{:S(2)}) %collective-permute-start.9) | collective-permute-done | bytes 524320 | tf_op jit(solution)/shard_map/ppermute | solution.py:842
  488.6 8.5 %collective-permute-done.4 = bf16[256,1024]{1,0:T(8,128)(2,1)S(1)} collective-permute-done((bf16[256,1024]{1,0:T(8,128)(2,1)S(1)}, bf16[256,1024]{1,0:T(8,128)(2,1)S(1)}, u32[]{:S(2)}, u32[]{:S(2)}) %collective-permute-start.4) | collective-permute-done | bytes 524320 | tf_op jit(solution)/shard_map/ppermute | solution.py:842
  497.5 2.7 convert_reduce_fusion.3
  500.2 2.2 constant_dynamic-slice_fusion.3
  503.7 3.8 collective-permute-done.11
  507.5 1.8 collective-permute-start.12
  509.4 9.2 %collective-permute-done.12 = f32[160,128]{1,0:T(8,128)S(1)} collective-permute-done((f32[160,128]{1,0:T(8,128)S(1)}, f32[160,128]{1,0:T(8,128)S(1)}, u32[]{:S(2)}, u32[]{:S(2)}) %collective-permute-start.12) | collective-permute-done | bytes 81952 | tf_op jit(solution)/shard_map/ppermute | solution.py:925
  521.7 2.4 reshape.268
  526.9 3.7 collective-permute-done.14
  530.9 8.5 %collective-permute-done.16 = bf16[1024,256]{1,0:T(8,128)(2,1)S(1)} collective-permute-done((bf16[1024,256]{1,0:T(8,128)(2,1)S(1)}, bf16[1024,256]{1,0:T(8,128)(2,1)S(1)}, u32[]{:S(2)}, u32[]{:S(2)}) %collective-permute-start.16) | collective-permute-done | bytes 524320 | tf_op jit(solution)/shard_map/ppermute | solution.py:842
  539.5 1.5 bitcast_convert_fusion
  541.1 1.3 bitcast_convert_fusion.1
  544.9 9.6 %collective-permute-done.17 = bf16[256,1024]{1,0:T(8,128)(2,1)S(1)} collective-permute-done((bf16[256,1024]{1,0:T(8,128)(2,1)S(1)}, bf16[256,1024]{1,0:T(8,128)(2,1)S(1)}, u32[]{:S(2)}, u32[]{:S(2)}) %collective-permute-start.17) | collective-permute-done | bytes 524320 | tf_op jit(solution)/shard_map/ppermute | solution.py:842
  554.7 1.6 maximum_select_fusion
  (167 shorter events, 39.0 us)
Async XLA Ops:
  7.2 185.1 %all-gather.2.cloned.1.call-start = ((), (), s32[]{:S(2)}) async-start(), calls=%async_computation.2 | async-start | bytes 5242880 | tf_op jit(solution)/shard_map/all_gather | solution.py:852
  7.9 95.9 %copy-start.14 = (f32[2048]{0:T(1024)}, f32[2048]{0:T(1024)S(1)}, u32[]{:S(2)}) copy-start(f32[2048]{0:T(1024)S(1)} %convert_element_type.157) | copy-start | bytes 24580
  8.6 1.2 copy-start
  16.3 95.0 %copy-start.38 = (bf16[3,512]{1,0:T(4,128)(2,1)S(1)}, bf16[3,512]{1,0:T(4,128)(2,1)}, u32[]{:S(2)}) copy-start(bf16[3,512]{1,0:T(4,128)(2,1)} %param.18) | copy-start | bytes 9220
  16.3 95.0 %copy-start.39 = (bf16[2048]{0:T(1024)(128)(2,1)S(1)}, bf16[2048]{0:T(1024)(128)(2,1)}, u32[]{:S(2)}) copy-start(bf16[2048]{0:T(1024)(128)(2,1)} %param.22) | copy-start | bytes 12292
  103.8 3.3 copy-start.17
  107.1 2.0 copy-start.18
  111.0 413.8 %reduce-scatter.5.cloned.1.call-start = ((), (), s32[]{:S(2)}) async-start(), calls=%async_computation.4 | async-start | bytes 5242880 | tf_op jit(solution)/shard_map/reduce_scatter | solution.py:887
  112.0 2.2 copy-start.19
  319.8 221.2 %reduce-scatter.3.cloned.1.call-start = ((), (), s32[]{:S(2)}) async-start(), calls=%async_computation.3 | async-start | bytes 5242880 | tf_op jit(solution)/shard_map/reduce_scatter | solution.py:887
  334.1 1.9 copy-start.33
  336.0 12.9 %copy-start.7 = (bf16[2048,256]{1,0:T(8,128)(2,1)S(1)}, bf16[2048,256]{1,0:T(8,128)(2,1)}, u32[]{:S(2)}) copy-start(bf16[2048,256]{1,0:T(8,128)(2,1)} %copy-done.6) | copy-start | bytes 3145732
  336.0 12.9 %copy-start.9 = (bf16[2048,256]{1,0:T(8,128)(2,1)S(1)}, bf16[2048,256]{1,0:T(8,128)(2,1)}, u32[]{:S(2)}) copy-start(bf16[2048,256]{1,0:T(8,128)(2,1)} %copy-done.8) | copy-start | bytes 3145732
  336.0 12.9 %copy-start.11 = (bf16[2048,256]{1,0:T(8,128)(2,1)S(1)}, bf16[2048,256]{1,0:T(8,128)(2,1)}, u32[]{:S(2)}) copy-start(bf16[2048,256]{1,0:T(8,128)(2,1)} %copy-done.10) | copy-start | bytes 3145732
  377.3 2.7 copy-start.23
  377.3 4.1 copy-start.25
  380.0 32.1 %collective-permute-start.5 = (bf16[2,2,256,2048]{3,2,0,1:T(8,128)(2,1)}, bf16[2,2,256,2048]{3,2,0,1:T(8,128)(2,1)}, u32[]{:S(2)}, u32[]{:S(2)}) collective-permute-start(bf16[2,2,256,2048]{3,2,0,1:T(8,128)(2,1)} %bitcast.93), channel_id=1, source_target_pairs={{0,1},{1,0},{2,3},{3,2},{4,5},{5,4},{6,7},{7,6},{8,9},{9,8},{10,11... | collective-permute-start | bytes 12582920 | tf_op jit(solution)/shard_map/ppermute | solution.py:848
  404.3 2.3 copy-start.36
  404.3 2.3 copy-start.37
  406.6 1.9 copy-start.1
  406.6 20.0 %collective-permute-start = (bf16[2,2,256,2048]{3,2,0,1:T(8,128)(2,1)}, bf16[2,2,256,2048]{3,2,0,1:T(8,128)(2,1)}, u32[]{:S(2)}, u32[]{:S(2)}) collective-permute-start(bf16[2,2,256,2048]{3,2,0,1:T(8,128)(2,1)} %bitcast.94), channel_id=1, source_target_pairs={{0,1},{1,0},{2,3},{3,2},{4,5},{5,4},{6,7},{7,6},{8,9},{9,8},{10,11... | collective-permute-start | bytes 12582920 | tf_op jit(solution)/shard_map/ppermute | solution.py:848
  408.7 3.5 copy-start.27
  420.1 6.5 %copy-start.29 = (f32[2,2,256,1024]{3,2,0,1:T(8,128)}, f32[2,2,256,1024]{3,2,0,1:T(8,128)S(1)}, u32[]{:S(2)}) copy-start(f32[2,2,256,1024]{3,2,0,1:T(8,128)S(1)} %get-tuple-element.73) | copy-start | bytes 12582916
  420.1 6.5 %copy-start.26 = (bf16[2,2,1,256,2048]{4,3,2,1,0:T(8,128)(2,1)S(1)}, bf16[2,2,1,256,2048]{4,3,2,1,0:T(8,128)(2,1)}, u32[]{:S(2)}) copy-start(bf16[2,2,1,256,2048]{4,3,2,1,0:T(8,128)(2,1)} %get-tuple-element.79) | copy-start | bytes 12582916
  424.4 26.3 %collective-permute-start.8 = (bf16[2,256,1024]{2,1,0:T(8,128)(2,1)}, bf16[2,256,1024]{2,1,0:T(8,128)(2,1)}, u32[]{:S(2)}, u32[]{:S(2)}) collective-permute-start(bf16[2,256,1024]{2,1,0:T(8,128)(2,1)} %fusion.14), channel_id=1, source_target_pairs={{0,2},{1,3},{2,0},{3,1},{4,6},{5,7},{6,4},{7,5},{8,10},{9,11},{10,... | collective-permute-start | bytes 3145736 | tf_op jit(solution)/shard_map/ppermute | solution.py:845
  426.6 26.5 %collective-permute-start.6 = (bf16[2,256,1024]{2,1,0:T(8,128)(2,1)}, bf16[2,256,1024]{2,1,0:T(8,128)(2,1)}, u32[]{:S(2)}, u32[]{:S(2)}) collective-permute-start(bf16[2,256,1024]{2,1,0:T(8,128)(2,1)} %fusion.13), channel_id=1, source_target_pairs={{0,4},{4,0},{8,12},{12,8},{16,20},{20,16},{24,28},{28,24},{1,5},{5... | collective-permute-start | bytes 3145736 | tf_op jit(solution)/shard_map/ppermute | solution.py:842
  433.9 2.1 copy-start.31
  433.9 4.2 copy-start.34
  437.2 36.0 %collective-permute-start.3 = (bf16[2,256,1024]{2,1,0:T(8,128)(2,1)}, bf16[2,256,1024]{2,1,0:T(8,128)(2,1)}, u32[]{:S(2)}, u32[]{:S(2)}) collective-permute-start(bf16[2,256,1024]{2,1,0:T(8,128)(2,1)} %fusion.12), channel_id=1, source_target_pairs={{0,2},{1,3},{2,0},{3,1},{4,6},{5,7},{6,4},{7,5},{8,10},{9,11},{10,... | collective-permute-start | bytes 3145736 | tf_op jit(solution)/shard_map/ppermute | solution.py:845
  440.6 12.6 %copy-start.30 = (f32[2,2,256,1024]{3,2,0,1:T(8,128)S(1)}, f32[2,2,256,1024]{3,2,0,1:T(8,128)}, u32[]{:S(2)}) copy-start(f32[2,2,256,1024]{3,2,0,1:T(8,128)} %copy-done.29) | copy-start | bytes 12582916
  440.6 34.8 %collective-permute-start.1 = (bf16[2,256,1024]{2,1,0:T(8,128)(2,1)S(1)}, bf16[2,256,1024]{2,1,0:T(8,128)(2,1)S(1)}, u32[]{:S(2)}, u32[]{:S(2)}) collective-permute-start(bf16[2,256,1024]{2,1,0:T(8,128)(2,1)S(1)} %fusion.11), channel_id=1, source_target_pairs={{0,4},{4,0},{8,12},{12,8},{16,20},{20,16},{24,28},{28,24},{1,5},{5... | collective-permute-start | bytes 3145736 | tf_op jit(solution)/shard_map/ppermute | solution.py:842
  453.1 20.2 %copy-start.32 = (f32[2,2,256,1024]{3,2,0,1:T(8,128)S(1)}, f32[2,2,256,1024]{3,2,0,1:T(8,128)}, u32[]{:S(2)}) copy-start(f32[2,2,256,1024]{3,2,0,1:T(8,128)} %copy-done.31) | copy-start | bytes 12582916
  453.1 33.5 %collective-permute-start.9 = (bf16[256,1024]{1,0:T(8,128)(2,1)S(1)}, bf16[256,1024]{1,0:T(8,128)(2,1)S(1)}, u32[]{:S(2)}, u32[]{:S(2)}) collective-permute-start(bf16[256,1024]{1,0:T(8,128)(2,1)S(1)} %fusion.20), channel_id=1, source_target_pairs={{0,4},{4,0},{8,12},{12,8},{16,20},{20,16},{24,28},{28,24},{1,5},{5... | collective-permute-start | bytes 1572872 | tf_op jit(solution)/shard_map/ppermute | solution.py:842
  455.1 20.2 %copy-start.28 = (f32[2,2,256,1024]{3,2,0,1:T(8,128)S(1)}, f32[2,2,256,1024]{3,2,0,1:T(8,128)}, u32[]{:S(2)}) copy-start(f32[2,2,256,1024]{3,2,0,1:T(8,128)} %get-tuple-element.77) | copy-start | bytes 12582916
  455.1 31.6 %collective-permute-start.7 = (bf16[256,1024]{1,0:T(8,128)(2,1)S(1)}, bf16[256,1024]{1,0:T(8,128)(2,1)S(1)}, u32[]{:S(2)}, u32[]{:S(2)}) collective-permute-start(bf16[256,1024]{1,0:T(8,128)(2,1)S(1)} %fusion.19), channel_id=1, source_target_pairs={{0,2},{1,3},{2,0},{3,1},{4,6},{5,7},{6,4},{7,5},{8,10},{9,11},{10,... | collective-permute-start | bytes 1572872 | tf_op jit(solution)/shard_map/ppermute | solution.py:845
  475.0 22.1 %collective-permute-start.4 = (bf16[256,1024]{1,0:T(8,128)(2,1)S(1)}, bf16[256,1024]{1,0:T(8,128)(2,1)S(1)}, u32[]{:S(2)}, u32[]{:S(2)}) collective-permute-start(bf16[256,1024]{1,0:T(8,128)(2,1)S(1)} %fusion.18), channel_id=1, source_target_pairs={{0,4},{4,0},{8,12},{12,8},{16,20},{20,16},{24,28},{28,24},{1,5},{5... | collective-permute-start | bytes 1572872 | tf_op jit(solution)/shard_map/ppermute | solution.py:842
  475.7 11.1 %copy-start.15 = (f32[2048]{0:T(1024)S(1)}, f32[2048]{0:T(1024)}, u32[]{:S(2)}) copy-start(f32[2048]{0:T(1024)} %copy-done.14) | copy-start | bytes 24580
  475.7 21.5 %collective-permute-start.2 = (bf16[256,1024]{1,0:T(8,128)(2,1)S(1)}, bf16[256,1024]{1,0:T(8,128)(2,1)S(1)}, u32[]{:S(2)}, u32[]{:S(2)}) collective-permute-start(bf16[256,1024]{1,0:T(8,128)(2,1)S(1)} %fusion.17), channel_id=1, source_target_pairs={{0,2},{1,3},{2,0},{3,1},{4,6},{5,7},{6,4},{7,5},{8,10},{9,11},{10,... | collective-permute-start | bytes 1572872 | tf_op jit(solution)/shard_map/ppermute | solution.py:845
  488.6 8.8 %copy-start.3 = (bf16[256,2048]{1,0:T(8,128)(2,1)S(1)}, bf16[256,2048]{1,0:T(8,128)(2,1)}, u32[]{:S(2)}) copy-start(bf16[256,2048]{1,0:T(8,128)(2,1)} %given_ref.1) | copy-start | bytes 3145732
  500.2 2.6 collective-permute-start.10
  502.5 17.3 %collective-permute-start.15 = (bf16[1024,256]{1,0:T(8,128)(2,1)S(1)}, bf16[1024,256]{1,0:T(8,128)(2,1)S(1)}, u32[]{:S(2)}, u32[]{:S(2)}) collective-permute-start(bf16[1024,256]{1,0:T(8,128)(2,1)S(1)} %bitcast.117), channel_id=1, source_target_pairs={{0,4},{4,0},{8,12},{12,8},{16,20},{20,16},{24,28},{28,24},{1,5},{5... | collective-permute-start | bytes 1572872 | tf_op jit(solution)/shard_map/ppermute | solution.py:842
  502.8 4.7 collective-permute-start.11
  507.5 11.1 %collective-permute-start.12 = (f32[160,128]{1,0:T(8,128)S(1)}, f32[160,128]{1,0:T(8,128)S(1)}, u32[]{:S(2)}, u32[]{:S(2)}) collective-permute-start(f32[160,128]{1,0:T(8,128)S(1)} %fusion.34), channel_id=1, source_target_pairs={{0,4},{4,0},{8,12},{12,8},{16,20},{20,16},{24,28},{28,24},{1,5},{5... | collective-permute-start | bytes 245768 | tf_op jit(solution)/shard_map/ppermute | solution.py:925
  518.6 5.5 collective-permute-start.13
  524.2 6.5 %collective-permute-start.14 = (f32[160,128]{1,0:T(8,128)S(1)}, f32[160,128]{1,0:T(8,128)S(1)}, u32[]{:S(2)}, u32[]{:S(2)}) collective-permute-start(f32[160,128]{1,0:T(8,128)S(1)} %add.221), channel_id=1, source_target_pairs={{0,16},{4,20},{8,24},{12,28},{16,0},{20,4},{24,8},{28,12},{1,17},{... | collective-permute-start | bytes 245768 | tf_op jit(solution)/shard_map/ppermute | solution.py:925
  526.3 13.1 %collective-permute-start.16 = (bf16[1024,256]{1,0:T(8,128)(2,1)S(1)}, bf16[1024,256]{1,0:T(8,128)(2,1)S(1)}, u32[]{:S(2)}, u32[]{:S(2)}) collective-permute-start(bf16[1024,256]{1,0:T(8,128)(2,1)S(1)} %bitcast.120), channel_id=1, source_target_pairs={{0,4},{4,0},{8,12},{12,8},{16,20},{20,16},{24,28},{28,24},{1,5},{5... | collective-permute-start | bytes 1572872 | tf_op jit(solution)/shard_map/ppermute | solution.py:842
  542.4 12.1 %collective-permute-start.17 = (bf16[256,1024]{1,0:T(8,128)(2,1)S(1)}, bf16[256,1024]{1,0:T(8,128)(2,1)S(1)}, u32[]{:S(2)}, u32[]{:S(2)}) collective-permute-start(bf16[256,1024]{1,0:T(8,128)(2,1)S(1)} %get-tuple-element.82), channel_id=1, source_target_pairs={{0,4},{4,0},{8,12},{12,8},{16,20},{20,16},{24,28},{28,24},{1,5},{5... | collective-permute-start | bytes 1572872 | tf_op jit(solution)/shard_map/ppermute | solution.py:842
  544.9 11.3 %copy-start.35 = (f32[2048]{0:T(1024)}, f32[2048]{0:T(1024)S(1)}, u32[]{:S(2)}) copy-start(f32[2048]{0:T(1024)S(1)} %get-tuple-element.120) | copy-start | bytes 24580
  (13 other events, 13.2 us)
Sparse Core Ops, SparseCore 0:
  111.2 81.0 all-gather.1
  320.0 75.2 reduce-scatter.4
  408.9 75.0 reduce-scatter.2

commit v4 on v3

--- a/solution.py
+++ b/solution.py
@@ -12,7 +12,7 @@
 HEAD_DIM = 64
 ROT = 32
 FF = 8192
-MIB = 1 << 20
+VMEM = 62 << 20
 
 wide = jnp.float32
 narrow = jnp.bfloat16
@@ -36,12 +36,12 @@
 
 
 def lane_constants():
-    place = jnp.arange(2 * HEAD_DIM, dtype=jnp.int32) % HEAD_DIM
+    place = lax.broadcasted_iota(jnp.int32, (1, 2 * HEAD_DIM), 1) % HEAD_DIM
     turned = (place % (ROT // 2)).astype(wide) * 2.0
     frequency = jnp.exp(turned * (-math.log(10000.0) / ROT))
     sign = jnp.where(place < ROT // 2, -1.0, 1.0)
     inside = place < ROT
-    return jnp.stack([jnp.where(inside, frequency, 0.0), jnp.where(inside, sign, 0.0)])
+    return jnp.where(inside, frequency, 0.0), jnp.where(inside, sign, 0.0)
 
 
 def nt(a, b):
@@ -156,7 +156,7 @@
             pltpu.VMEM((length, lanes), wide),
             pltpu.VMEM((length, lanes), wide),
         ],
-        compiler_params=pltpu.CompilerParams(vmem_limit_bytes=48 * MIB),
+        compiler_params=pltpu.CompilerParams(vmem_limit_bytes=VMEM),
         cost_estimate=pl.CostEstimate(
             flops=tokens * length * width * 12, bytes_accessed=tokens * width * 32, transcendentals=0
         ),
@@ -286,15 +286,16 @@
     bias_ref,
     w_out_ref,
     w_fc2_ref,
-    lane_ref,
     given_ref,
     qkv_ref,
     fc1_ref,
     normed_all,
     given_all,
     qo_all,
+    head_all,
     fc1_block,
-    fc2_ref,
+    fc2_kept_ref,
+    fc2_going_ref,
     bound_ref,
     cos_ref,
     sin_ref,
@@ -304,6 +305,8 @@
     recv_sems,
     plane_send_sems,
     plane_recv_sems,
+    head_send_sems,
+    head_recv_sems,
 ):
     side, chip, core, over_x, over_y, over_core = neighbours()
     plane, above, below, has_above, has_below = chain(planes)
@@ -328,70 +331,95 @@
         qo_came.append(copies.remote(source.at[:, half(1 - side, width)], target, over_x))
     bounds = copies.remote(bound_ref.at[side], bound_ref.at[side], over_x)
     mine = [whole.at[side, chip, core] for whole in (normed_all, given_all)]
+    y_slot = [whole.at[side, 1 - chip, core] for whole in (normed_all, given_all)]
+    x_slot = [whole.at[1 - side, chip, core] for whole in (normed_all, given_all)]
     y_given = copies.remote(given_ref, mine[1], over_y)
     for copy in qo_kept:
         copy.wait()
     qo.send(1, 0)
 
     tokens = input_ref[...].astype(wide)
-    normed_ref[...] = layer_norm(tokens, gain_ref[...], bias_ref[...]).astype(narrow)
-    x_normed = copies.remote(normed_ref, mine[0], over_x)
-    y_normed = copies.remote(normed_ref, mine[0], over_y)
+    normed_ref[...] = layer_norm(
+        tokens, gain_ref[...].astype(wide), bias_ref[...].astype(wide)
+    ).astype(narrow)
     kept = [copies.local(normed_ref, mine[0]), copies.local(given_ref, mine[1])]
     last = [
         copies.remote(normed_ref, mine[0], over_core),
         copies.remote(given_ref, mine[1], over_core),
     ]
+    ff_width, head_width = fc1_ref.shape[1] // 2, head_all.shape[3]
+    head = PlaneGather(planes, head_all, head_send_sems, head_recv_sems)
+
+    def fc1_head(which):
+        return fc1_ref.at[:, pl.ds(pl.multiple_of(which * ff_width, 128), head_width)]
+
+    def fc1_tail(which):
+        start = pl.multiple_of(which * ff_width + head_width, 128)
+        return fc1_ref.at[:, pl.ds(start, ff_width - head_width)]
+
+    head_kept = copies.local(fc1_head(side), head_all.at[plane, side])
+    kept.append(copies.local(fc1_tail(side), fc1_block.at[side]))
     for copy in qo_came:
         copy.wait_recv()
     qo.send(1, 1)
-    x_given = copies.remote(given_ref, mine[1], over_x)
-    ff_width = fc1_ref.shape[1] // 2
-    kept.append(copies.local(fc1_ref.at[:, half(side, ff_width)], fc1_block.at[side]))
-
+    x_normed = copies.remote(normed_ref, mine[0], over_x)
+    y_normed = copies.remote(normed_ref, mine[0], over_y)
+    head_came = copies.remote(fc1_head(1 - side), head_all.at[plane, side], over_x)
+
+    def forward(gather, step, piece):
+        gather.receive(step - 1, piece)
+        gather.send(step, piece)
+
+    if planes > 2:
+        forward(qo, 2, 0)
     bounds.wait_recv()
     step = min(256, length)
+    frequency, sign = lane_constants()
 
     def tables(i, carry):
         here = pl.ds(pl.multiple_of(i * step, 8), step)
         sequence, first = i // (length // step), (i % (length // step)) * step
         place = (first + lax.broadcasted_iota(jnp.int32, (step, 1), 0)).astype(wide)
         bound = bound_ref[sequence, 0:1, 0:1]
-        angles = (place - jnp.where(place >= bound, bound, 0.0)) * lane_ref[0:1]
+        angles = (place - jnp.where(place >= bound, bound, 0.0)) * frequency
         cos_ref[here] = jnp.cos(angles)
-        sin_ref[here] = jnp.sin(angles) * lane_ref[1:2]
+        sin_ref[here] = jnp.sin(angles) * sign
         return carry
 
     lax.fori_loop(0, 2 * length // step, tables, 0)
-
-    def forward(step):
-        for piece in range(2):
-            qo.receive(step - 1, piece)
-            qo.send(step, piece)
-
     if planes > 2:
-        forward(2)
-    fc2_ref[...] = w_fc2_ref[...].T
-    y_slot = [whole.at[side, 1 - chip, core] for whole in (normed_all, given_all)]
-    x_slot = [whole.at[1 - side, chip, core] for whole in (normed_all, given_all)]
+        forward(qo, 2, 1)
+    ff_rows = w_fc2_ref.shape[0] // 2
+    for target, which in ((fc2_kept_ref, side), (fc2_going_ref, 1 - side)):
+        target[...] = w_fc2_ref[pl.ds(pl.multiple_of(which * ff_rows, 128), ff_rows)].T
+    if planes > 3:
+        forward(qo, 3, 0)
     x_normed.wait_recv()
+    x_given = copies.remote(given_ref, mine[1], over_x)
     corner = [[copies.remote(x_slot[0], x_slot[0], over_y)]]
     last.append(copies.remote(x_slot[0], x_slot[0], over_core))
+    if planes > 3:
+        forward(qo, 3, 1)
+    for k in range(4, planes):
+        for piece in range(2):
+            forward(qo, k, piece)
+    head_kept.wait()
+    head.send(1, 0)
+    head_came.wait_recv()
+    head.send(1, 1)
     y_given.wait_recv()
-    part = y_slot[1].at[pl.ds(0, cut)]
-    corner.append([copies.remote(part, part, over_x)])
-    last.append(
-        copies.remote(fc1_ref.at[:, half(1 - side, ff_width)], fc1_block.at[side], over_x)
-    )
     last.append(copies.remote(y_slot[1], y_slot[1], over_core))
-    for k in range(3, planes):
-        forward(k)
     y_normed.wait_recv()
     last.append(copies.remote(y_slot[0], y_slot[0], over_core))
     x_given.wait_recv()
-    part = x_slot[1].at[pl.ds(cut, rows - cut)]
-    corner[1].append(copies.remote(part, part, over_y))
+    part = y_slot[1].at[pl.ds(0, cut)]
+    other_part = x_slot[1].at[pl.ds(cut, rows - cut)]
+    corner.append([copies.remote(part, part, over_x), copies.remote(other_part, other_part, over_y)])
+    last.append(copies.remote(fc1_tail(1 - side), fc1_block.at[side], over_x))
     last.append(copies.remote(x_slot[1], x_slot[1], over_core))
+    for k in range(2, planes):
+        for piece in range(2):
+            forward(head, k, piece)
     for whole, parts in zip((normed_all, given_all), corner):
         for copy in parts:
             copy.wait_recv()
@@ -399,11 +427,13 @@
         last.append(copies.remote(slot, slot, over_core))
     for piece in range(2):
         qo.receive(planes - 1, piece)
+        head.receive(planes - 1, piece)
     for copy in kept:
         copy.wait()
     for copy in copies.started:
         copy.wait_send()
     qo.drain()
+    head.drain()
     for copy in last:
         copy.wait_recv()
 
@@ -413,20 +443,24 @@
     tokens, length = 8 * mine, segments.shape[1]
     columns = 2 * w_out.shape[0]
     whole = jax.ShapeDtypeStruct((2, 2, 2, mine, D), narrow)
-    block = jax.ShapeDtypeStruct((2, rows, fc1.shape[1] // 2), narrow)
+    head = max(128, fc1.shape[1] // 8)
+    block = jax.ShapeDtypeStruct((2, rows, fc1.shape[1] // 2 - head), narrow)
     table = jax.ShapeDtypeStruct((2 * length, lanes), wide)
     weights = jax.ShapeDtypeStruct((planes, 2, rows, columns), narrow)
     anywhere, vmem = pl.BlockSpec(memory_space=pl.ANY), pl.BlockSpec(memory_space=pltpu.VMEM)
-    normed_all, given_all, qo_all, fc1_block, fc2_rows, bounds, cosine, sine = pl.pallas_call(
+    ff_half = jax.ShapeDtypeStruct((rows, w_fc2.shape[0] // 2), narrow)
+    outs = pl.pallas_call(
         functools.partial(gather_kernel, planes),
-        in_specs=[vmem] * 7 + [anywhere] * 3,
-        out_specs=[anywhere] * 4 + [vmem] * 4,
+        in_specs=[vmem] * 6 + [anywhere] * 3,
+        out_specs=[anywhere] * 5 + [vmem] * 5,
         out_shape=[
             whole,
             whole,
             weights,
+            jax.ShapeDtypeStruct((planes, 2, rows, head), narrow),
             block,
-            jax.ShapeDtypeStruct((rows, w_fc2.shape[0]), narrow),
+            ff_half,
+            ff_half,
             jax.ShapeDtypeStruct((2, 8, 128), wide),
             table,
             table,
@@ -438,22 +472,21 @@
             pltpu.SemaphoreType.DMA((32,)),
             pltpu.SemaphoreType.DMA((2, planes, 2)),
             pltpu.SemaphoreType.DMA((2, planes, 2)),
+            pltpu.SemaphoreType.DMA((2, planes, 2)),
+            pltpu.SemaphoreType.DMA((2, planes, 2)),
         ],
         compiler_params=pltpu.CompilerParams(
-            collective_id=1, has_side_effects=True, vmem_limit_bytes=32 * MIB
+            collective_id=1, has_side_effects=True, vmem_limit_bytes=VMEM
         ),
         name="gather_tokens",
-    )(inputs, segments, gain, bias, w_out, w_fc2, lane_constants(), given, w_qkv, fc1)
+    )(inputs, segments, gain, bias, w_out, w_fc2, given, w_qkv, fc1)
+    normed_all, given_all, qo_all, head_all = outs[:4]
     return (
         normed_all.reshape(tokens, D),
         given_all.reshape(tokens, D),
         qo_all.reshape(D, columns),
-        fc1_block,
-        fc2_rows,
-        bounds,
-        cosine,
-        sine,
-    )
+        head_all.reshape(D, head),
+    ) + tuple(outs[4:])
 
 
 def scatter_kernel(planes, which, *refs):
@@ -461,15 +494,18 @@
     n_left, n_right = len(lefts), len(which)
     left_refs, right_refs = refs[:n_left], refs[n_left : n_left + n_right]
     (
-        fc1_ref,
+        fc1_head_ref,
+        fc1_tail_ref,
         bias_ref,
-        weight_ref,
+        kept_ref,
+        came_ref,
         out_ref,
         weight_all,
         active_all,
         slope_all,
         grad_all,
         left_vmem,
+        own,
         turned,
         going,
         came,
@@ -479,16 +515,13 @@
         load_sems,
         send_sems,
         recv_sems,
-        x_send_sems,
-        x_recv_sems,
         store_sems,
     ) = refs[n_left + n_right :]
-    side, _, _, over_x, _, _ = neighbours()
+    side = lax.axis_index("fsdp") % 2
     plane, above, below, has_above, has_below = chain(planes)
     devices, has_after, has_before = (above, below), (has_above, has_below), (has_below, has_above)
-    group, width = out_ref.shape[1], right_refs[0].shape[1]
-    tokens = right_refs[0].shape[0]
-    own = out_ref
+    group, width = own.shape[1], right_refs[0].shape[1]
+    rows, tokens = group // 2, right_refs[0].shape[0]
 
     def load(j):
         return [
@@ -506,13 +539,11 @@
     for k in range(planes):
         for copy in load(order(k)):
             copy.start()
-    greet((over_x, True), (above, has_above), (below, has_below))
-    copies = Copies(x_send_sems, x_recv_sems)
-    columns = weight_ref.shape[1] // 2
-    kept = copies.local(weight_ref.at[:, half(side, columns)], weight_all.at[plane, side])
-    other = copies.remote(
-        weight_ref.at[:, half(1 - side, columns)], weight_all.at[plane, side], over_x
-    )
+    greet((above, has_above), (below, has_below))
+    own_weight = [
+        pltpu.make_async_copy(ref, weight_all.at[plane, at], store_sems.at[3, piece])
+        for piece, (ref, at) in enumerate(((kept_ref, side), (came_ref, 1 - side)))
+    ]
 
     def depth(way):
         return plane if way == 0 else planes - 1 - plane
@@ -521,91 +552,89 @@
         return block if way == 0 else planes - 1 - block
 
     def is_weight(at, number):
-        return (number <= at) | (number == at + 2)
+        return number <= at + 1
 
     def weight_block(at, number):
-        return jnp.where(number <= at, at - number + 1, 0)
+        return at - number + 1
 
     def sum_block(at, number):
-        return jnp.where(number == at + 1, planes - 1, planes + 1 + at - number)
-
-    def weight_copies(way, number, at, pieces=(0, 1)):
+        return planes + 1 + at - number
+
+    def weight_copy(way, number, at, piece):
         j = named(way, weight_block(at, number))
-        return [
-            pltpu.make_async_remote_copy(
-                src_ref=weight_all.at[j, piece_side],
-                dst_ref=weight_all.at[j, piece_side],
-                send_sem=send_sems.at[way, number, piece],
-                recv_sem=recv_sems.at[way, number, piece],
-                device_id=devices[way],
-                device_id_type=MESH,
-            )
-            for piece, piece_side in enumerate((side, 1 - side))
-            if piece in pieces
-        ]
-
-    def landing(way, j, receiver):
-        return j if way == 0 else jnp.where(j == receiver, planes, j)
-
-    def sum_copy(way, number, at, receiver, arriving):
-        j = named(way, sum_block(at, number))
-        spot = landing(way, j, receiver)
-        return j, spot, pltpu.make_async_remote_copy(
-            src_ref=came.at[spot] if arriving else going.at[j],
-            dst_ref=came.at[spot],
-            send_sem=send_sems.at[way, number, 2],
-            recv_sem=recv_sems.at[way, number, 2],
+        ref = weight_all.at[j, side if piece == 0 else 1 - side]
+        return pltpu.make_async_remote_copy(
+            src_ref=(kept_ref, came_ref)[piece] if number == 1 else ref,
+            dst_ref=ref,
+            send_sem=send_sems.at[way, number, piece],
+            recv_sem=recv_sems.at[way, number, piece],
             device_id=devices[way],
             device_id_type=MESH,
         )
 
+    cut = own.shape[0] // 2
+    spans = (slice(0, cut), slice(cut, 2 * cut))
+
+    def sum_copy(way, number, at, receiver, arriving, piece):
+        j = named(way, sum_block(at, number))
+        spot = j if way == 0 else jnp.where(j == receiver, planes, j)
+        here = pl.ds(piece * cut, cut)
+        return j, spot, pltpu.make_async_remote_copy(
+            src_ref=came.at[spot, here] if arriving else going.at[j, here],
+            dst_ref=came.at[spot, here],
+            send_sem=send_sems.at[way, number, 2 + piece],
+            recv_sem=recv_sems.at[way, number, 2 + piece],
+            device_id=devices[way],
+            device_id_type=MESH,
+        )
+
     def next_plane(way):
         return plane + 1 if way == 0 else plane - 1
 
-    def finish_send(way, number):
+    def finish_send(way, number, piece):
         at = depth(way)
 
         @pl.when(has_after[way] & is_weight(at, number))
         def _():
-            for copy in weight_copies(way, number, at):
-                copy.wait_send()
+            weight_copy(way, number, at, piece).wait_send()
 
         @pl.when(has_after[way] & jnp.logical_not(is_weight(at, number)))
         def _():
-            sum_copy(way, number, at, next_plane(way), False)[2].wait_send()
-
-    def take(way, number):
+            sum_copy(way, number, at, next_plane(way), False, piece)[2].wait_send()
+
+    def take(way, number, piece):
         at = depth(way) - 1
 
         @pl.when(has_before[way] & is_weight(at, number))
         def _():
-            for copy in weight_copies(way, number, at):
-                copy.wait_recv()
+            weight_copy(way, number, at, piece).wait_recv()
 
         @pl.when(has_before[way] & jnp.logical_not(is_weight(at, number)))
         def _():
-            j, spot, copy = sum_copy(way, number, at, plane, True)
+            j, spot, copy = sum_copy(way, number, at, plane, True, piece)
             copy.wait_recv()
+            here = spans[piece]
 
             @pl.when(j == plane)
             def _():
-                own[...] += came[spot].astype(wide)
+                own[here] += came[spot, here].astype(wide)
 
             @pl.when(j != plane)
             def _():
-                going[j] = (going[j].astype(wide) + came[spot].astype(wide)).astype(narrow)
-
-    def give(way, number):
+                going[j, here] = (
+                    going[j, here].astype(wide) + came[spot, here].astype(wide)
+                ).astype(narrow)
+
+    def give(way, number, piece):
         at = depth(way)
 
         @pl.when(has_after[way] & is_weight(at, number))
         def _():
-            for copy in weight_copies(way, number, at):
-                copy.start()
+            weight_copy(way, number, at, piece).start()
 
         @pl.when(has_after[way] & jnp.logical_not(is_weight(at, number)))
         def _():
-            sum_copy(way, number, at, next_plane(way), False)[2].start()
+            sum_copy(way, number, at, next_plane(way), False, piece)[2].start()
 
     step = slope_stage.shape[1]
     blocks = tokens // step
@@ -640,9 +669,13 @@
     def hidden_units(i, carry):
         here = pl.ds(pl.multiple_of(i * step, 128), step)
         slot = i % 2
-        hidden = bias_ref[...] + nn(left_vmem[0, 0, here], fc1_ref[0:group])
-        for j in range(1, planes):
-            hidden += nn(left_vmem[0, j, here], fc1_ref[j * group : (j + 1) * group])
+        parts = []
+        for part_ref in (fc1_head_ref, fc1_tail_ref):
+            part = nn(left_vmem[0, 0, here], part_ref[0:group])
+            for j in range(1, planes):
+                part += nn(left_vmem[0, j, here], part_ref[j * group : (j + 1) * group])
+            parts.append(part)
+        hidden = bias_ref[...] + jnp.concatenate(parts, axis=1)
         squared = hidden * hidden
         inner = jnp.tanh(0.7978845608028654 * hidden * (1.0 + 0.044715 * squared))
         half_sum = 0.5 * (1.0 + inner)
@@ -672,97 +705,99 @@
         def _():
             store_grad(j - 2, slot).wait()
 
-        grad_stage[slot] = nn(turned[...], left_vmem[n_left - 1, j]).astype(narrow)
+        block = nn(turned[...], left_vmem[n_left - 1, j]).astype(narrow)
+        for number in range(2):
+            grad_stage[slot, number] = block[:, number * rows : (number + 1) * rows]
         store_grad(j, slot).start()
         return carry
 
-    kept.wait()
-    for way in range(2):
-
-        @pl.when(has_after[way] & (depth(way) > 0))
-        def _():
-            weight_copies(way, 1, depth(way), (0,))[0].start()
-
+    for piece in range(2):
+        for way in range(2):
+            give(way, 1, piece)
+    for copy in own_weight:
+        copy.start()
     lax.fori_loop(0, blocks, turn, 0)
     multiply(0)
-    for way in range(2):
-
-        @pl.when(has_after[way] & (depth(way) == 0))
-        def _():
-            sum_copy(way, 1, 0, next_plane(way), False)[2].start()
-
-    other.wait_recv()
-    for way in range(2):
-
-        @pl.when(has_after[way] & (depth(way) > 0))
-        def _():
-            weight_copies(way, 1, depth(way), (1,))[0].start()
-
-    for k in range(1, planes):
-        multiply(k)
-
-    lax.fori_loop(0, blocks // 2, hidden_units, 0)
+    multiply(1)
+
+    work = [lambda: [multiply(k) for k in range(2, planes)]]
+    parts = min(4, blocks)
+    for part in range(parts):
+        work.append(
+            functools.partial(
+                lax.fori_loop, part * blocks // parts, (part + 1) * blocks // parts, hidden_units, 0
+            )
+        )
+    for part in range(2):
+        work.append(
+            functools.partial(
+                lax.fori_loop, part * planes // 2, (part + 1) * planes // 2, fc2_gradient, 0
+            )
+        )
     for number in range(2, planes + 1):
+        for piece in range(2):
+            for way in range(2):
+                take(way, number - 1, piece)
+                finish_send(way, number - 1, piece)
+                give(way, number, piece)
+            if work:
+                work.pop(0)()
+    for part in work:
+        part()
+    for piece in range(2):
         for way in range(2):
-            take(way, number - 1)
-            finish_send(way, number - 1)
-            give(way, number)
-        if number == 2:
-            lax.fori_loop(blocks // 2, blocks, hidden_units, 0)
-            lax.fori_loop(0, planes // 2, fc2_gradient, 0)
-        if number == min(3, planes):
-            lax.fori_loop(planes // 2, planes, fc2_gradient, 0)
-    for way in range(2):
-        take(way, planes)
-    for way in range(2):
-        finish_send(way, planes)
+            take(way, planes, piece)
+    for number in range(2):
+        out_ref[number] = own[:, number * rows : (number + 1) * rows].astype(narrow)
+    for piece in range(2):
+        for way in range(2):
+            finish_send(way, planes, piece)
     for slot in range(2):
         for copy in store_hidden(blocks - 2 + slot, slot) + [store_grad(planes - 2 + slot, slot)]:
             copy.wait()
-    for copy in copies.started:
-        copy.wait_send()
+    for copy in own_weight:
+        copy.wait()
 
 
 def backward_step(planes, lefts, rights, which, fc1, bias, weight, collective_id):
     tokens, width = rights[0].shape
-    group, columns, hidden = D // planes, width * len(rights), fc1.shape[1]
+    group, columns, hidden = D // planes, width * len(rights), bias.shape[1]
     rows, step = group // 2, min(256, tokens // 2)
     anywhere, vmem = pl.BlockSpec(memory_space=pl.ANY), pl.BlockSpec(memory_space=pltpu.VMEM)
     total, weight_all, active, slope, grad = pl.pallas_call(
         functools.partial(scatter_kernel, planes, which),
-        in_specs=[anywhere] * len(lefts) + [vmem] * (len(rights) + 2) + [anywhere],
+        in_specs=[anywhere] * len(lefts) + [vmem] * (len(rights) + 3) + [anywhere] * 2,
         out_specs=[vmem] + [anywhere] * 4,
         out_shape=[
-            jax.ShapeDtypeStruct((columns, group), wide),
-            jax.ShapeDtypeStruct((planes, 2, rows, weight.shape[1] // 2), narrow),
+            jax.ShapeDtypeStruct((2, columns, rows), narrow),
+            jax.ShapeDtypeStruct((planes, 2, rows, weight[0].shape[1]), narrow),
             jax.ShapeDtypeStruct((tokens, hidden), narrow),
             jax.ShapeDtypeStruct((tokens, hidden), wide),
-            jax.ShapeDtypeStruct((planes, hidden, group), narrow),
+            jax.ShapeDtypeStruct((planes, 2, hidden, rows), narrow),
         ],
         scratch_shapes=[
             pltpu.VMEM((len(lefts), planes, tokens, group), narrow),
+            pltpu.VMEM((columns, group), wide),
             pltpu.VMEM((columns, tokens), narrow),
             pltpu.VMEM((planes, columns, group), narrow),
             pltpu.VMEM((planes + 1, columns, group), narrow),
             pltpu.VMEM((2, step, hidden), narrow),
             pltpu.VMEM((2, step, hidden), wide),
-            pltpu.VMEM((2, hidden, group), narrow),
+            pltpu.VMEM((2, 2, hidden, rows), narrow),
             pltpu.SemaphoreType.DMA((len(lefts), planes)),
-            pltpu.SemaphoreType.DMA((2, planes + 1, 3)),
-            pltpu.SemaphoreType.DMA((2, planes + 1, 3)),
-            pltpu.SemaphoreType.DMA((2,)),
-            pltpu.SemaphoreType.DMA((2,)),
-            pltpu.SemaphoreType.DMA((3, 2)),
+            pltpu.SemaphoreType.DMA((2, planes + 1, 4)),
+            pltpu.SemaphoreType.DMA((2, planes + 1, 4)),
+            pltpu.SemaphoreType.DMA((4, 2)),
         ],
         compiler_params=pltpu.CompilerParams(
-            collective_id=collective_id, has_side_effects=True, vmem_limit_bytes=62 * MIB
+            collective_id=collective_id, has_side_effects=True, vmem_limit_bytes=VMEM
         ),
         cost_estimate=pl.CostEstimate(
             flops=40 * tokens * D * columns, bytes_accessed=2 * tokens * D, transcendentals=0
         ),
         name="backward_step",
-    )(*lefts, *rights, fc1, bias, weight)
-    return total, weight_all.reshape(D, weight.shape[1] // 2), active, slope, grad
+    )(*lefts, *rights, *fc1, bias, *weight)
+    return total, weight_all.reshape(D, weight[0].shape[1]), active, slope, grad
 
 
 def project_kernel(normed_ref, given_ref, in_ref, out_ref, bias_ref, projected_ref, given_attn_ref):
@@ -792,7 +827,7 @@
             jax.ShapeDtypeStruct((tokens, 3 * width), wide),
             jax.ShapeDtypeStruct((tokens, width), narrow),
         ],
-        compiler_params=pltpu.CompilerParams(vmem_limit_bytes=48 * MIB),
+        compiler_params=pltpu.CompilerParams(vmem_limit_bytes=VMEM),
         cost_estimate=pl.CostEstimate(
             flops=8 * tokens * D * width, bytes_accessed=8 * tokens * D, transcendentals=0
         ),
@@ -800,34 +835,163 @@
     )(normed, given, weights, weights, bias)
 
 
-def product_kernel(count, *refs):
-    total = nt(refs[0][...], refs[count][...])
-    for number in range(1, count):
-        total += nt(refs[number][...], refs[count + number][...])
-    refs[2 * count][...] = total.astype(narrow)
-
-
-def sum_of_products(pairs):
-    tokens = pairs[0][0].shape[0]
-    block = min(256, tokens)
-    left = [pl.BlockSpec((block, a.shape[1]), lambda i: (i, 0)) for a, _, _ in pairs]
-    right = [
-        pl.BlockSpec((w.shape[0], a.shape[1]), functools.partial(lambda c, i: (0, c), c))
-        for a, w, c in pairs
-    ]
-    depth = sum(a.shape[1] for a, _, _ in pairs)
+def reduce_kernel(terms, n_left, n_right, *refs):
+    left_refs, right_refs = refs[:n_left], refs[n_left : n_left + n_right]
+    (
+        extra_ref,
+        out_ref,
+        extra_came,
+        core_going,
+        core_came,
+        sums,
+        x_going,
+        x_came,
+        y_going,
+        y_came,
+        send_sems,
+        recv_sems,
+    ) = refs[n_left + n_right :]
+    side, chip, core, over_x, over_y, over_core = neighbours()
+    mine, columns = out_ref.shape
+    cut = columns // 4
+    first, second = slice(0, cut), slice(cut, columns)
+    greet((over_x, True), (over_y, True), (over_core, True))
+
+    extra = pltpu.make_async_remote_copy(
+        src_ref=extra_ref.at[1 - side],
+        dst_ref=extra_came,
+        send_sem=send_sems.at[0, 4],
+        recv_sem=recv_sems.at[0, 4],
+        device_id=over_x,
+        device_id_type=MESH,
+    )
+    extra.start()
+
+    def copy(lane, number):
+        going, came, other = (
+            (core_going, core_came, over_core),
+            (x_going, x_came, over_x),
+            (y_going, y_came, over_y),
+        )[lane]
+        if lane == 0:
+            here = number
+        else:
+            here = (number, slice(None), first if (lane == 1) == (number < 2) else second)
+        return pltpu.make_async_remote_copy(
+            src_ref=going.at[here],
+            dst_ref=came.at[here],
+            send_sem=send_sems.at[lane, number],
+            recv_sem=recv_sems.at[lane, number],
+            device_id=other,
+            device_id_type=MESH,
+        )
+
+    def product(number):
+        here = pl.ds(pl.multiple_of(number * mine, 16), mine)
+        total = None
+        for left, start, width, right, column in terms:
+            part = nt(
+                left_refs[left][here, start : start + width],
+                right_refs[right][:, column : column + width],
+            )
+            total = part if total is None else total + part
+        return total
+
+    def quarter(q, carry):
+        its_side = jnp.where(q < 2, 1 - side, side)
+        its_chip = jnp.where(q % 2 == 0, 1 - chip, chip)
+        base = (its_side * 2 + its_chip) * 2
+        core_going[q] = product(base + 1 - core).astype(narrow)
+        copy(0, q).start()
+        block = product(base + core)
+        copy(0, q).wait_recv()
+        sums[q] = block + core_came[q].astype(wide)
+
+        for number in range(2):
+
+            @pl.when(q == number)
+            def _():
+                x_going[number, :, first] = sums[number, :, first].astype(narrow)
+                copy(1, number).start()
+
+            @pl.when(q == 2 * number)
+            def _():
+                y_going[number, :, second] = sums[2 * number, :, second].astype(narrow)
+                copy(2, number).start()
+
+        return carry
+
+    lax.fori_loop(0, 4, quarter, 0)
+    copy(1, 0).wait_recv()
+    y_going[2, :, first] = (sums[2, :, first] + x_came[0, :, first].astype(wide)).astype(narrow)
+    copy(2, 2).start()
+    copy(2, 0).wait_recv()
+    x_going[2, :, second] = (sums[1, :, second] + y_came[0, :, second].astype(wide)).astype(narrow)
+    copy(1, 2).start()
+    copy(1, 1).wait_recv()
+    out_ref[:, first] = sums[3, :, first] + x_came[1, :, first].astype(wide)
+    copy(2, 1).wait_recv()
+    out_ref[:, second] = sums[3, :, second] + y_came[1, :, second].astype(wide)
+    copy(2, 2).wait_recv()
+    out_ref[:, first] += y_came[2, :, first].astype(wide)
+    copy(1, 2).wait_recv()
+    out_ref[:, second] += x_came[2, :, second].astype(wide)
+    extra.wait()
+    for q in range(4):
+        copy(0, q).wait_send()
+    for lane in (1, 2):
+        for number in range(3):
+            copy(lane, number).wait_send()
+
+
+def distinct(values):
+    kept = []
+    for value in values:
+        if not any(value is other for other in kept):
+            kept.append(value)
+    return kept
+
+
+def place_of(value, values):
+    return next(i for i, other in enumerate(values) if other is value)
+
+
+def reduce_products(mine, terms, extra, collective_id):
+    lefts = distinct([term[0] for term in terms])
+    rights = distinct([term[3] for term in terms])
+    places = tuple(
+        (place_of(a, lefts), start, width, place_of(w, rights), column)
+        for a, start, width, w, column in terms
+    )
+    tokens, depth = terms[0][0].shape[0], sum(term[2] for term in terms)
+    anywhere, vmem = pl.BlockSpec(memory_space=pl.ANY), pl.BlockSpec(memory_space=pltpu.VMEM)
     return pl.pallas_call(
-        functools.partial(product_kernel, len(pairs)),
-        grid=(tokens // block,),
-        in_specs=left + right,
-        out_specs=pl.BlockSpec((block, D), lambda i: (i, 0)),
-        out_shape=jax.ShapeDtypeStruct((tokens, D), narrow),
-        compiler_params=pltpu.CompilerParams(vmem_limit_bytes=48 * MIB),
+        functools.partial(reduce_kernel, places, len(lefts), len(rights)),
+        in_specs=[vmem] * (len(lefts) + len(rights)) + [anywhere],
+        out_specs=[vmem, anywhere],
+        out_shape=[
+            jax.ShapeDtypeStruct((mine, D), wide),
+            jax.ShapeDtypeStruct(extra.shape[1:], extra.dtype),
+        ],
+        scratch_shapes=[
+            pltpu.VMEM((4, mine, D), narrow),
+            pltpu.VMEM((4, mine, D), narrow),
+            pltpu.VMEM((4, mine, D), wide),
+            pltpu.VMEM((3, mine, D), narrow),
+            pltpu.VMEM((3, mine, D), narrow),
+            pltpu.VMEM((3, mine, D), narrow),
+            pltpu.VMEM((3, mine, D), narrow),
+            pltpu.SemaphoreType.DMA((3, 5)),
+            pltpu.SemaphoreType.DMA((3, 5)),
+        ],
+        compiler_params=pltpu.CompilerParams(
+            collective_id=collective_id, has_side_effects=True, vmem_limit_bytes=VMEM
+        ),
         cost_estimate=pl.CostEstimate(
-            flops=2 * tokens * depth * D, bytes_accessed=2 * depth * (tokens + D), transcendentals=0
+            flops=8 * tokens * depth * D, bytes_accessed=2 * depth * (tokens + D), transcendentals=0
         ),
-        name="sum_of_products",
-    )(*[a for a, _, _ in pairs], *[w for _, w, _ in pairs])
+        name="reduce_products",
+    )(*lefts, *rights, extra)
 
 
 def solution(mesh):
@@ -895,29 +1059,6 @@
         def halves_of(kept, came):
             return in_order(kept, came).astype(wide)
 
-        def scatter_sides(total):
-            parts = total.astype(narrow).reshape(total.shape[0], 2, rows)
-            return halves_of(pick(parts, side, 1), send_x(pick(parts, 1 - side, 1)))
-
-        def scatter_tokens(total):
-            parts = total.reshape(2, 2, 2, mine, D)
-            came = send_core(pick(parts, 1 - core, 2).astype(narrow))
-            summed = pick(parts, core, 2).astype(wide) + came.astype(wide)
-            halves = []
-            for number, columns in enumerate((summed[..., : D // 2], summed[..., D // 2 :])):
-                if number == 0:
-                    came = send_x(pick(columns, 1 - side, 0).astype(narrow))
-                    part = pick(columns, side, 0) + came.astype(wide)
-                    came = send_y(pick(part, 1 - chip, 0).astype(narrow))
-                    part = pick(part, chip, 0) + came.astype(wide)
-                else:
-                    came = send_y(pick(columns, 1 - chip, 1).astype(narrow))
-                    part = pick(columns, chip, 1) + came.astype(wide)
-                    came = send_x(pick(part, 1 - side, 0).astype(narrow))
-                    part = pick(part, side, 0) + came.astype(wide)
-                halves.append(part)
-            return jnp.concatenate(halves, axis=1)
-
         def reduce_all(v):
             for axis, size in (("tp", nt_axis), ("fsdp", nf)):
                 bit = 1
@@ -926,19 +1067,31 @@
                     bit *= 2
             return v
 
-        normed, grad_rows, full_qo, fc1_block, fc2_rows, bounds, cosine, sine = gather_tokens(
+        (
+            normed,
+            grad_rows,
+            full_qo,
+            fc1_head,
+            fc1_block,
+            fc2_kept,
+            fc2_going,
+            bounds,
+            cosine,
+            sine,
+        ) = gather_tokens(
             nf // 2,
             inputs,
             segments,
-            ln_gain.astype(wide).reshape(1, D),
-            ln_bias.astype(wide).reshape(1, D),
+            ln_gain.reshape(1, D),
+            ln_bias.reshape(1, D),
             cotangent,
             w_qkv,
             w_out,
             w_fc1,
             w_fc2,
         )
-        full_fc1 = gather_planes(fc1_block)
+        fc1_tail = gather_planes(fc1_block)
+        fc2_came = send_x(fc2_going)
         tokens_in = inputs.astype(wide)
         _, norm_back = jax.vjp(
             layer_norm, tokens_in, ln_gain.astype(wide), ln_bias.astype(wide)
@@ -958,30 +1111,47 @@
             [normed, grad_rows],
             [grad_q, grad_k, grad_v, mixed],
             (0, 0, 0, 1),
-            full_fc1,
+            (fc1_head, fc1_tail),
             bias_fc1.astype(wide).reshape(1, half_ff),
-            fc2_rows,
+            (fc2_kept, fc2_came),
             2,
         )
-        sum_fc2 = scatter_sides(sum_planes(grad_w2.reshape(-1, grad_w2.shape[2])))
+        grad_q, grad_k, grad_v, sum_qo = lax.optimization_barrier((grad_q, grad_k, grad_v, sum_qo))
+        total_fc2 = sum_planes(grad_w2.reshape(-1, rows))
         grad_hidden = (nn(grad_rows, full_fc2) * slope).astype(narrow)
         grad_w1 = tn(normed, grad_hidden).astype(narrow)
+        mixed, grad_w1 = lax.optimization_barrier((mixed, grad_w1))
+        branch_local, came_qo = reduce_products(
+            mine,
+            [(mixed, 0, half_qkv, full_qo, 3 * half_qkv), (active_low, 0, half_ff, full_fc2, 0)],
+            sum_qo,
+            4,
+        )
+        total_fc2, grad_hidden, grad_w1, branch_local = lax.optimization_barrier(
+            (total_fc2, grad_hidden, grad_w1, branch_local)
+        )
         total_fc1 = sum_planes(grad_w1)
-        grad_hidden, mixed, grad_w1 = lax.optimization_barrier((grad_hidden, mixed, grad_w1))
+        total_fc2 = total_fc2.reshape(2, half_ff, rows)
+        head = fc1_head.shape[1]
+        grad_normed, came_fc2 = reduce_products(
+            mine,
+            [
+                (grad_q, 0, half_qkv, full_qo, 0),
+                (grad_k, 0, half_qkv, full_qo, half_qkv),
+                (grad_v, 0, half_qkv, full_qo, 2 * half_qkv),
+                (grad_hidden, 0, head, fc1_head, 0),
+                (grad_hidden, head, half_ff - head, fc1_tail, 0),
+            ],
+            total_fc2,
+            3,
+        )
+        sum_qo = halves_of(pick(sum_qo, side), came_qo)
+        sum_fc2 = halves_of(pick(total_fc2, side), came_fc2)
         grad_projected = jnp.concatenate([grad_q, grad_k, grad_v], axis=1)
-        grad_normed = scatter_tokens(
-            sum_of_products(
-                [(grad_q, full_qo, 0), (grad_k, full_qo, 1), (grad_v, full_qo, 2), (grad_hidden, full_fc1, 0)]
-            )
-        )
-        branch_local = scatter_tokens(
-            sum_of_products([(mixed, full_qo, 3), (active_low, full_fc2, 0)])
-        )
         outputs = (tokens_in + branch_local + b_out.astype(wide) + b_fc2.astype(wide)).astype(narrow)
         grad_tokens, grad_gain, grad_offset = norm_back(grad_normed)
         grad_tokens = grad_tokens + cotangent.astype(wide)
 
-        sum_qo = scatter_sides(sum_qo)
         grad_w_qkv = sum_qo[:, : 3 * half_qkv].reshape(2, 3, half_qkv, rows)
         grad_w_qkv = grad_w_qkv.transpose(1, 3, 0, 2).reshape(3, rows, 2 * half_qkv)
         grad_w_out = sum_qo[:, 3 * half_qkv :].reshape(2 * half_qkv, rows)
@@ -1004,9 +1174,9 @@
                 [bias_qkv_full.reshape(-1), bias_fc1_full, grad_gain, grad_offset, cotangent_sum]
             ).reshape(-1, 128)
         ).reshape(-1)
-        total_fc1, outputs, grad_tokens, small, grad_w_qkv, grad_w_out, grad_w_fc2 = (
+        total_fc1, outputs, grad_tokens, grad_w_qkv, grad_w_out, grad_w_fc2 = (
             lax.optimization_barrier(
-                (total_fc1, outputs, grad_tokens, small, grad_w_qkv, grad_w_out, grad_w_fc2)
+                (total_fc1, outputs, grad_tokens, grad_w_qkv, grad_w_out, grad_w_fc2)
             )
         )
         parts = total_fc1.reshape(2, rows, total_fc1.shape[1])

time: 567 us -> 471 us (0.83)
  waiting for transfers between devices: 94.1 us -> 15.9 us
  Pallas kernels: 304 us -> 374 us
  local copies, waits for them, and re-layouts: 79.3 us -> 13.9 us
  other arithmetic: 32 us -> 18.3 us
    pallas_call x2, Pallas kernels: 37.5 us -> 109 us  [reduce_products(): pl.pallas_call(functools.partial(reduce_kernel, places, len(lefts), len(r...]
    ppermute x7 -> x2, waiting for transfers between devices: 36.6 us -> 6.29 us  [send_x(): return lax.ppermute(v, 'fsdp', swap_f)]
    ppermute x6 -> x0, waiting for transfers between devices: 25 us -> none  [the longest x4 25 us: send_y(): return lax.ppermute(v, 'tp', swap_chip)]
    pallas_call x1, Pallas kernels: 121 us -> 97.7 us  [backward_step(): pl.pallas_call(functools.partial(scatter_kernel, planes, which), in_specs...]
    unnamed x88 -> x56, local copies, waits for them, and re-layouts: 28.2 us -> 4.89 us
    dynamic_slice x8 -> x1, local copies, waits for them, and re-layouts: 22.7 us -> 0.07 us  [pick(): return lax.dynamic_index_in_dim(v, index, axis, keepdims=False)]
    pallas_call x1, Pallas kernels: 87.5 us -> 108 us  [gather_tokens(): pl.pallas_call(functools.partial(gather_kernel, planes), in_specs=[vmem]...]
    all_gather x1, waiting for transfers between devices: 15.7 us -> 0.02 us  [gather_planes(): lax.all_gather(block, 'fsdp', axis=0, tiled=True, axis_index_groups=colum...]
  transfers between devices with their start and end apart: 21 -> 10, of which waited for: 11 -> 5; matrix products, arithmetic and copies ran while one was open for 18% -> 10% of each run, Pallas kernels for 17% -> 36%
where the time goes in v4:
time: 471 us; the launch traced here: 468 us
  Pallas kernels  374 us (79%)
  matrix products  24.4 us (5%)
  other arithmetic  18.3 us (4%)
  waiting for transfers between devices  15.9 us (3%)
  between operations  14.3 us (3%)
  local copies, waits for them, and re-layouts  13.9 us (3%)
  starting transfers between devices  7.5 us (2%)
    pallas_call x2, Pallas kernels, reduce_products(): pl.pallas_call(functools.partial(reduce_kernel, places, len(lefts), len(r...  109 us
    pallas_call x1, Pallas kernels, gather_tokens(): pl.pallas_call(functools.partial(gather_kernel, planes), in_specs=[vmem]...  108 us
    pallas_call x1, Pallas kernels, backward_step(): pl.pallas_call(functools.partial(scatter_kernel, planes, which), in_specs...  97.7 us
    pallas_call x1, Pallas kernels, attention(): pl.pallas_call(functools.partial(attention_kernel, rows), grid=(tokens //...  42.8 us
    pallas_call x1, Pallas kernels, project(): pl.pallas_call(project_kernel, grid=(tokens // block,), in_specs=[row, ro...  16.6 us
    dot_general x1, matrix products, nn(): lax.dot_general(a, b, (((1,), (0,)), ((), ())), preferred_element_type=wide)  13.9 us
    dot_general x1, matrix products, tn(): lax.dot_general(a, b, (((0,), (0,)), ((), ())), preferred_element_type=wide)  10.5 us
    ppermute x5, waiting for transfers between devices, reduce_all(): v = v + lax.ppermute(v, axis, [(i, i ^ bit) for i in range(size)])  9.47 us
  transfers between devices with their start and end apart: 10, of which 5 were waited for; matrix products, arithmetic and copies ran while one was open for 10% of the time, Pallas kernels for 36%

profile of v4, /device:TPU:0, one launch (start us, length us, event | category | flops | bytes accessed | tf_op | source)
XLA Modules:
  0.0 468.0 jit_solution(8520781933928259921)
XLA Ops:
  7.2 1.3 reshape.143.gain_ref
  8.5 1.3 reshape.144.bias_ref
  9.8 107.6 %gather_tokens.1 = (bf16[2,2,2,256,2048]{4,3,2,1,0:T(8,128)(2,1)}, bf16[2,2,2,256,2048]{4,3,2,1,0:T(8,128)(2,1)}, bf16[4,2,256,1024]{3,2,1,0:T(8,128)(2,1)}, bf1...) custom-call(bf16[256,2048]{1,0:T(8,128)(2,1)} %input_ref.1, ...), custom_call_target="tpu_custom_call" | custom-call | tf_op jit(solution)/shard_map/gather_tokens/pallas_call | solution.py:452
  117.7 1.6 collective-permute-start
  119.2 0.6 convert_element_type.58
  119.8 0.6 copy.26
  120.4 0.6 convert_element_type.56
  121.0 0.6 convert_element_type.55
  121.6 0.6 dynamic-slice_convert_fusion
  122.2 0.2 convert_reduce_fusion.2
  122.4 0.6 broadcast_multiply_fusion
  123.0 16.6 %project.1 = (f32[2048,768]{1,0:T(8,128)}, bf16[2048,256]{1,0:T(8,128)(2,1)}) custom-call(bf16[2048,2048]{1,0:T(8,128)(2,1)} %bitcast.56, bf16[2048,2048]{1,0:T(8,128)(2,1)} %bitcast.59, bf16[2048,1024]{1,0:T(8,128)(2,1)} %bitcast.62, bf16[2048,1024]{1,0:T(8,128)(2,1)} %bitcast.63, f32[1,768]{1,0:T(1,128)} %bitcast.55), custom_call_target="tpu_custom_call" | custom-call | flops 8589934592 | bytes 33554432 | tf_op jit(solution)/shard_map/project/pallas_call | solution.py:812
  139.6 42.8 %attention.1 = (bf16[2048,256]{1,0:T(8,128)(2,1)}, bf16[2048,256]{1,0:T(8,128)(2,1)}, bf16[2048,256]{1,0:T(8,128)(2,1)}, bf16[2048,256]{1,0:T(8,128)(2,1)}) custom-call(f32[2,8,128]{2,1,0:T(8,128)} %get-tuple-element.55.bound_ref, f32[2048,128]{1,0:T(8,128)} %get-tuple-element.56.cos_ref, f32[2048,128]{1,0:T(8,128)} %get-tuple-element.57.sin_ref, ...), custom_call_target="tpu_custom_call" | custom-call | flops 6442450944 | bytes 16777216 | tf_op jit(solution)/shard_map/attention/pallas_call | solution.py:147
  182.5 0.8 copy-done.24
  183.2 97.7 %backward_step.1 = (bf16[2,1024,256]{2,1,0:T(8,128)(2,1)}, bf16[4,2,256,1024]{3,2,1,0:T(8,128)(2,1)}, bf16[2048,1024]{1,0:T(8,128)(2,1)}, f32[2048,1024]{1,0:T(8,128)}, bf16[4,2,1024,256]{3,2,1,0:T(8,128)(2,1)}) custom-call(bf16[2048,2048]{1,0:T(8,128)(2,1)} %bitcast.57, bf16[2048,2048]{1,0:T(8,128)(2,1)} %bitcast.60, ...), custom_call_target="tpu_custom_call" | custom-call | flops 171798691840 | bytes 8388608 | tf_op jit(solution)/shard_map/backward_step/pallas_call | solution.py:767
  281.2 13.9 %multiply_convert_fusion.refs_3_ = bf16[2048,1024]{1,0:T(8,128)(2,1)S(1)} fusion(f32[2048,1024]{1,0:T(8,128)} %get-tuple-element.71, bf16[2048,2048]{1,0:T(8,128)(2,1)} %bitcast.61, bf16[2048,1024]{1,0:T(8,128)(2,1)} %bitcast.68), kind=kOutput, calls=%fused_computation.1 | convolution fusion | flops 8594128896 | bytes 25165824 | tf_op jit(solution)/shard_map/dot_general | solution.py:52
  295.1 2.0 copy-done.3
  297.1 10.5 %convolution_convert_fusion = bf16[2048,1024]{1,0:T(8,128)(2,1)} fusion(bf16[2048,2048]{1,0:T(8,128)(2,1)S(1)} %bitcast.58, bf16[2048,1024]{1,0:T(8,128)(2,1)S(1)} %multiply_convert_fusion.refs_3_), kind=kOutput, calls=%fused_computation.3 | convolution fusion | flops 8592031744 | bytes 16777216 | tf_op jit(solution)/shard_map/dot_general | solution.py:56
  307.6 0.6 convert_reduce_fusion.1
  308.2 53.5 %reduce_products.2 = (f32[256,2048]{1,0:T(8,128)}, bf16[1024,256]{1,0:T(8,128)(2,1)}) custom-call(bf16[2048,256]{1,0:T(8,128)(2,1)} %get-tuple-element.73.refs_5_.refs_0_, bf16[2048,1024]{1,0:T(8,128)(2,1)} %get-tuple-element.74.refs_1_, bf16[2048,1024]{1,0:T(8,128)(2,1)} %bitcast.64, bf16[2048,1024]{1,0:T(8,128)(2,1)} %bitcast.69, ...), custom_call_target="tpu_custom_call" | custom-call | flops 42949672960 | bytes 10485760 | tf_op jit(solution)/shard_map/reduce_products/pallas_call | solution.py:968
  361.8 2.9 convert_reduce_fusion
  364.7 0.3 dynamic_update_slice.7
  365.0 55.4 %reduce_products.3 = (f32[256,2048]{1,0:T(8,128)}, bf16[1024,256]{1,0:T(8,128)(2,1)}) custom-call(bf16[2048,256]{1,0:T(8,128)(2,1)} %get-tuple-element.80.refs_2_.refs_0_, bf16[2048,256]{1,0:T(8,128)(2,1)} %get-tuple-element.81.refs_3_.refs_1_, bf16[2048,256]{1,0:T(8,128)(2,1)} %get-tuple-element.82.refs_4_.refs_2_, bf16[2048,1024]{1,0:T(8,128)(2,1)} %copy-done.3, ...), custom_call_target="tpu_custom_call" | custom-call | flops 60129542144 | bytes 14680064 | tf_op jit(solution)/shard_map/reduce_products/pallas_call | solution.py:968
  420.5 2.4 fusion.14
  423.0 1.0 fusion.7
  424.1 0.7 copy-done.5
  424.8 3.3 convert_reduce_fusion.3
  428.3 1.1 collective-permute-done.1
  429.4 0.8 collective-permute-start.2
  430.4 3.6 collective-permute-done.2
  434.0 0.8 collective-permute-start.3
  434.8 1.5 bitcast_convert_fusion
  436.4 2.2 collective-permute-done.3
  438.6 1.5 collective-permute-start.4
  440.0 0.2 fusion.11
  440.4 0.8 slice.30
  441.2 0.8 copy.25
  442.0 2.4 reshape.158
  444.5 1.5 collective-permute-start.5
  446.0 1.3 bitcast_convert_fusion.1
  447.3 0.8 collective-permute-start.6
  448.1 2.6 collective-permute-done.5
  450.8 0.6 reshape.163
  451.4 0.6 slice_bitcast_fusion.1
  452.0 0.6 slice_bitcast_fusion
  452.6 6.3 %collective-permute-done.6 = bf16[256,1024]{1,0:T(8,128)(2,1)S(1)} collective-permute-done((bf16[256,1024]{1,0:T(8,128)(2,1)S(1)}, bf16[256,1024]{1,0:T(8,128)(2,1)S(1)}, u32[]{:S(2)}, u32[]{:S(2)}) %collective-permute-start.6) | collective-permute-done | bytes 524320 | tf_op jit(solution)/shard_map/ppermute | solution.py:1006
  459.0 1.6 maximum_select_fusion
  460.6 0.6 copy.34
  (82 shorter events, 1.5 us)
Async XLA Ops:
  7.2 175.3 %all-gather.2.cloned.1.call-start = ((), (), s32[]{:S(2)}) async-start(), calls=%async_computation.2 | async-start | bytes 3932160 | tf_op jit(solution)/shard_map/all_gather | solution.py:1016
  9.8 109.4 %copy-start.18 = (bf16[2048]{0:T(1024)(128)(2,1)S(1)}, bf16[2048]{0:T(1024)(128)(2,1)}, u32[]{:S(2)}) copy-start(bf16[2048]{0:T(1024)(128)(2,1)} %param.15) | copy-start | bytes 12292
  9.8 110.0 %copy-start.21 = (bf16[3,512]{1,0:T(4,128)(2,1)S(1)}, bf16[3,512]{1,0:T(4,128)(2,1)}, u32[]{:S(2)}) copy-start(bf16[3,512]{1,0:T(4,128)(2,1)} %param.18) | copy-start | bytes 9220
  9.8 110.6 %copy-start.19 = (bf16[2048]{0:T(1024)(128)(2,1)S(1)}, bf16[2048]{0:T(1024)(128)(2,1)}, u32[]{:S(2)}) copy-start(bf16[2048]{0:T(1024)(128)(2,1)} %param.24) | copy-start | bytes 12292
  9.8 111.2 %copy-start.20 = (bf16[2048]{0:T(1024)(128)(2,1)S(1)}, bf16[2048]{0:T(1024)(128)(2,1)}, u32[]{:S(2)}) copy-start(bf16[2048]{0:T(1024)(128)(2,1)} %param.20) | copy-start | bytes 12292
  9.8 111.8 %copy-start.22 = (bf16[2048]{0:T(1024)(128)(2,1)S(1)}, bf16[2048]{0:T(1024)(128)(2,1)}, u32[]{:S(2)}) copy-start(bf16[2048]{0:T(1024)(128)(2,1)} %param.22) | copy-start | bytes 12292
  9.8 112.4 %copy-start = (bf16[256,2048]{1,0:T(8,128)(2,1)S(1)}, bf16[256,2048]{1,0:T(8,128)(2,1)}, u32[]{:S(2)}) copy-start(bf16[256,2048]{1,0:T(8,128)(2,1)} %input_ref.1) | copy-start | bytes 3145732
  117.4 244.3 %reduce-scatter.3.cloned.1.call-start = ((), (), s32[]{:S(2)}) async-start(), calls=%async_computation.3 | async-start | bytes 5242880 | tf_op jit(solution)/shard_map/reduce_scatter | solution.py:1051
  117.7 64.8 %collective-permute-start = (bf16[256,1024]{1,0:T(8,128)(2,1)}, bf16[256,1024]{1,0:T(8,128)(2,1)S(1)}, u32[]{:S(2)}, u32[]{:S(2)}) collective-permute-start(bf16[256,1024]{1,0:T(8,128)(2,1)} %get-tuple-element.68), channel_id=1, source_target_pairs={{0,4},{4,0},{8,12},{12,8},{16,20},{20,16},{24,28},{28,24},{1,5},{5... | collective-permute-start | bytes 1572872 | tf_op jit(solution)/shard_map/ppermute | solution.py:1006
  182.4 0.8 copy-start.24
  281.0 165.0 %reduce-scatter.5.cloned.1.call-start = ((), (), s32[]{:S(2)}) async-start(), calls=%async_computation.4 | async-start | bytes 5242880 | tf_op jit(solution)/shard_map/reduce_scatter | solution.py:1051
  281.2 15.8 %copy-start.23 = (bf16[2,2,2,256,2048]{4,3,2,1,0:T(8,128)(2,1)S(1)}, bf16[2,2,2,256,2048]{4,3,2,1,0:T(8,128)(2,1)}, u32[]{:S(2)}) copy-start(bf16[2,2,2,256,2048]{4,3,2,1,0:T(8,128)(2,1)} %get-tuple-element.53) | copy-start | bytes 25165828
  295.1 2.0 copy-start.3
  297.0 10.5 %copy-start.6 = (bf16[2048,256]{1,0:T(8,128)(2,1)S(1)}, bf16[2048,256]{1,0:T(8,128)(2,1)}, u32[]{:S(2)}) copy-start(bf16[2048,256]{1,0:T(8,128)(2,1)} %get-tuple-element.80.refs_2_.refs_0_) | copy-start | bytes 3145732
  297.0 10.5 %copy-start.7 = (bf16[2048,256]{1,0:T(8,128)(2,1)S(1)}, bf16[2048,256]{1,0:T(8,128)(2,1)}, u32[]{:S(2)}) copy-start(bf16[2048,256]{1,0:T(8,128)(2,1)} %get-tuple-element.81.refs_3_.refs_1_) | copy-start | bytes 3145732
  297.0 10.5 %copy-start.8 = (bf16[2048,256]{1,0:T(8,128)(2,1)S(1)}, bf16[2048,256]{1,0:T(8,128)(2,1)}, u32[]{:S(2)}) copy-start(bf16[2048,256]{1,0:T(8,128)(2,1)} %get-tuple-element.82.refs_4_.refs_2_) | copy-start | bytes 3145732
  365.0 55.5 %copy-start.1 = (bf16[256,2048]{1,0:T(8,128)(2,1)S(1)}, bf16[256,2048]{1,0:T(8,128)(2,1)}, u32[]{:S(2)}) copy-start(bf16[256,2048]{1,0:T(8,128)(2,1)} %input_ref.1) | copy-start | bytes 3145732
  365.0 55.5 %copy-start.13 = (f32[2048]{0:T(1024)S(1)}, f32[2048]{0:T(1024)}, u32[]{:S(2)}) copy-start(f32[2048]{0:T(1024)} %convert_element_type.58) | copy-start | bytes 24580
  365.0 55.5 %copy-start.17 = (f32[256]{0:T(256)S(1)}, f32[256]{0:T(256)}, u32[]{:S(2)}) copy-start(f32[256]{0:T(256)} %broadcast_multiply_fusion) | copy-start | bytes 3076
  420.4 2.5 copy-start.2
  422.9 1.2 copy-start.4
  422.9 1.9 copy-start.5
  422.9 1.9 copy-start.15
  422.9 1.9 copy-start.16
  424.8 3.4 copy-start.11
  424.8 3.4 copy-start.12
  428.1 2.1 copy-start.9
  428.1 1.3 collective-permute-start.1
  429.4 4.6 collective-permute-start.2
  430.4 9.6 %copy-start.10 = (bf16[1024,256]{1,0:T(8,128)(2,1)S(1)}, bf16[1024,256]{1,0:T(8,128)(2,1)}, u32[]{:S(2)}) copy-start(bf16[1024,256]{1,0:T(8,128)(2,1)} %get-tuple-element.86) | copy-start | bytes 1572868
  434.0 4.5 collective-permute-start.3
  438.6 5.9 %collective-permute-start.4 = (f32[160,128]{1,0:T(8,128)S(1)}, f32[160,128]{1,0:T(8,128)S(1)}, u32[]{:S(2)}, u32[]{:S(2)}) collective-permute-start(f32[160,128]{1,0:T(8,128)S(1)} %add.102), channel_id=1, source_target_pairs={{0,8},{4,12},{8,0},{12,4},{16,24},{20,28},{24,16},{28,20},{1,9},{5... | collective-permute-start | bytes 245768 | tf_op jit(solution)/shard_map/ppermute | solution.py:1066
  444.5 6.3 %collective-permute-start.5 = (f32[160,128]{1,0:T(8,128)S(1)}, f32[160,128]{1,0:T(8,128)S(1)}, u32[]{:S(2)}, u32[]{:S(2)}) collective-permute-start(f32[160,128]{1,0:T(8,128)S(1)} %add.103), channel_id=1, source_target_pairs={{0,16},{4,20},{8,24},{12,28},{16,0},{20,4},{24,8},{28,12},{1,17},{... | collective-permute-start | bytes 245768 | tf_op jit(solution)/shard_map/ppermute | solution.py:1066
  447.3 11.6 %collective-permute-start.6 = (bf16[256,1024]{1,0:T(8,128)(2,1)S(1)}, bf16[256,1024]{1,0:T(8,128)(2,1)S(1)}, u32[]{:S(2)}, u32[]{:S(2)}) collective-permute-start(bf16[256,1024]{1,0:T(8,128)(2,1)S(1)} %get-tuple-element.100), channel_id=1, source_target_pairs={{0,4},{4,0},{8,12},{12,8},{16,20},{20,16},{24,28},{28,24},{1,5},{5... | collective-permute-start | bytes 1572872 | tf_op jit(solution)/shard_map/ppermute | solution.py:1006
  452.0 8.6 %copy-start.14 = (f32[2048]{0:T(1024)}, f32[2048]{0:T(1024)S(1)}, u32[]{:S(2)}) copy-start(f32[2048]{0:T(1024)S(1)} %get-tuple-element.134) | copy-start | bytes 24580
Sparse Core Ops, SparseCore 0:
  117.6 63.5 all-gather.1
  281.1 75.6 reduce-scatter.2
  361.9 74.9 reduce-scatter.4

commit v5 on v4

--- a/solution.py
+++ b/solution.py
@@ -106,38 +106,38 @@
         row_start = first + lax.broadcasted_iota(jnp.int32, (rows, 1), 0)
         opening = jnp.where(row_start >= bound, bound, 0)
         allowed = (key_place <= row_place) & (key_place >= opening)
-        attn_parts, dq_parts, dk_parts, dv_parts = [], [], [], []
-        for head in range(2):
-            cols = slice(head * HEAD_DIM, (head + 1) * HEAD_DIM)
-            q = q_both[:, cols]
-            k, v = kb_ref[0:seen, cols], vb_ref[0:seen, cols]
-            do = do_ref[here, cols]
-            scores = jnp.where(allowed, nt(q, k), masked_score)
-            largest = jnp.max(scores, axis=-1, keepdims=True)
-            exponent = jnp.exp(scores - largest)
-            probs = exponent * (1.0 / jnp.sum(exponent, axis=-1, keepdims=True))
-            probs_low = probs.astype(narrow)
-            attn_parts.append(nn(probs_low, v))
-            grad_probs = nt(do, v)
-            inner = jnp.sum(probs * grad_probs, axis=-1, keepdims=True)
-            grad_scores = (probs * (grad_probs - inner)).astype(narrow)
-            dq_parts.append(nn(grad_scores, k))
-            dk_parts.append(tn(grad_scores, q))
-            dv_parts.append(tn(probs_low, do))
+        cols = [slice(head * HEAD_DIM, (head + 1) * HEAD_DIM) for head in range(2)]
+        q = [q_both[:, c] for c in cols]
+        k, v = [kb_ref[0:seen, c] for c in cols], [vb_ref[0:seen, c] for c in cols]
+        do = [do_ref[here, c] for c in cols]
+        scores = [jnp.where(allowed, nt(a, b), masked_score) for a, b in zip(q, k)]
+        grad_probs = [nt(a, b) for a, b in zip(do, v)]
+        largest = [jnp.max(x, axis=-1, keepdims=True) for x in scores]
+        exponent = [jnp.exp(x - m) for x, m in zip(scores, largest)]
+        probs = [e * (1.0 / jnp.sum(e, axis=-1, keepdims=True)) for e in exponent]
+        probs_low = [p.astype(narrow) for p in probs]
+        attn_parts = [nn(p, x) for p, x in zip(probs_low, v)]
+        inner = [jnp.sum(p * g, axis=-1, keepdims=True) for p, g in zip(probs, grad_probs)]
+        grad_scores = [
+            (p * (g - i)).astype(narrow) for p, g, i in zip(probs, grad_probs, inner)
+        ]
+        dv_parts = [tn(x, p) for x, p in zip(do, probs_low)]
+        dq_parts = [nn(g, x) for g, x in zip(grad_scores, k)]
+        dk_parts = [tn(x, g) for x, g in zip(q, grad_scores)]
         attn_ref[here] = jnp.concatenate(attn_parts, axis=1).astype(narrow)
         dq = jnp.concatenate(dq_parts, axis=1) * scale
         gq_ref[here] = turn_back(dq, cosine, sine).astype(narrow)
-        dk_ref[0:seen] += jnp.concatenate(dk_parts, axis=1)
-        dv_ref[0:seen] += jnp.concatenate(dv_parts, axis=1)
-    gk_ref[...] = turn_back(dk_ref[...], cos_ref[...], sin_ref[...]).astype(narrow)
-    gv_ref[...] = dv_ref[...].astype(narrow)
+        dk_ref[:, 0:seen] += jnp.concatenate(dk_parts, axis=0)
+        dv_ref[:, 0:seen] += jnp.concatenate(dv_parts, axis=0)
+    gk_ref[...] = turn_back(dk_ref[...].T, cos_ref[...], sin_ref[...]).astype(narrow)
+    gv_ref[...] = dv_ref[...].T.astype(narrow)
 
 
 def attention(bounds, cosine, sine, projected, grad_attn, length):
     tokens, width = grad_attn.shape
     lanes = 2 * HEAD_DIM
     pairs = width // lanes
-    rows = min(256, length)
+    rows = min(512, length)
     bound = pl.BlockSpec((1, 8, 128), lambda s, h: (s, 0, 0))
     table = pl.BlockSpec((length, lanes), lambda s, h: (s, 0))
     block = pl.BlockSpec((length, lanes), lambda s, h: (s, h))
@@ -153,8 +153,8 @@
         scratch_shapes=[
             pltpu.VMEM((length, lanes), narrow),
             pltpu.VMEM((length, lanes), narrow),
-            pltpu.VMEM((length, lanes), wide),
-            pltpu.VMEM((length, lanes), wide),
+            pltpu.VMEM((lanes, length), wide),
+            pltpu.VMEM((lanes, length), wide),
         ],
         compiler_params=pltpu.CompilerParams(vmem_limit_bytes=VMEM),
         cost_estimate=pl.CostEstimate(
@@ -282,8 +282,7 @@
     planes,
     input_ref,
     segment_ref,
-    gain_ref,
-    bias_ref,
+    affine_ref,
     w_out_ref,
     w_fc2_ref,
     given_ref,
@@ -299,7 +298,9 @@
     bound_ref,
     cos_ref,
     sin_ref,
+    given_sum_ref,
     normed_ref,
+    given_vmem,
     out_ref,
     send_sems,
     recv_sems,
@@ -340,9 +341,10 @@
 
     tokens = input_ref[...].astype(wide)
     normed_ref[...] = layer_norm(
-        tokens, gain_ref[...].astype(wide), bias_ref[...].astype(wide)
+        tokens, affine_ref[0:1].astype(wide), affine_ref[1:2].astype(wide)
     ).astype(narrow)
     kept = [copies.local(normed_ref, mine[0]), copies.local(given_ref, mine[1])]
+    own_given = copies.local(given_ref, given_vmem)
     last = [
         copies.remote(normed_ref, mine[0], over_core),
         copies.remote(given_ref, mine[1], over_core),
@@ -392,6 +394,8 @@
     ff_rows = w_fc2_ref.shape[0] // 2
     for target, which in ((fc2_kept_ref, side), (fc2_going_ref, 1 - side)):
         target[...] = w_fc2_ref[pl.ds(pl.multiple_of(which * ff_rows, 128), ff_rows)].T
+    own_given.wait()
+    given_sum_ref[...] = jnp.sum(given_vmem[...].astype(wide), axis=0, keepdims=True)
     if planes > 3:
         forward(qo, 3, 0)
     x_normed.wait_recv()
@@ -438,12 +442,12 @@
         copy.wait_recv()
 
 
-def gather_tokens(planes, inputs, segments, gain, bias, given, w_qkv, w_out, fc1, w_fc2):
+def gather_tokens(planes, inputs, segments, affine, given, w_qkv, w_out, fc1, w_fc2):
     mine, rows, lanes = inputs.shape[0], fc1.shape[0], 2 * HEAD_DIM
     tokens, length = 8 * mine, segments.shape[1]
     columns = 2 * w_out.shape[0]
     whole = jax.ShapeDtypeStruct((2, 2, 2, mine, D), narrow)
-    head = max(128, fc1.shape[1] // 8)
+    head = max(128, 3 * fc1.shape[1] // 16)
     block = jax.ShapeDtypeStruct((2, rows, fc1.shape[1] // 2 - head), narrow)
     table = jax.ShapeDtypeStruct((2 * length, lanes), wide)
     weights = jax.ShapeDtypeStruct((planes, 2, rows, columns), narrow)
@@ -451,8 +455,8 @@
     ff_half = jax.ShapeDtypeStruct((rows, w_fc2.shape[0] // 2), narrow)
     outs = pl.pallas_call(
         functools.partial(gather_kernel, planes),
-        in_specs=[vmem] * 6 + [anywhere] * 3,
-        out_specs=[anywhere] * 5 + [vmem] * 5,
+        in_specs=[vmem] * 5 + [anywhere] * 3,
+        out_specs=[anywhere] * 5 + [vmem] * 6,
         out_shape=[
             whole,
             whole,
@@ -464,8 +468,10 @@
             jax.ShapeDtypeStruct((2, 8, 128), wide),
             table,
             table,
+            jax.ShapeDtypeStruct((1, D), wide),
         ],
         scratch_shapes=[
+            pltpu.VMEM((mine, D), narrow),
             pltpu.VMEM((mine, D), narrow),
             pltpu.VMEM((rows, w_out.shape[0]), narrow),
             pltpu.SemaphoreType.DMA((32,)),
@@ -479,7 +485,7 @@
             collective_id=1, has_side_effects=True, vmem_limit_bytes=VMEM
         ),
         name="gather_tokens",
-    )(inputs, segments, gain, bias, w_out, w_fc2, given, w_qkv, fc1)
+    )(inputs, segments, affine, w_out, w_fc2, given, w_qkv, fc1)
     normed_all, given_all, qo_all, head_all = outs[:4]
     return (
         normed_all.reshape(tokens, D),
@@ -807,7 +813,7 @@
 
 def project(normed, given, weights, bias):
     tokens, width = normed.shape[0], weights.shape[1] // 4
-    block = min(256, tokens)
+    block = min(512, tokens)
     row = pl.BlockSpec((block, D), lambda i: (i, 0))
     return pl.pallas_call(
         project_kernel,
@@ -835,12 +841,14 @@
     )(normed, given, weights, weights, bias)
 
 
-def reduce_kernel(terms, n_left, n_right, *refs):
+def reduce_kernel(terms, n_left, n_right, has_extra, n_sums, *refs):
     left_refs, right_refs = refs[:n_left], refs[n_left : n_left + n_right]
+    rest = list(refs[n_left + n_right :])
+    extra_ref = rest.pop(0) if has_extra else None
+    out_ref = rest.pop(0)
+    extra_came = rest.pop(0) if has_extra else None
+    sum_refs = [rest.pop(0) for _ in range(n_sums)]
     (
-        extra_ref,
-        out_ref,
-        extra_came,
         core_going,
         core_came,
         sums,
@@ -850,22 +858,23 @@
         y_came,
         send_sems,
         recv_sems,
-    ) = refs[n_left + n_right :]
+    ) = rest
     side, chip, core, over_x, over_y, over_core = neighbours()
     mine, columns = out_ref.shape
-    cut = columns // 4
+    cut = columns // 4 if has_extra else columns // 2
     first, second = slice(0, cut), slice(cut, columns)
     greet((over_x, True), (over_y, True), (over_core, True))
 
-    extra = pltpu.make_async_remote_copy(
-        src_ref=extra_ref.at[1 - side],
-        dst_ref=extra_came,
-        send_sem=send_sems.at[0, 4],
-        recv_sem=recv_sems.at[0, 4],
-        device_id=over_x,
-        device_id_type=MESH,
-    )
-    extra.start()
+    if has_extra:
+        extra = pltpu.make_async_remote_copy(
+            src_ref=extra_ref.at[1 - side],
+            dst_ref=extra_came,
+            send_sem=send_sems.at[0, 4],
+            recv_sem=recv_sems.at[0, 4],
+            device_id=over_x,
+            device_id_type=MESH,
+        )
+        extra.start()
 
     def copy(lane, number):
         going, came, other = (
@@ -928,6 +937,15 @@
     copy(2, 0).wait_recv()
     x_going[2, :, second] = (sums[1, :, second] + y_came[0, :, second].astype(wide)).astype(narrow)
     copy(1, 2).start()
+    for left_ref, sum_ref in zip(left_refs, sum_refs):
+        sum_ref[...] = jnp.zeros_like(sum_ref)
+
+        def add(i, carry):
+            here = pl.ds(pl.multiple_of(i * mine, 16), mine)
+            sum_ref[...] += jnp.sum(left_ref[here].astype(wide), axis=0, keepdims=True)
+            return carry
+
+        lax.fori_loop(0, left_ref.shape[0] // mine, add, 0)
     copy(1, 1).wait_recv()
     out_ref[:, first] = sums[3, :, first] + x_came[1, :, first].astype(wide)
     copy(2, 1).wait_recv()
@@ -936,7 +954,8 @@
     out_ref[:, first] += y_came[2, :, first].astype(wide)
     copy(1, 2).wait_recv()
     out_ref[:, second] += x_came[2, :, second].astype(wide)
-    extra.wait()
+    if has_extra:
+        extra.wait()
     for q in range(4):
         copy(0, q).wait_send()
     for lane in (1, 2):
@@ -956,23 +975,31 @@
     return next(i for i, other in enumerate(values) if other is value)
 
 
-def reduce_products(mine, terms, extra, collective_id):
+def reduce_products(mine, terms, collective_id, extra=None, sums=False):
     lefts = distinct([term[0] for term in terms])
     rights = distinct([term[3] for term in terms])
     places = tuple(
         (place_of(a, lefts), start, width, place_of(w, rights), column)
         for a, start, width, w, column in terms
     )
+    extras = [] if extra is None else [extra]
+    totals = [jax.ShapeDtypeStruct((1, a.shape[1]), wide) for a in lefts] if sums else []
     tokens, depth = terms[0][0].shape[0], sum(term[2] for term in terms)
     anywhere, vmem = pl.BlockSpec(memory_space=pl.ANY), pl.BlockSpec(memory_space=pltpu.VMEM)
     return pl.pallas_call(
-        functools.partial(reduce_kernel, places, len(lefts), len(rights)),
-        in_specs=[vmem] * (len(lefts) + len(rights)) + [anywhere],
-        out_specs=[vmem, anywhere],
-        out_shape=[
-            jax.ShapeDtypeStruct((mine, D), wide),
-            jax.ShapeDtypeStruct(extra.shape[1:], extra.dtype),
-        ],
+        functools.partial(
+            reduce_kernel,
+            places,
+            len(lefts),
+            len(rights),
+            extra is not None,
+            len(lefts) if sums else 0,
+        ),
+        in_specs=[vmem] * (len(lefts) + len(rights)) + [anywhere] * len(extras),
+        out_specs=[vmem] + [anywhere] * len(extras) + [vmem] * len(totals),
+        out_shape=[jax.ShapeDtypeStruct((mine, D), wide)]
+        + [jax.ShapeDtypeStruct(e.shape[1:], e.dtype) for e in extras]
+        + totals,
         scratch_shapes=[
             pltpu.VMEM((4, mine, D), narrow),
             pltpu.VMEM((4, mine, D), narrow),
@@ -991,7 +1018,7 @@
             flops=8 * tokens * depth * D, bytes_accessed=2 * depth * (tokens + D), transcendentals=0
         ),
         name="reduce_products",
-    )(*lefts, *rights, extra)
+    )(*lefts, *rights, *extras)
 
 
 def solution(mesh):
@@ -1078,12 +1105,12 @@
             bounds,
             cosine,
             sine,
+            cotangent_sum,
         ) = gather_tokens(
             nf // 2,
             inputs,
             segments,
-            ln_gain.reshape(1, D),
-            ln_bias.reshape(1, D),
+            jnp.stack([ln_gain, ln_bias]),
             cotangent,
             w_qkv,
             w_out,
@@ -1092,11 +1119,6 @@
         )
         fc1_tail = gather_planes(fc1_block)
         fc2_came = send_x(fc2_going)
-        tokens_in = inputs.astype(wide)
-        _, norm_back = jax.vjp(
-            layer_norm, tokens_in, ln_gain.astype(wide), ln_bias.astype(wide)
-        )
-
         bias_qkv = lax.dynamic_slice_in_dim(b_qkv, side * half_qkv, half_qkv, axis=1)
         bias_fc1 = lax.dynamic_slice_in_dim(b_fc1, side * half_ff, half_ff, axis=0)
 
@@ -1116,15 +1138,23 @@
             (fc2_kept, fc2_came),
             2,
         )
-        grad_q, grad_k, grad_v, sum_qo = lax.optimization_barrier((grad_q, grad_k, grad_v, sum_qo))
+        (
+            grad_q, grad_k, grad_v, sum_qo, inputs, ln_gain, ln_bias, b_out, b_fc2, cotangent, cotangent_sum
+        ) = lax.optimization_barrier(
+            (grad_q, grad_k, grad_v, sum_qo, inputs, ln_gain, ln_bias, b_out, b_fc2, cotangent, cotangent_sum)
+        )
+        tokens_in = inputs.astype(wide)
+        _, norm_back = jax.vjp(
+            layer_norm, tokens_in, ln_gain.astype(wide), ln_bias.astype(wide)
+        )
         total_fc2 = sum_planes(grad_w2.reshape(-1, rows))
         grad_hidden = (nn(grad_rows, full_fc2) * slope).astype(narrow)
         grad_w1 = tn(normed, grad_hidden).astype(narrow)
         mixed, grad_w1 = lax.optimization_barrier((mixed, grad_w1))
-        branch_local, came_qo = reduce_products(
+        came_qo = send_x(pick(sum_qo, 1 - side))
+        (branch_local,) = reduce_products(
             mine,
             [(mixed, 0, half_qkv, full_qo, 3 * half_qkv), (active_low, 0, half_ff, full_fc2, 0)],
-            sum_qo,
             4,
         )
         total_fc2, grad_hidden, grad_w1, branch_local = lax.optimization_barrier(
@@ -1133,7 +1163,7 @@
         total_fc1 = sum_planes(grad_w1)
         total_fc2 = total_fc2.reshape(2, half_ff, rows)
         head = fc1_head.shape[1]
-        grad_normed, came_fc2 = reduce_products(
+        grad_normed, came_fc2, sum_q, sum_k, sum_v, sum_hidden = reduce_products(
             mine,
             [
                 (grad_q, 0, half_qkv, full_qo, 0),
@@ -1142,12 +1172,13 @@
                 (grad_hidden, 0, head, fc1_head, 0),
                 (grad_hidden, head, half_ff - head, fc1_tail, 0),
             ],
-            total_fc2,
             3,
-        )
+            extra=total_fc2,
+            sums=True,
+        )
+        sum_qo, came_qo, grad_normed = lax.optimization_barrier((sum_qo, came_qo, grad_normed))
         sum_qo = halves_of(pick(sum_qo, side), came_qo)
         sum_fc2 = halves_of(pick(total_fc2, side), came_fc2)
-        grad_projected = jnp.concatenate([grad_q, grad_k, grad_v], axis=1)
         outputs = (tokens_in + branch_local + b_out.astype(wide) + b_fc2.astype(wide)).astype(narrow)
         grad_tokens, grad_gain, grad_offset = norm_back(grad_normed)
         grad_tokens = grad_tokens + cotangent.astype(wide)
@@ -1160,18 +1191,17 @@
         anchor = jnp.zeros((), jnp.int32)
         bias_qkv_full = lax.dynamic_update_slice(
             jnp.zeros((3, D), wide),
-            jnp.sum(grad_projected.astype(wide), axis=0).reshape(3, half_qkv),
+            jnp.concatenate([sum_q, sum_k, sum_v], axis=0),
             (anchor, (2 * t_place + side) * half_qkv),
         )
         bias_fc1_full = lax.dynamic_update_slice(
             jnp.zeros((FF,), wide),
-            jnp.sum(grad_hidden.astype(wide), axis=0),
+            sum_hidden.reshape(-1),
             ((2 * t_place + side) * half_ff,),
         )
-        cotangent_sum = jnp.sum(cotangent.astype(wide), axis=0)
         small = reduce_all(
             jnp.concatenate(
-                [bias_qkv_full.reshape(-1), bias_fc1_full, grad_gain, grad_offset, cotangent_sum]
+                [bias_qkv_full.reshape(-1), bias_fc1_full, grad_gain, grad_offset, cotangent_sum.reshape(-1)]
             ).reshape(-1, 128)
         ).reshape(-1)
         total_fc1, outputs, grad_tokens, grad_w_qkv, grad_w_out, grad_w_fc2 = (

time: 471 us -> 463 us (0.983)
  Pallas kernels: 374 us -> 366 us
    pallas_call x1, Pallas kernels: 42.8 us -> 33.9 us  [attention(): pl.pallas_call(functools.partial(attention_kernel, rows), grid=(tokens //...]
    pallas_call x1, Pallas kernels: 108 us -> 116 us  [gather_tokens(): pl.pallas_call(functools.partial(gather_kernel, planes), in_specs=[vmem]...]
    reduce_sum x3 -> x0, other arithmetic: 6.77 us -> none  [the longest x1 3.31 us: local(): cotangent_sum = jnp.sum(cotangent.astype(wide), axis=0)]
    pallas_call x2, Pallas kernels: 109 us -> 104 us  [reduce_products(): pl.pallas_call(functools.partial(reduce_kernel, places, len(lefts), len(r...]
  transfers between devices with their start and end apart: 10 -> 11, of which waited for: 5 -> 5; matrix products, arithmetic and copies ran while one was open for 10% -> 10% of each run, Pallas kernels for 36% -> 33%
where the time goes in v5:
time: 463 us; the launch traced here: 460 us
  Pallas kernels  366 us (79%)
  matrix products  24.3 us (5%)
  waiting for transfers between devices  18.7 us (4%)
  other arithmetic  14.5 us (3%)
  between operations  14.3 us (3%)
  local copies, waits for them, and re-layouts  12.9 us (3%)
  starting transfers between devices  9.17 us (2%)
    pallas_call x1, Pallas kernels, gather_tokens(): pl.pallas_call(functools.partial(gather_kernel, planes), in_specs=[vmem]...  116 us
    pallas_call x2, Pallas kernels, reduce_products(): pl.pallas_call(functools.partial(reduce_kernel, places, len(lefts), len(r...  104 us
    pallas_call x1, Pallas kernels, backward_step(): pl.pallas_call(functools.partial(scatter_kernel, planes, which), in_specs...  98.1 us
    pallas_call x1, Pallas kernels, attention(): pl.pallas_call(functools.partial(attention_kernel, rows), grid=(tokens //...  33.9 us
    pallas_call x1, Pallas kernels, project(): pl.pallas_call(project_kernel, grid=(tokens // block,), in_specs=[row, ro...  14.8 us
    dot_general x1, matrix products, nn(): lax.dot_general(a, b, (((1,), (0,)), ((), ())), preferred_element_type=wide)  13.8 us
    dot_general x1, matrix products, tn(): lax.dot_general(a, b, (((0,), (0,)), ((), ())), preferred_element_type=wide)  10.5 us
  transfers between devices with their start and end apart: 11, of which 5 were waited for; matrix products, arithmetic and copies ran while one was open for 10% of the time, Pallas kernels for 33%

profile of v5, /device:TPU:0, one launch (start us, length us, event | category | flops | bytes accessed | tf_op | source)
XLA Modules:
  0.0 460.2 jit_solution(83883393409522606)
XLA Ops:
  7.2 0.7 stack.34
  7.9 0.7 stack.33
  8.6 0.6 pad_maximum_fusion.affine_ref
  9.2 115.9 %gather_tokens.1 = (bf16[2,2,2,256,2048]{4,3,2,1,0:T(8,128)(2,1)}, bf16[2,2,2,256,2048]{4,3,2,1,0:T(8,128)(2,1)}, bf16[4,2,256,1024]{3,2,1,0:T(8,128)(2,1)}, bf1...) custom-call(bf16[256,2048]{1,0:T(8,128)(2,1)} %input_ref.1, ...), custom_call_target="tpu_custom_call" | custom-call | tf_op jit(solution)/shard_map/gather_tokens/pallas_call | solution.py:456
  125.2 0.2 reduce-scatter.3.cloned.1.call-start
  125.4 1.6 collective-permute-start
  126.9 0.6 copy.26
  127.5 0.6 dynamic-slice_convert_fusion
  128.1 14.8 %project.1 = (f32[2048,768]{1,0:T(8,128)}, bf16[2048,256]{1,0:T(8,128)(2,1)}) custom-call(bf16[2048,2048]{1,0:T(8,128)(2,1)} %bitcast.61, bf16[2048,2048]{1,0:T(8,128)(2,1)} %bitcast.64, bf16[2048,1024]{1,0:T(8,128)(2,1)} %bitcast.67, bf16[2048,1024]{1,0:T(8,128)(2,1)} %bitcast.68, f32[1,768]{1,0:T(1,128)} %bitcast.60), custom_call_target="tpu_custom_call" | custom-call | flops 8589934592 | bytes 33554432 | tf_op jit(solution)/shard_map/project/pallas_call | solution.py:818
  142.9 33.9 %attention.1 = (bf16[2048,256]{1,0:T(8,128)(2,1)}, bf16[2048,256]{1,0:T(8,128)(2,1)}, bf16[2048,256]{1,0:T(8,128)(2,1)}, bf16[2048,256]{1,0:T(8,128)(2,1)}) custom-call(f32[2,8,128]{2,1,0:T(8,128)} %get-tuple-element.67.bound_ref, f32[2048,128]{1,0:T(8,128)} %get-tuple-element.68.cos_ref, f32[2048,128]{1,0:T(8,128)} %get-tuple-element.69.sin_ref, ...), custom_call_target="tpu_custom_call" | custom-call | flops 6442450944 | bytes 16777216 | tf_op jit(solution)/shard_map/attention/pallas_call | solution.py:147
  176.9 3.3 all-gather.2.cloned.1.call-done.refs_7_.refs_6_
  180.2 98.1 %backward_step.1 = (bf16[2,1024,256]{2,1,0:T(8,128)(2,1)}, bf16[4,2,256,1024]{3,2,1,0:T(8,128)(2,1)}, bf16[2048,1024]{1,0:T(8,128)(2,1)}, f32[2048,1024]{1,0:T(8,128)}, bf16[4,2,1024,256]{3,2,1,0:T(8,128)(2,1)}) custom-call(bf16[2048,2048]{1,0:T(8,128)(2,1)} %bitcast.62, bf16[2048,2048]{1,0:T(8,128)(2,1)} %bitcast.65, ...), custom_call_target="tpu_custom_call" | custom-call | flops 171798691840 | bytes 8388608 | tf_op jit(solution)/shard_map/backward_step/pallas_call | solution.py:773
  278.3 0.2 reduce-scatter.5.cloned.1.call-start
  278.5 13.8 %multiply_convert_fusion.refs_3_ = bf16[2048,1024]{1,0:T(8,128)(2,1)S(1)} fusion(f32[2048,1024]{1,0:T(8,128)} %get-tuple-element.83, bf16[2048,2048]{1,0:T(8,128)(2,1)} %bitcast.66, bf16[2048,1024]{1,0:T(8,128)(2,1)} %bitcast.73), kind=kOutput, calls=%fused_computation | convolution fusion | flops 8594128896 | bytes 25165824 | tf_op jit(solution)/shard_map/dot_general | solution.py:52
  292.4 2.0 copy-done.17
  294.4 10.5 %convolution_convert_fusion = bf16[2048,1024]{1,0:T(8,128)(2,1)} fusion(bf16[2048,2048]{1,0:T(8,128)(2,1)S(1)} %bitcast.63, bf16[2048,1024]{1,0:T(8,128)(2,1)S(1)} %multiply_convert_fusion.refs_3_), kind=kOutput, calls=%fused_computation.1 | convolution fusion | flops 8592031744 | bytes 16777216 | tf_op jit(solution)/shard_map/dot_general | solution.py:56
  304.9 1.5 collective-permute-start.1
  306.5 0.2 convert_reduce_fusion
  306.7 47.9 %reduce_products.2 = f32[256,2048]{1,0:T(8,128)} custom-call(bf16[2048,256]{1,0:T(8,128)(2,1)} %get-tuple-element.85.refs_5_.refs_0_, bf16[2048,1024]{1,0:T(8,128)(2,1)} %get-tuple-element.86.refs_1_, bf16[2048,1024]{1,0:T(8,128)(2,1)} %bitcast.69, bf16[2048,1024]{1,0:T(8,128)(2,1)} %bitcast.74), custom_call_target="tpu_custom_call" | custom-call | flops 42949672960 | bytes 10485760 | tf_op jit(solution)/shard_map/reduce_products/pallas_call | solution.py:989
  354.6 55.7 %reduce_products.3 = (f32[256,2048]{1,0:T(8,128)}, bf16[1024,256]{1,0:T(8,128)(2,1)}, f32[1,256]{1,0:T(1,128)}, f32[1,256]{1,0:T(1,128)}, f32[1,256]{1,0:T(1,128)}, /*index=5*/f32[1,1024]{1,0:T(1,128)}) custom-call(bf16[2048,256]{1,0:T(8,128)(2,1)} %get-tuple-element.95.refs_2_.refs_0_, bf16[2048,256]{1,0:T(8,128)(2,1)} %get-tuple-element.96.refs_3_.refs_1_, ...), custom_call_target="tpu_custom_call" | custom-call | flops 60129542144 | bytes 14680064 | tf_op jit(solution)/shard_map/reduce_products/pallas_call | solution.py:989
  410.4 0.7 maximum_dynamic-update-slice_fusion
  411.2 1.0 dynamic_update_slice.7
  412.2 2.3 fusion.14
  414.5 1.0 fusion.7
  415.7 0.3 copy-done.2
  416.0 0.7 copy-done.3
  416.7 2.9 convert_add_fusion.1
  419.6 0.2 maximum_select_fusion.2
  419.8 0.6 collective-permute-start.3
  420.4 1.5 bitcast_convert_fusion
  422.0 2.3 collective-permute-done.3
  424.3 0.6 collective-permute-start.4
  425.0 3.8 collective-permute-done.4
  428.9 1.5 collective-permute-start.5
  430.4 1.5 fusion.11
  432.0 0.8 slice.30
  432.8 0.8 copy.25
  433.7 2.4 reshape.153
  436.1 2.0 collective-permute-start.6
  438.1 1.3 bitcast_convert_fusion.1
  439.4 0.8 collective-permute-start.7
  440.2 2.2 collective-permute-done.6
  442.4 0.6 reshape.159
  443.0 0.6 slice_bitcast_fusion.1
  443.6 0.6 slice_bitcast_fusion
  444.2 6.9 %collective-permute-done.7 = bf16[256,1024]{1,0:T(8,128)(2,1)S(1)} collective-permute-done((bf16[256,1024]{1,0:T(8,128)(2,1)S(1)}, bf16[256,1024]{1,0:T(8,128)(2,1)S(1)}, u32[]{:S(2)}, u32[]{:S(2)}) %collective-permute-start.7) | collective-permute-done | bytes 524320 | tf_op jit(solution)/shard_map/ppermute | solution.py:1033
  451.2 1.6 maximum_select_fusion
  452.8 0.6 copy.34
  (70 shorter events, 0.8 us)
Async XLA Ops:
  7.2 173.0 %all-gather.2.cloned.1.call-start = ((), (), s32[]{:S(2)}) async-start(), calls=%async_computation.2 | async-start | bytes 3276800 | tf_op jit(solution)/shard_map/all_gather | solution.py:1043
  9.2 117.7 %copy-start.13 = (bf16[3,512]{1,0:T(4,128)(2,1)S(1)}, bf16[3,512]{1,0:T(4,128)(2,1)}, u32[]{:S(2)}) copy-start(bf16[3,512]{1,0:T(4,128)(2,1)} %param.18) | copy-start | bytes 9220
  9.2 118.3 %copy-start.14 = (bf16[2048]{0:T(1024)(128)(2,1)S(1)}, bf16[2048]{0:T(1024)(128)(2,1)}, u32[]{:S(2)}) copy-start(bf16[2048]{0:T(1024)(128)(2,1)} %param.22) | copy-start | bytes 12292
  125.2 229.5 %reduce-scatter.3.cloned.1.call-start = ((), (), s32[]{:S(2)}) async-start(), calls=%async_computation.3 | async-start | bytes 5242880 | tf_op jit(solution)/shard_map/reduce_scatter | solution.py:1078
  125.4 51.5 %collective-permute-start = (bf16[256,1024]{1,0:T(8,128)(2,1)}, bf16[256,1024]{1,0:T(8,128)(2,1)S(1)}, u32[]{:S(2)}, u32[]{:S(2)}) collective-permute-start(bf16[256,1024]{1,0:T(8,128)(2,1)} %get-tuple-element.80), channel_id=1, source_target_pairs={{0,4},{4,0},{8,12},{12,8},{16,20},{20,16},{24,28},{28,24},{1,5},{5... | collective-permute-start | bytes 1572872 | tf_op jit(solution)/shard_map/ppermute | solution.py:1033
  176.8 3.4 copy-start.16
  278.3 159.7 %reduce-scatter.5.cloned.1.call-start = ((), (), s32[]{:S(2)}) async-start(), calls=%async_computation.4 | async-start | bytes 5242880 | tf_op jit(solution)/shard_map/reduce_scatter | solution.py:1078
  278.5 15.8 %copy-start.15 = (bf16[2,2,2,256,2048]{4,3,2,1,0:T(8,128)(2,1)S(1)}, bf16[2,2,2,256,2048]{4,3,2,1,0:T(8,128)(2,1)}, u32[]{:S(2)}) copy-start(bf16[2,2,2,256,2048]{4,3,2,1,0:T(8,128)(2,1)} %get-tuple-element.65) | copy-start | bytes 25165828
  292.4 2.0 copy-start.17
  294.3 10.5 %copy-start.4 = (bf16[2,1024,256]{2,1,0:T(8,128)(2,1)S(1)}, bf16[2,1024,256]{2,1,0:T(8,128)(2,1)}, u32[]{:S(2)}) copy-start(bf16[2,1024,256]{2,1,0:T(8,128)(2,1)} %get-tuple-element.104) | copy-start | bytes 3145732
  294.3 12.1 %copy-start.9 = (bf16[2048]{0:T(1024)(128)(2,1)S(1)}, bf16[2048]{0:T(1024)(128)(2,1)}, u32[]{:S(2)}) copy-start(bf16[2048]{0:T(1024)(128)(2,1)} %param.15) | copy-start | bytes 12292
  294.3 12.1 %copy-start.11 = (bf16[2048]{0:T(1024)(128)(2,1)S(1)}, bf16[2048]{0:T(1024)(128)(2,1)}, u32[]{:S(2)}) copy-start(bf16[2048]{0:T(1024)(128)(2,1)} %param.24) | copy-start | bytes 12292
  294.3 12.1 %copy-start.12 = (bf16[2048]{0:T(1024)(128)(2,1)S(1)}, bf16[2048]{0:T(1024)(128)(2,1)}, u32[]{:S(2)}) copy-start(bf16[2048]{0:T(1024)(128)(2,1)} %param.20) | copy-start | bytes 12292
  294.4 12.1 %copy-start = (bf16[256,2048]{1,0:T(8,128)(2,1)S(1)}, bf16[256,2048]{1,0:T(8,128)(2,1)}, u32[]{:S(2)}) copy-start(bf16[256,2048]{1,0:T(8,128)(2,1)} %input_ref.1) | copy-start | bytes 3145732
  304.9 105.5 %collective-permute-start.1 = (bf16[1024,256]{1,0:T(8,128)(2,1)S(1)}, bf16[1024,256]{1,0:T(8,128)(2,1)}, u32[]{:S(2)}, u32[]{:S(2)}) collective-permute-start(bf16[1024,256]{1,0:T(8,128)(2,1)S(1)} %dynamic-slice_bitcast_fusion.1), channel_id=1, source_target_pairs={{0,4},{4,0},{8,12},{12,8},{16,20},{20,16},{24,28},{28,24},{1,5},{5... | collective-permute-start | bytes 1572872 | tf_op jit(solution)/shard_map/ppermute | solution.py:1033
  411.1 3.4 copy-start.1
  414.5 1.0 copy-start.10
  414.5 1.2 copy-start.7
  414.5 1.5 copy-start.2
  414.5 2.2 copy-start.3
  415.5 4.3 collective-permute-start.2
  416.7 2.9 copy-start.6
  419.8 5.2 %copy-start.5 = (bf16[2,1024,256]{2,1,0:T(8,128)(2,1)S(1)}, bf16[2,1024,256]{2,1,0:T(8,128)(2,1)}, u32[]{:S(2)}) copy-start(bf16[2,1024,256]{2,1,0:T(8,128)(2,1)} %get-tuple-element.104) | copy-start | bytes 3145732
  419.8 4.5 collective-permute-start.3
  424.3 4.5 collective-permute-start.4
  428.9 7.2 %collective-permute-start.5 = (f32[160,128]{1,0:T(8,128)S(1)}, f32[160,128]{1,0:T(8,128)S(1)}, u32[]{:S(2)}, u32[]{:S(2)}) collective-permute-start(f32[160,128]{1,0:T(8,128)S(1)} %add.104), channel_id=1, source_target_pairs={{0,8},{4,12},{8,0},{12,4},{16,24},{20,28},{24,16},{28,20},{1,9},{5... | collective-permute-start | bytes 245768 | tf_op jit(solution)/shard_map/ppermute | solution.py:1093
  436.1 6.3 %collective-permute-start.6 = (f32[160,128]{1,0:T(8,128)S(1)}, f32[160,128]{1,0:T(8,128)S(1)}, u32[]{:S(2)}, u32[]{:S(2)}) collective-permute-start(f32[160,128]{1,0:T(8,128)S(1)} %add.105), channel_id=1, source_target_pairs={{0,16},{4,20},{8,24},{12,28},{16,0},{20,4},{24,8},{28,12},{1,17},{... | collective-permute-start | bytes 245768 | tf_op jit(solution)/shard_map/ppermute | solution.py:1093
  439.4 11.7 %collective-permute-start.7 = (bf16[256,1024]{1,0:T(8,128)(2,1)S(1)}, bf16[256,1024]{1,0:T(8,128)(2,1)S(1)}, u32[]{:S(2)}, u32[]{:S(2)}) collective-permute-start(bf16[256,1024]{1,0:T(8,128)(2,1)S(1)} %get-tuple-element.124), channel_id=1, source_target_pairs={{0,4},{4,0},{8,12},{12,8},{16,20},{20,16},{24,28},{28,24},{1,5},{5... | collective-permute-start | bytes 1572872 | tf_op jit(solution)/shard_map/ppermute | solution.py:1033
  443.6 9.2 %copy-start.8 = (f32[2048]{0:T(1024)}, f32[2048]{0:T(1024)S(1)}, u32[]{:S(2)}) copy-start(f32[2048]{0:T(1024)S(1)} %get-tuple-element.155) | copy-start | bytes 24580
Sparse Core Ops, SparseCore 0:
  125.3 54.8 all-gather.1
  278.4 75.8 reduce-scatter.2
  356.7 77.6 reduce-scatter.4
